TPU v7x, 128 devices: a whole 4x4x4 slice. The times are simulated.
128 devices in a mesh: section: 4 (over y), group: 32 (over x, z, core).
Axes of the slice: x: 4, y: 4, z: 4, core: 2. Of those that a mesh axis runs over, the one named last changes fastest.
Arguments:
- hidden: bfloat16 [256, 4096], P(('section', 'group')), may hold values from -16 to 16
- targets: int32 [256], P(('section', 'group')), may hold values from 0 to 131071
- token_weight: bfloat16 [256], P(('section', 'group')), may hold values from 2 to 32
- head_weight: bfloat16 [131072, 4096], P(('section', 'group')), may hold values from -0.5 to 0.5
- token_ids: int32 [256], P(('section', 'group')), may hold values from 0 to 131071
- embed_cotangent: bfloat16 [256, 4096], P(('section', 'group')), may hold values from -6 to 6
- new_rows: int32 [8, 2], replicated, may hold values from 0 to 131072, as said below
Outputs:
- mean_loss: float32 [], replicated
- grad_hidden: bfloat16 [256, 4096], P('section', 'group')
- grad_head: bfloat16 [131072, 4096], P(('section', 'group'))
- grad_embed: bfloat16 [131072, 4096], P(('section', 'group'))
Inputs may be any that keep to these rules, and one draw needn't show every extreme that they name: `new_rows`: 8 disjoint ascending ranges [start, end) with start < end; the first starts at 0 and the last ends at 131072.
All inputs are finite; a program needn't handle non-finite values.
Results may differ from a plain program's by a relative error of at most 0.0095.
Values may be sent and summed in bfloat16 or wider, within the bound.
No kernel may reach another device: no remote copies, remote signals or barrier semaphores. Data moves between devices by JAX's collectives and lax.ppermute only.
A program may use at most 128 MiB of HBM per device.

v0:
```python
import jax
import jax.numpy as jnp
from jax import lax
from jax.sharding import PartitionSpec as P


def local(hidden, targets, token_weight, head_weight, token_ids, embed_cotangent, new_rows):
    voc_rows = head_weight.shape[0]
    row_start = (
        lax.axis_index("section") * lax.axis_size("group") + lax.axis_index("group")
    ) * voc_rows
    row_ids = row_start + jnp.arange(voc_rows, dtype=jnp.int32)
    inside = (row_ids[:, None] >= new_rows[None, :, 0]) & (row_ids[:, None] < new_rows[None, :, 1])
    trainable = jnp.any(inside, axis=1)
    keep_gate = trainable.astype(jnp.float32)[:, None]
    all_hidden, all_targets, all_weights = (
        lax.all_gather(hidden, ("section", "group"), axis=0, tiled=True),
        lax.all_gather(targets, ("section", "group"), axis=0, tiled=True),
        lax.all_gather(token_weight, ("section", "group"), axis=0, tiled=True),
    )
    logits = lax.dot_general(
        all_hidden, head_weight, (((1,), (1,)), ((), ())), preferred_element_type=jnp.float32
    )
    target_hits = all_targets[:, None] == row_ids[None, :]
    picked_local = jnp.sum(jnp.where(target_hits, logits, 0.0), axis=1)
    row_peak = lax.pmax(jnp.max(logits, axis=1), ("section", "group"))
    exp_total, picked = lax.psum(
        (jnp.sum(jnp.exp(logits - row_peak[:, None]), axis=1), picked_local), ("section", "group")
    )
    log_norm = row_peak + jnp.log(exp_total)
    weights = all_weights.astype(jnp.float32)
    mean_loss = jnp.sum(weights * (log_norm - picked)) / jnp.sum(weights)
    slopes = (
        weights[:, None] * (jnp.exp(logits - log_norm[:, None]) - target_hits.astype(jnp.float32))
    ).astype(jnp.bfloat16)
    partial_grad = jnp.dot(slopes, head_weight, preferred_element_type=jnp.float32)
    half_summed = lax.psum_scatter(partial_grad, "section", scatter_dimension=0, tiled=True)
    grad_hidden = lax.psum_scatter(half_summed, "group", scatter_dimension=1, tiled=True)
    grad_hidden = grad_hidden.astype(jnp.bfloat16)
    product = lax.dot_general(
        slopes, all_hidden, (((0,), (0,)), ((), ())), preferred_element_type=jnp.float32
    )
    grad_head = (product * keep_gate).astype(jnp.bfloat16)
    all_cotangent, all_ids = (
        lax.all_gather(embed_cotangent, ("section", "group"), axis=0, tiled=True),
        lax.all_gather(token_ids, ("section", "group"), axis=0, tiled=True),
    )
    onehot = (all_ids[:, None] == row_ids[None, :]).astype(jnp.bfloat16)
    embed_sum = lax.dot_general(
        onehot, all_cotangent, (((0,), (0,)), ((), ())), preferred_element_type=jnp.float32
    )
    grad_embed = (embed_sum * keep_gate).astype(jnp.bfloat16)
    return (mean_loss, grad_hidden, grad_head, grad_embed)


def solution(mesh):
    in_specs = (
        P(("section", "group"), None),
        P(("section", "group")),
        P(("section", "group")),
        P(("section", "group"), None),
        P(("section", "group")),
        P(("section", "group"), None),
        P(),
    )
    out_specs = (
        P(),
        P("section", "group"),
        P(("section", "group"), None),
        P(("section", "group"), None),
    )
    return jax.shard_map(local, mesh=mesh, in_specs=in_specs, out_specs=out_specs, check_vma=False)
```

profile of v0, /device:TPU:0, one launch (start us, length us, event | category | flops | bytes accessed | tf_op | source)
XLA Modules:
  0.0 486.7 jit_solution(14790307677342971465)
XLA Ops:
  7.2 0.7 all-gather.5.cloned.1.call-update
  8.0 0.9 dynamic-update-slice
  8.8 68.7 %all-reduce = bf16[256]{0:T(256)(128)(2,1)S(1)} all-reduce(bf16[256]{0:T(256)(128)(2,1)S(1)} %dynamic-update-slice), channel_id=1, replica_groups=mesh['section'=4,'group'=32] {'section','group'}, use_global_device_ids=true, to_apply=%add | all-reduce | flops 256 | bytes 1024
  77.5 0.9 dynamic-update-slice.1
  78.4 0.8 dynamic-update-slice.2
  79.2 62.1 %all-reduce.3 = (s32[256]{0:T(256)S(1)}, s32[256]{0:T(256)S(1)}) all-reduce(s32[256]{0:T(256)S(1)} %dynamic-update-slice.1, s32[256]{0:T(256)S(1)} %dynamic-update-slice.2), channel_id=1, replica_groups=mesh['section'=4,'group'=32] {'section','group'}, use_global_device_ids=true, to_apply=%add.1 | all-reduce | flops 512 | bytes 4096
  141.4 2.7 reshape.33
  144.2 5.8 %fusion.10 = (f32[256]{0:T(256)S(1)}, f32[256,1024]{1,0:T(8,128)S(1)}) fusion(bf16[256,4096]{1,0:T(8,128)(2,1)S(1)} %reshape.33, bf16[1024,4096]{1,0:T(8,128)(2,1)} %param.10), kind=kOutput, calls=%fused_computation.20 | convolution fusion | flops 2147745536 | bytes 11535360 | tf_op jit(solution)/shard_map/dot_general | solution.py:21
  150.0 64.4 %pmax.7 = f32[256]{0:T(256)S(1)} all-reduce(f32[256]{0:T(256)S(1)} %get-tuple-element.15), channel_id=1, replica_groups=mesh['section'=4,'group'=32] {'section','group'}, use_global_device_ids=true, to_apply=%region_1.2 | all-reduce | flops 256 | bytes 2048 | tf_op jit(solution)/shard_map/pmax | solution.py:26
  214.5 0.4 fusion
  214.9 62.3 %all-reduce.4 = (f32[256]{0:T(256)S(1)}, f32[256]{0:T(256)S(1)}) all-reduce(f32[256]{0:T(256)S(1)} %get-tuple-element.5, f32[256]{0:T(256)S(1)} %get-tuple-element.4), channel_id=1, replica_groups=mesh['section'=4,'group'=32] {'section','group'}, use_global_device_ids=true, to_apply=%region_3.4 | all-reduce | flops 512 | bytes 4096 | tf_op jit(solution)/shard_map/psum | solution.py:27
  277.1 0.6 convert_reduce_fusion
  277.7 7.9 %fusion.8 = f32[256,4096]{1,0:T(8,128)} fusion(bf16[1024,4096]{1,0:T(8,128)(2,1)} %param.10, f32[256,1024]{1,0:T(8,128)S(1)} %get-tuple-element.16, f32[256]{0:T(256)S(1)} %get-tuple-element.12, f32[256]{0:T(256)S(1)} %convert_element_type.26, s32[1024]{0:T(1024)S(1)} %iota_add_fusion, s32[256]{0:T(256)S(1)} %get-tuple-element.8), kind=kOutput, calls=%fused_computation.19 | convolution fusion | flops 2149056512 | bytes 13638656 | tf_op jit(solution)/shard_map/dot_general | solution.py:36
  285.7 0.0 all-gather.7.cloned.1.call-start
  285.8 0.7 all-gather.7.cloned.1.call-update
  286.4 0.2 reduce-scatter.5.cloned.1.call-start
  286.7 43.4 %reduce-scatter.3.cloned.1.call-done = f32[64,4096]{1,0:T(8,128)} async-done(((f32[256,4096]{1,0:T(8,128)}), f32[64,4096]{1,0:T(8,128)}) %reduce-scatter.3.cloned.1.call-update) | async-done | bytes 1048592 | tf_op jit(solution)/shard_map/reduce_scatter | solution.py:37
  330.1 0.1 and_reduce_fusion
  331.5 67.2 %all-gather.7.cloned.1.call-done = bf16[128,2,4096]{2,1,0:T(2,128)(2,1)} async-done(((bf16[1,2,4096]{2,1,0:T(2,128)(2,1)}), bf16[128,2,4096]{2,1,0:T(2,128)(2,1)}) %all-gather.7.cloned.1.call-update) | async-done | bytes 2097168 | tf_op jit(solution)/shard_map/all_gather | solution.py:45
  398.7 4.1 reshape.35
  402.8 7.5 %multiply_convert_fusion = bf16[1024,4096]{1,0:T(8,128)(2,1)} fusion(bf16[256,4096]{1,0:T(8,128)(2,1)} %reshape.35, f32[1024]{0:T(1024)S(1)} %convert_element_type.30, s32[1024]{0:T(1024)S(1)} %iota_add_fusion, s32[256]{0:T(256)S(1)} %get-tuple-element.9), kind=kOutput, calls=%fused_computation | convolution fusion | flops 2156134400 | bytes 10494976 | tf_op jit(solution)/shard_map/dot_general | solution.py:49
  410.3 5.0 %multiply_convert_fusion.1 = bf16[1024,4096]{1,0:T(8,128)(2,1)} fusion(bf16[256,4096]{1,0:T(8,128)(2,1)S(1)} %reshape.33, f32[1024]{0:T(1024)S(1)} %convert_element_type.30, f32[256,1024]{1,0:T(8,128)S(1)} %get-tuple-element.16, f32[256]{0:T(256)S(1)} %get-tuple-element.12, f32[256]{0:T(256)S(1)} %convert_element_type.26, s32[1024]{0:T(1024)S(1)} %iota_add_fusion, ...), kind=kOutput, calls=%fused_computation.1 | convolution fusion | flops 2157445120 | bytes 11545600 | tf_op jit(solution)/shard_map/dot_general | solution.py:40
  415.3 62.4 %reduce-scatter.5.cloned.1.call-done = f32[64,128]{1,0:T(8,128)} async-done(((f32[64,4096]{1,0:T(8,128)}), f32[64,128]{1,0:T(8,128)}) %reduce-scatter.5.cloned.1.call-update) | async-done | bytes 32784 | tf_op jit(solution)/shard_map/reduce_scatter | solution.py:38
  477.7 1.4 convert_element_type.29
  (14 shorter events, 0.2 us)
Async XLA Ops:
  7.2 134.3 %all-gather.5.cloned.1.call-start = ((), (), s32[]{:S(2)}) async-start(), calls=%async_computation.4 | async-start | bytes 2113536 | tf_op jit(solution)/shard_map/all_gather | solution.py:17
  7.9 322.1 %reduce-scatter.3.cloned.1.call-start = ((), (), s32[]{:S(2)}) async-start(), calls=%async_computation.2 | async-start | bytes 5242880 | tf_op jit(solution)/shard_map/reduce_scatter | solution.py:37
  277.7 52.3 %copy-start = (s32[8,2]{0,1:T(2,128)S(1)}, s32[8,2]{0,1:T(2,128)}, u32[]{:S(2)}) copy-start(s32[8,2]{0,1:T(2,128)} %param.13) | copy-start | bytes 196
  285.7 113.0 %all-gather.7.cloned.1.call-start = ((), (), s32[]{:S(2)}) async-start(), calls=%async_computation.5 | async-start | bytes 2113536 | tf_op jit(solution)/shard_map/all_gather | solution.py:45
  286.4 191.3 %reduce-scatter.5.cloned.1.call-start = ((), (), s32[]{:S(2)}) async-start(), calls=%async_computation.3 | async-start | bytes 1081344 | tf_op jit(solution)/shard_map/reduce_scatter | solution.py:38
Sparse Core Ops, SparseCore 0:
  11.1 68.0 all-gather.4
  285.8 44.1 reduce-scatter.2
  333.7 65.0 all-gather.6
  402.5 75.1 reduce-scatter.4
where the time goes:
time: 488 us; the launch traced here: 487 us
  blocking collectives  258 us (53%)
  waiting for transfers between devices  174 us (36%)
  matrix products  26.3 us (5%)
  between operations  16.3 us (3%)
  local copies, waits for them, and re-layouts  9.41 us (2%)
    unnamed x2, blocking collectives  131 us
    all_gather x1, waiting for transfers between devices, local(): lax.all_gather(embed_cotangent, ('section', 'group'), axis=0, tiled=True)  67.2 us
    pmax x1, blocking collectives, local(): row_peak = lax.pmax(jnp.max(logits, axis=1), ('section', 'group'))  64.4 us
    reduce_scatter x1, waiting for transfers between devices, local(): lax.psum_scatter(half_summed, 'group', scatter_dimension=1, tiled=True)  62.4 us
    psum x1, blocking collectives, local(): lax.psum((jnp.sum(jnp.exp(logits - row_peak[:, None]), axis=1), picked_lo...  62.3 us
    reduce_scatter x1, waiting for transfers between devices, local(): lax.psum_scatter(partial_grad, 'section', scatter_dimension=0, tiled=True)  43.4 us
  transfers between devices with their start and end apart: 4, of which 3 were waited for; matrix products, arithmetic and copies ran while one was open for 4% of the time, Pallas kernels for 0%

commit v1 on v0

v1 whole, which is shorter than its diff:
```python
import jax
import jax.numpy as jnp
from jax import lax
from jax.experimental import pallas as pl
from jax.experimental.pallas import tpu as pltpu
from jax.sharding import Mesh, PartitionSpec as P

CHIPS = ("y", "x", "z")
ALL = ("y", "x", "z", "c")
LANES = 128


def swap_cores(value):
    return lax.ppermute(value, "c", [(0, 1), (1, 0)])


def encode_ids(ids):
    digits = [(ids >> 12) & 63, (ids >> 6) & 63, ids & 63]
    return [digit.astype(jnp.bfloat16) for digit in digits]


def decode_ids(digits):
    high, mid, low = (digits[:, place].astype(jnp.int32) for place in range(3))
    return (high << 12) + (mid << 6) + low


def feature_partials(core, slopes, head_weight):
    tokens, rows = slopes.shape
    width = head_weight.shape[1]
    blocks = width // (2 * LANES)

    def kernel(core_ref, slopes_ref, first_ref, second_ref, out_ref):
        pair = jnp.concatenate([first_ref[...], second_ref[...]], axis=1)
        total = jnp.dot(slopes_ref[...], pair, preferred_element_type=jnp.float32)
        total = total.astype(jnp.bfloat16)
        out_ref[0] = total[:, :LANES]
        out_ref[1] = total[:, LANES:]

    return pl.pallas_call(
        kernel,
        out_shape=jax.ShapeDtypeStruct((blocks, tokens, LANES), jnp.bfloat16),
        grid_spec=pltpu.PrefetchScalarGridSpec(
            num_scalar_prefetch=1,
            grid=(blocks // 2,),
            in_specs=[
                pl.BlockSpec((tokens, rows), lambda i, core: (0, 0)),
                pl.BlockSpec((rows, LANES), lambda i, core: (0, 4 * i + core[0])),
                pl.BlockSpec((rows, LANES), lambda i, core: (0, 4 * i + 2 + core[0])),
            ],
            out_specs=pl.BlockSpec((2, tokens, LANES), lambda i, core: (i, 0, 0)),
        ),
        compiler_params=pltpu.CompilerParams(vmem_limit_bytes=16 * 1024 * 1024),
        cost_estimate=pl.CostEstimate(
            flops=tokens * rows * width,
            bytes_accessed=rows * width + tokens * rows * 2 + tokens * width,
            transcendentals=0,
        ),
    )(core, slopes, head_weight, head_weight)


def local(hidden, targets, token_weight, head_weight, token_ids, embed_cotangent, new_rows):
    core = lax.axis_index("c")
    chips = lax.axis_size("y") * lax.axis_size("x") * lax.axis_size("z")
    devices = 2 * chips
    held, width = hidden.shape
    half = width // 2
    tokens = held * devices
    voc_rows = head_weight.shape[0]

    all_cotangent = lax.all_gather(embed_cotangent, ALL, axis=0, tiled=True)

    meta = jnp.stack(
        encode_ids(targets) + encode_ids(token_ids) + [token_weight], axis=1
    )
    meta = jnp.pad(meta, ((0, 0), (0, LANES - meta.shape[1])))
    low, high = hidden[:, :half], hidden[:, half:]
    mine = jnp.concatenate([jnp.where(core == 0, low, high), meta], axis=1)
    theirs = jnp.concatenate([jnp.where(core == 0, high, low), meta], axis=1)
    theirs = swap_cores(theirs)
    block = jnp.where(
        core == 0,
        jnp.concatenate([mine, theirs], axis=0),
        jnp.concatenate([theirs, mine], axis=0),
    )
    block = jnp.broadcast_to(block[None], (chips,) + block.shape)
    gathered = lax.all_to_all(block, CHIPS, 0, 0, tiled=True)
    near = gathered[:, :, :half]
    far = swap_cores(near)
    near, far = near.reshape(tokens, half), far.reshape(tokens, half)
    all_hidden = jnp.where(
        core == 0,
        jnp.concatenate([near, far], axis=1),
        jnp.concatenate([far, near], axis=1),
    )
    all_meta = gathered[:, :, half:].reshape(tokens, LANES)
    all_targets = decode_ids(all_meta[:, 0:3])
    all_ids = decode_ids(all_meta[:, 3:6])
    weights = all_meta[:, 6].astype(jnp.float32)

    device = ((lax.axis_index("y") * lax.axis_size("x") + lax.axis_index("x"))
              * lax.axis_size("z") + lax.axis_index("z")) * 2 + core
    row_ids = device * voc_rows + jnp.arange(voc_rows, dtype=jnp.int32)
    inside = (row_ids[:, None] >= new_rows[None, :, 0]) & (row_ids[:, None] < new_rows[None, :, 1])
    trainable = jnp.any(inside, axis=1)

    logits = lax.dot_general(
        all_hidden, head_weight, (((1,), (1,)), ((), ())), preferred_element_type=jnp.float32
    )
    target_hits = all_targets[:, None] == row_ids[None, :]
    peak_local = jnp.max(logits, axis=1)
    total_local = jnp.sum(jnp.exp(logits - peak_local[:, None]), axis=1)
    picked_local = jnp.sum(jnp.where(target_hits, logits, 0.0), axis=1)

    stats = jnp.concatenate([peak_local, total_local, picked_local])
    stats = jnp.broadcast_to(stats[None, None], (devices, 1, 3 * tokens))
    stats = lax.all_to_all(stats, ALL, 0, 0, tiled=True)[:, 0]
    peaks, totals, picks = stats[:, :tokens], stats[:, tokens:2 * tokens], stats[:, 2 * tokens:]
    row_peak = jnp.max(peaks, axis=0)
    exp_total = jnp.sum(totals * jnp.exp(peaks - row_peak[None]), axis=0)
    picked = jnp.sum(picks, axis=0)
    log_norm = row_peak + jnp.log(exp_total)
    mean_loss = jnp.sum(weights * (log_norm - picked)) / jnp.sum(weights)

    slopes = (
        weights[:, None] * (jnp.exp(logits - log_norm[:, None]) - target_hits.astype(jnp.float32))
    ).astype(jnp.bfloat16)

    away = feature_partials((1 - core)[None].astype(jnp.int32), slopes, head_weight)
    away = swap_cores(away)
    home = feature_partials(core[None].astype(jnp.int32), slopes, head_weight)
    pair = (home.astype(jnp.float32) + away.astype(jnp.float32)).astype(jnp.bfloat16)
    sections = lax.axis_size("y")
    owned = tokens // sections
    pair = pair.reshape(chips // sections, sections, owned, LANES).transpose(1, 0, 2, 3)
    pair = pair.reshape(chips, owned, LANES)
    parts = lax.all_to_all(pair, CHIPS, 0, 0, tiled=True)
    grad_hidden = jnp.sum(parts.astype(jnp.float32), axis=0).astype(jnp.bfloat16)

    gate = trainable[None, :]
    head_slopes = jnp.where(gate, slopes, jnp.zeros_like(slopes))
    grad_head = lax.dot_general(
        head_slopes, all_hidden, (((0,), (0,)), ((), ())), preferred_element_type=jnp.float32
    ).astype(jnp.bfloat16)
    onehot = ((all_ids[:, None] == row_ids[None, :]) & gate).astype(jnp.bfloat16)
    grad_embed = lax.dot_general(
        onehot, all_cotangent, (((0,), (0,)), ((), ())), preferred_element_type=jnp.float32
    ).astype(jnp.bfloat16)
    return (mean_loss, grad_hidden, grad_head, grad_embed)


def solution(mesh):
    grid = Mesh(mesh.devices.reshape(4, 4, 4, 2), ALL)
    rows = P(ALL)
    in_specs = (P(ALL, None), rows, rows, P(ALL, None), rows, P(ALL, None), P())
    out_specs = (P(), P("y", ("x", "z", "c")), P(ALL, None), P(ALL, None))
    return jax.shard_map(local, mesh=grid, in_specs=in_specs, out_specs=out_specs, check_vma=False)
```

time: 488 us -> 131 us (0.27)
  the two profiles are of different devices: /device:TPU:0 before, /device:TPU:3 now
where the time goes in v1:
time: 131 us; the launch traced here: 130 us
  blocking collectives  28.4 us (22%)
  waiting for transfers between devices  22.2 us (17%)
  matrix products  19.4 us (15%)
  between operations  16.7 us (13%)
  local copies, waits for them, and re-layouts  16.4 us (13%)
  starting transfers between devices  14.2 us (11%)
  Pallas kernels  7.48 us (6%)
  other arithmetic  5.44 us (4%)
    all_to_all x1, blocking collectives, local(): gathered = lax.all_to_all(block, CHIPS, 0, 0, tiled=True)  28.4 us
    all_to_all x1, waiting for transfers between devices, local(): stats = lax.all_to_all(stats, ALL, 0, 0, tiled=True)[:, 0]  10.6 us
    unnamed x20, local copies, waits for them, and re-layouts  10.2 us
    all_gather x1, waiting for transfers between devices, local(): all_cotangent = lax.all_gather(embed_cotangent, ALL, axis=0, tiled=True)  9.16 us
    pallas_call x2, Pallas kernels, feature_partials(): pl.pallas_call(kernel, out_shape=jax.ShapeDtypeStruct((blocks, tokens, LA...  7.48 us
    dot_general x1, matrix products, local(): lax.dot_general(head_slopes, all_hidden, (((0,), (0,)), ((), ())), prefer...  7.36 us
    dot_general x1, matrix products, local(): lax.dot_general(all_hidden, head_weight, (((1,), (1,)), ((), ())), prefer...  6.23 us
    dot_general x1, matrix products, local(): lax.dot_general(onehot, all_cotangent, (((0,), (0,)), ((), ())), preferre...  5.85 us
  transfers between devices with their start and end apart: 6, of which 4 were waited for; matrix products, arithmetic and copies ran while one was open for 22% of the time, Pallas kernels for 6%

profile of v1, /device:TPU:3, one launch (start us, length us, event | category | flops | bytes accessed | tf_op | source)
XLA Modules:
  0.0 130.2 jit_solution(17868605180456935925)
XLA Ops:
  7.2 0.8 copy.50
  10.0 0.7 broadcast_select_fusion.1
  10.8 0.8 collective-permute-start
  11.6 0.8 collective-permute-done
  12.7 28.4 %all_to_all.15 = bf16[64,4,2176]{2,1,0:T(4,128)(2,1)S(1)} all-to-all(bf16[64,4,2176]{2,1,0:T(4,128)(2,1)S(1)} %broadcast_in_dim.19), channel_id=1, replica_groups=mesh['y'=4,'x'=4,'z'=4,'c'=2] {'y','x','z'}, dimensions={0} | all-to-all | bytes 2228224 | tf_op jit(solution)/shard_map/all_to_all | solution.py:86
  41.7 2.0 %collective-permute-start.1 = (bf16[64,4,2048]{2,1,0:T(4,128)(2,1)S(1)}, bf16[64,4,2048]{2,1,0:T(4,128)(2,1)}, u32[]{:S(2)}, u32[]{:S(2)}) collective-permute-start(bf16[64,4,2048]{2,1,0:T(4,128)(2,1)S(1)} %slice.74), channel_id=1, source_target_pairs={{0,1},{1,0},{2,3},{3,2},{4,5},{5,4},{6,7},{7,6},{8,9},{9,8},{10,11... | collective-permute-start | bytes 3145736 | tf_op jit(solution)/shard_map/ppermute | solution.py:14
  44.6 1.6 %collective-permute-done.1 = bf16[64,4,2048]{2,1,0:T(4,128)(2,1)} collective-permute-done((bf16[64,4,2048]{2,1,0:T(4,128)(2,1)S(1)}, bf16[64,4,2048]{2,1,0:T(4,128)(2,1)}, u32[]{:S(2)}, u32[]{:S(2)}) %collective-permute-start.1) | collective-permute-done | bytes 1048608 | tf_op jit(solution)/shard_map/ppermute | solution.py:14
  46.2 1.3 %reshape.77 = bf16[256,2048]{1,0:T(8,128)(2,1)S(1)} reshape(bf16[64,4,2048]{2,1,0:T(4,128)(2,1)} %collective-permute-done.1) | data formatting | bytes 2097152 | tf_op jit(solution)/shard_map/reshape | solution.py:89
  47.5 6.2 %fusion.18 = (f32[256]{0:T(256)S(1)}, f32[256,1024]{1,0:T(8,128)S(1)}) fusion(bf16[1024,4096]{1,0:T(8,128)(2,1)} %second_ref.3, bf16[256,2048]{1,0:T(8,128)(2,1)S(1)} %reshape.77, bf16[256,2048]{1,0:T(8,128)(2,1)S(1)} %reshape.76, pred[]{:T(512)S(6)} %eq.16), kind=kOutput, calls=%fused_computation.50 | convolution fusion | flops 2157182720 | bytes 11535361 | tf_op jit(solution)/shard_map/dot_general | solution.py:106
  54.2 1.0 broadcast_in_dim.21
  55.1 4.9 %all-to-all-start.1 = ((f32[128,1,768]{2,1,0:T(1,128)}), f32[128,1,768]{2,1,0:T(1,128)S(1)}, u32[]{:S(2)}, u32[]{:S(2)}) async-start(f32[128,1,768]{2,1,0:T(1,128)} %broadcast_in_dim.21), calls=%async_computation.1 | async-start | bytes 786432 | tf_op jit(solution)/shard_map/all_to_all | solution.py:116
  60.7 10.6 %all-to-all-done.1 = f32[128,1,768]{2,1,0:T(1,128)S(1)} async-done(((f32[128,1,768]{2,1,0:T(1,128)}), f32[128,1,768]{2,1,0:T(1,128)S(1)}, u32[]{:S(2)}, u32[]{:S(2)}) %all-to-all-start.1) | async-done | bytes 393248 | tf_op jit(solution)/shard_map/all_to_all | solution.py:116
  72.4 3.4 %copy-done = bf16[1024,4096]{1,0:T(8,128)(2,1)S(1)} copy-done((bf16[1024,4096]{1,0:T(8,128)(2,1)S(1)}, bf16[1024,4096]{1,0:T(8,128)(2,1)}, u32[]{:S(2)}) %copy-start) | copy-done | bytes 8388632
  75.8 3.7 %shard_map.103 = bf16[16,256,128]{2,1,0:T(8,128)(2,1)S(1)} custom-call(s32[1]{0:T(128)} %bitcast.10.core_ref, bf16[256,1024]{1,0:T(8,128)(2,1)S(1)} %fusion.3.slopes_ref, bf16[1024,4096]{1,0:T(8,128)(2,1)S(1)} %copy-done, bf16[1024,4096]{1,0:T(8,128)(2,1)S(1)} %copy-done), custom_call_target="tpu_custom_call" | custom-call | flops 1073741824 | bytes 5767168 | tf_op jit(solution)/shard_map/pallas_call | solution.py:39
  79.6 1.2 collective-permute-start.2
  82.6 3.4 %copy-done.1 = bf16[1024,4096]{1,0:T(8,128)(2,1)S(1)} copy-done((bf16[1024,4096]{1,0:T(8,128)(2,1)S(1)}, bf16[1024,4096]{1,0:T(8,128)(2,1)}, u32[]{:S(2)}) %copy-start.1) | copy-done | bytes 8388632
  86.0 3.7 %shard_map.102 = bf16[16,256,128]{2,1,0:T(8,128)(2,1)S(1)} custom-call(s32[1]{0:T(128)} %bitcast.9.core_ref, bf16[256,1024]{1,0:T(8,128)(2,1)S(1)} %fusion.3.slopes_ref, bf16[1024,4096]{1,0:T(8,128)(2,1)S(1)} %copy-done.1, bf16[1024,4096]{1,0:T(8,128)(2,1)S(1)} %copy-done.1), custom_call_target="tpu_custom_call" | custom-call | flops 1073741824 | bytes 5767168 | tf_op jit(solution)/shard_map/pallas_call | solution.py:39
  90.0 1.1 copy.54
  91.1 5.2 %all-to-all-start.2 = ((bf16[64,64,128]{2,1,0:T(8,128)(2,1)}), bf16[64,64,128]{2,1,0:T(8,128)(2,1)S(1)}, u32[]{:S(2)}, u32[]{:S(2)}) async-start(bf16[64,64,128]{2,1,0:T(8,128)(2,1)} %bitcast.13), calls=%async_computation.2 | async-start | bytes 2097152 | tf_op jit(solution)/shard_map/all_to_all | solution.py:136
  96.3 7.4 %convolution_convert_fusion.1 = bf16[1024,4096]{1,0:T(8,128)(2,1)} fusion(bf16[256,1024]{1,0:T(8,128)(2,1)S(1)} %fusion.3.slopes_ref, pred[1024]{0:T(1024)(128)(4,1)S(1)} %and_reduce_fusion, bf16[256,2048]{1,0:T(8,128)(2,1)} %copy-done.4, bf16[256,2048]{1,0:T(8,128)(2,1)S(1)} %copy-done.3, pred[]{:T(512)S(6)} %eq.16), kind=kOutput, calls=%fused_computation.1 | convolution fusion | flops 2161377280 | bytes 11011073 | tf_op jit(solution)/shard_map/dot_general | solution.py:141
  103.7 9.2 %all-gather.3.cloned.1.call-done = bf16[128,2,4096]{2,1,0:T(2,128)(2,1)} async-done(((bf16[1,2,4096]{2,1,0:T(2,128)(2,1)}), bf16[128,2,4096]{2,1,0:T(2,128)(2,1)}) %all-gather.3.cloned.1.call-update) | async-done | bytes 2097168 | tf_op jit(solution)/shard_map/all_gather | solution.py:70
  112.9 2.7 %reshape.82 = bf16[256,4096]{1,0:T(8,128)(2,1)S(1)} reshape(bf16[128,2,4096]{2,1,0:T(2,128)(2,1)} %all-gather.3.cloned.1.call-done) | data formatting | bytes 4194304
  115.6 5.9 %convolution_convert_fusion = bf16[1024,4096]{1,0:T(8,128)(2,1)} fusion(bf16[256,4096]{1,0:T(8,128)(2,1)S(1)} %reshape.82, s32[1024]{0:T(1024)S(1)} %iota_add_fusion, s32[256]{0:T(256)S(1)} %bitcast.38, pred[1024]{0:T(1024)(128)(4,1)S(1)} %and_reduce_fusion), kind=kOutput, calls=%fused_computation | convolution fusion | flops 2152202240 | bytes 10491904 | tf_op jit(solution)/shard_map/dot_general | solution.py:145
  121.5 0.8 reduce_sum.72
  (51 shorter events, 6.7 us)
Async XLA Ops:
  7.2 105.7 %all-gather.3.cloned.1.call-start = ((), (), s32[]{:S(2)}) async-start(), calls=%async_computation.3 | async-start | bytes 2113536 | tf_op jit(solution)/shard_map/all_gather | solution.py:70
  10.8 1.6 %collective-permute-start = (bf16[2,2176]{1,0:T(2,128)(2,1)S(1)}, bf16[2,2176]{1,0:T(2,128)(2,1)S(1)}, u32[]{:S(2)}, u32[]{:S(2)}) collective-permute-start(bf16[2,2176]{1,0:T(2,128)(2,1)S(1)} %pad_maximum_fusion), channel_id=1, source_target_pairs={{0,1},{1,0},{2,3},{3,2},{4,5},{5,4},{6,7},{7,6},{8,9},{9,8},{10,11... | collective-permute-start | bytes 26120 | tf_op jit(solution)/shard_map/ppermute | solution.py:14
  41.7 4.4 %collective-permute-start.1 = (bf16[64,4,2048]{2,1,0:T(4,128)(2,1)S(1)}, bf16[64,4,2048]{2,1,0:T(4,128)(2,1)}, u32[]{:S(2)}, u32[]{:S(2)}) collective-permute-start(bf16[64,4,2048]{2,1,0:T(4,128)(2,1)S(1)} %slice.74), channel_id=1, source_target_pairs={{0,1},{1,0},{2,3},{3,2},{4,5},{5,4},{6,7},{7,6},{8,9},{9,8},{10,11... | collective-permute-start | bytes 3145736 | tf_op jit(solution)/shard_map/ppermute | solution.py:14
  44.1 9.7 %copy-start.2 = (bf16[256,2048]{1,0:T(8,128)(2,1)}, bf16[256,2048]{1,0:T(8,128)(2,1)S(1)}, u32[]{:S(2)}) copy-start(bf16[256,2048]{1,0:T(8,128)(2,1)S(1)} %reshape.76) | copy-start | bytes 3145732
  47.5 6.3 %copy-start.4 = (bf16[256,2048]{1,0:T(8,128)(2,1)}, bf16[256,2048]{1,0:T(8,128)(2,1)S(1)}, u32[]{:S(2)}) copy-start(bf16[256,2048]{1,0:T(8,128)(2,1)S(1)} %reshape.77) | copy-start | bytes 3145732
  55.1 16.2 %all-to-all-start.1 = ((f32[128,1,768]{2,1,0:T(1,128)}), f32[128,1,768]{2,1,0:T(1,128)S(1)}, u32[]{:S(2)}, u32[]{:S(2)}) async-start(f32[128,1,768]{2,1,0:T(1,128)} %broadcast_in_dim.21), calls=%async_computation.1 | async-start | bytes 786432 | tf_op jit(solution)/shard_map/all_to_all | solution.py:116
  72.4 3.4 %copy-start = (bf16[1024,4096]{1,0:T(8,128)(2,1)S(1)}, bf16[1024,4096]{1,0:T(8,128)(2,1)}, u32[]{:S(2)}) copy-start(bf16[1024,4096]{1,0:T(8,128)(2,1)} %second_ref.3) | copy-start | bytes 25165828
  75.8 5.0 %copy-start.5 = (s32[8,2]{0,1:T(2,128)S(1)}, s32[8,2]{0,1:T(2,128)}, u32[]{:S(2)}) copy-start(s32[8,2]{0,1:T(2,128)} %param.13) | copy-start | bytes 196
  79.6 10.1 %collective-permute-start.2 = (bf16[16,256,128]{2,1,0:T(8,128)(2,1)S(1)}, bf16[16,256,128]{2,1,0:T(8,128)(2,1)S(1)}, u32[]{:S(2)}, u32[]{:S(2)}) collective-permute-start(bf16[16,256,128]{2,1,0:T(8,128)(2,1)S(1)} %shard_map.103), channel_id=1, source_target_pairs={{0,1},{1,0},{2,3},{3,2},{4,5},{5,4},{6,7},{7,6},{8,9},{9,8},{10,11... | collective-permute-start | bytes 3145736 | tf_op jit(solution)/shard_map/ppermute | solution.py:14
  82.6 3.4 %copy-start.1 = (bf16[1024,4096]{1,0:T(8,128)(2,1)S(1)}, bf16[1024,4096]{1,0:T(8,128)(2,1)}, u32[]{:S(2)}) copy-start(bf16[1024,4096]{1,0:T(8,128)(2,1)} %second_ref.3) | copy-start | bytes 25165828
  90.0 6.3 %copy-start.3 = (bf16[256,2048]{1,0:T(8,128)(2,1)S(1)}, bf16[256,2048]{1,0:T(8,128)(2,1)}, u32[]{:S(2)}) copy-start(bf16[256,2048]{1,0:T(8,128)(2,1)} %copy-done.2) | copy-start | bytes 3145732
  91.1 30.4 %all-to-all-start.2 = ((bf16[64,64,128]{2,1,0:T(8,128)(2,1)}), bf16[64,64,128]{2,1,0:T(8,128)(2,1)S(1)}, u32[]{:S(2)}, u32[]{:S(2)}) async-start(bf16[64,64,128]{2,1,0:T(8,128)(2,1)} %bitcast.13), calls=%async_computation.2 | async-start | bytes 2097152 | tf_op jit(solution)/shard_map/all_to_all | solution.py:136
Sparse Core Ops, SparseCore 0:
  43.9 68.9 all-gather.2

commit v2 on v0

v2 whole, which is shorter than its diff:
```python
import jax
import jax.numpy as jnp
from jax import lax
from jax.experimental import pallas as pl
from jax.experimental.pallas import tpu as pltpu
from jax.sharding import Mesh, PartitionSpec as P

CHIPS = ("y", "x", "z")
ALL = ("y", "x", "z", "c")
LANES = 128
VMEM_LIMIT = 24 * 1024 * 1024
F32, BF16, I32 = jnp.float32, jnp.bfloat16, jnp.int32
NT = (((1,), (1,)), ((), ()))
WHOLE = pl.BlockSpec(memory_space=pltpu.VMEM)
IN_HBM = pl.BlockSpec(memory_space=pltpu.HBM)


def call(kernel, name, out_shape, grid, in_specs, out_specs, scratch, flops, moved, scalars, *arrays):
    return pl.pallas_call(
        kernel,
        name=name,
        out_shape=out_shape,
        grid_spec=pltpu.PrefetchScalarGridSpec(
            num_scalar_prefetch=len(scalars),
            grid=grid,
            in_specs=in_specs,
            out_specs=out_specs,
            scratch_shapes=scratch,
        ),
        compiler_params=pltpu.CompilerParams(vmem_limit_bytes=VMEM_LIMIT),
        cost_estimate=pl.CostEstimate(flops=flops, bytes_accessed=moved, transcendentals=0),
    )(*scalars, *arrays)


def in_hbm(value):
    return pltpu.with_memory_space_constraint(value, pltpu.HBM)


def swap_cores(value):
    return lax.ppermute(value, "c", [(0, 1), (1, 0)])


def own_block(core, targets, weights, ids, hidden, cotangent):
    held, width = hidden.shape
    half = width // 2

    def kernel(core_ref, targets_hbm, weights_ref, ids_hbm, hidden_hbm, cotangent_hbm, mine_ref, theirs_ref,
               targets_ref, ids_ref, hidden_ref, cotangent_ref, sems):
        pairs = [(targets_hbm, targets_ref), (ids_hbm, ids_ref),
                 (hidden_hbm, hidden_ref), (cotangent_hbm, cotangent_ref)]
        copies = [pltpu.make_async_copy(source, target, sems.at[place])
                  for place, (source, target) in enumerate(pairs)]
        for copy in copies:
            copy.start()
        for copy in copies:
            copy.wait()
        row = lax.broadcasted_iota(I32, (held, LANES), 0)
        lane = lax.broadcasted_iota(I32, (held, LANES), 1)
        meta = jnp.zeros((held, LANES), F32)
        for token in range(held):
            target, name = targets_ref[token], ids_ref[token]
            values = [(target >> 12) & 63, (target >> 6) & 63, target & 63,
                      (name >> 12) & 63, (name >> 6) & 63, name & 63]
            values = [value.astype(F32) for value in values] + [weights_ref[token]]
            for place, value in enumerate(values):
                meta = jnp.where((row == token) & (lane == place), value, meta)
        meta = meta.astype(BF16)
        low = jnp.concatenate([hidden_ref[:, :half], meta, cotangent_ref[:, :half]], axis=1)
        high = jnp.concatenate([hidden_ref[:, half:], meta, cotangent_ref[:, half:]], axis=1)

        @pl.when(core_ref[0] == 0)
        def _():
            mine_ref[...] = low
            theirs_ref[...] = high

        @pl.when(core_ref[0] == 1)
        def _():
            mine_ref[...] = high
            theirs_ref[...] = low

    shape = jax.ShapeDtypeStruct((held, width + LANES), BF16)
    return call(
        kernel, "own_block", [shape, shape], (),
        [IN_HBM, pl.BlockSpec(memory_space=pltpu.SMEM), IN_HBM, IN_HBM, IN_HBM], [WHOLE] * 2,
        [
            pltpu.SMEM((held,), I32), pltpu.SMEM((held,), I32),
            pltpu.VMEM((held, width), BF16), pltpu.VMEM((held, width), BF16),
            pltpu.SemaphoreType.DMA((4,)),
        ], 0, 8 * held * width, [core],
        in_hbm(targets), weights, in_hbm(ids), in_hbm(hidden), in_hbm(cotangent),
    )


def chip_blocks(core, chips, mine, theirs):
    held, width = mine.shape

    def kernel(core_ref, mine_ref, theirs_ref, out_ref):
        own, other = mine_ref[...].astype(F32), theirs_ref[...].astype(F32)
        first = core_ref[0] == 0
        both = jnp.concatenate([jnp.where(first, own, other), jnp.where(first, other, own)], axis=0).astype(BF16)
        out_ref[...] = jnp.broadcast_to(both[None], out_ref.shape)

    return call(
        kernel, "chip_blocks", jax.ShapeDtypeStruct((chips, 2 * held, width), BF16), (),
        [WHOLE] * 2, WHOLE, [], 0, 4 * chips * held * width, [core], mine, theirs,
    )


def token_rows(gathered):
    chips, held, width = gathered.shape
    tokens, half = chips * held, (width - LANES) // 2

    def kernel(gathered_ref, hidden_ref, cotangent_ref, info_ref):
        hidden_ref[...] = gathered_ref[:, :, :half].reshape(tokens, half)
        cotangent_ref[...] = gathered_ref[:, :, half + LANES:].reshape(tokens, half)
        rows = jnp.transpose(gathered_ref[:, :, half:half + LANES].reshape(tokens, LANES).astype(F32))
        targets = rows[0:1] * 4096.0 + rows[1:2] * 64.0 + rows[2:3]
        ids = rows[3:4] * 4096.0 + rows[4:5] * 64.0 + rows[5:6]
        info_ref[...] = jnp.concatenate([targets, ids, rows[6:7], jnp.zeros((5, tokens), F32)], axis=0)

    shape = jax.ShapeDtypeStruct((tokens, half), BF16)
    return call(
        kernel, "token_rows", [shape, shape, jax.ShapeDtypeStruct((8, tokens), F32)],
        (), [WHOLE], [WHOLE] * 3, [], 0, 4 * tokens * width, [], gathered,
    )


def near_logits(core, gathered, head_weight):
    tokens = gathered.shape[0]
    rows, width = head_weight.shape
    half, step = width // 2, 256

    def kernel(core_ref, gathered_ref, head_hbm, out_ref, head_ref, sems):
        copies = [
            pltpu.make_async_copy(
                head_hbm.at[pl.ds(place, step)], head_ref.at[pl.ds(place, step)], sems.at[place // step])
            for place in range(0, rows, step)]
        for copy in copies:
            copy.start()
        columns = pl.ds(pl.multiple_of(core_ref[0] * half, half), half)
        for copy, place in zip(copies, range(0, rows, step)):
            copy.wait()
            out_ref[place:place + step, :] = lax.dot_general(
                head_ref[place:place + step, columns], gathered_ref[:, :half], NT, preferred_element_type=F32)

    return call(
        kernel, "near_logits",
        [jax.ShapeDtypeStruct((rows, tokens), F32), pltpu.VMEM((rows, width), BF16)],
        (), [WHOLE, IN_HBM], [WHOLE] * 2,
        [pltpu.SemaphoreType.DMA((rows // step,))],
        2 * tokens * rows * half, 4 * rows * half, [core], gathered, in_hbm(head_weight),
    )


def feature_products(side, left_ref, head_ref, first, blocks):
    count = left_ref.shape[0]
    for block in range(first, first + blocks, 2):
        columns = jnp.concatenate([
            head_ref[:, pl.ds(pl.multiple_of((2 * place + side) * LANES, LANES), LANES)]
            for place in (block, block + 1)], axis=1)
        for line in range(0, count, count // 2):
            lines = slice(line, line + count // 2)
            total = jnp.dot(left_ref[lines, :], columns, preferred_element_type=F32).astype(BF16)
            yield block, lines, total[:, :LANES], total[:, LANES:]


def far_logits(core, start, devices, partial, info, gathered, head_weight):
    tokens = gathered.shape[0]
    rows, width = head_weight.shape
    half, step = width // 2, 256
    blocks = half // LANES

    def kernel(core_ref, start_ref, partial_ref, info_ref, gathered_ref, head_ref,
               logits_hbm, stats_hbm, left_hbm, away_hbm,
               logits_ref, stats_ref, left_ref, away_ref, sems, away_sems):
        other = 1 - core_ref[0]
        columns = pl.ds(pl.multiple_of(other * half, half), half)
        for place in range(0, rows, step):
            logits_ref[place:place + step, :] = partial_ref[place:place + step, :] + lax.dot_general(
                head_ref[place:place + step, columns], gathered_ref[:, :half], NT, preferred_element_type=F32)
        copies = [pltpu.make_async_copy(logits_ref, logits_hbm, sems.at[0])]
        copies[-1].start()
        logits = logits_ref[...]
        peak = jnp.max(logits, axis=0, keepdims=True)
        powers = jnp.exp(logits - peak)
        total = jnp.sum(powers, axis=0, keepdims=True)
        row = lax.broadcasted_iota(I32, (rows, tokens), 0) + start_ref[0]
        hits = row == info_ref[0:1, :].astype(I32)
        picked = jnp.sum(jnp.where(hits, logits, 0.0), axis=0, keepdims=True)
        parts = [value[:, place:place + LANES] for value in (peak, total, picked) for place in range(0, tokens, LANES)]
        block = jnp.concatenate(parts + [jnp.zeros((8 - len(parts), LANES), F32)], axis=0)
        stats_ref[...] = jnp.broadcast_to(block[None], stats_ref.shape)
        copies.append(pltpu.make_async_copy(stats_ref, stats_hbm, sems.at[1]))
        copies[-1].start()
        left_ref[:tokens, :] = jnp.transpose(jnp.where(hits, 0.0, powers)).astype(BF16)
        left_ref[tokens:, :] = jnp.transpose(hits.astype(F32)).astype(BF16)
        copies.append(pltpu.make_async_copy(left_ref, left_hbm, sems.at[2]))
        copies[-1].start()
        for first in range(0, blocks, 4):
            for block, lines, even, odd in feature_products(other, left_ref, head_ref, first, 4):
                away_ref[block, lines, :] = even
                away_ref[block + 1, lines, :] = odd
            part = pl.ds(first, 4)
            copies.append(pltpu.make_async_copy(away_ref.at[part], away_hbm.at[part], away_sems.at[first // 4]))
            copies[-1].start()
        for copy in copies:
            copy.wait()

    shapes = [
        ((rows, tokens), F32), ((devices, 8, LANES), F32),
        ((2 * tokens, rows), BF16), ((blocks, 2 * tokens, LANES), BF16),
    ]
    return call(
        kernel, "far_logits", [pltpu.HBM(*shape) for shape in shapes],
        (), [WHOLE] * 4, [IN_HBM] * 4,
        [pltpu.VMEM(*shape) for shape in shapes]
        + [pltpu.SemaphoreType.DMA((3,)), pltpu.SemaphoreType.DMA((blocks // 4,))],
        6 * tokens * rows * half, 2 * rows * half, [core, start], partial, info, gathered, head_weight,
    )


def feature_partials(core, left, head_weight):
    count, rows = left.shape
    width = head_weight.shape[1]
    blocks = width // (2 * LANES)
    step = 1024
    held = step // (2 * LANES)

    def kernel(core_ref, left_ref, head_ref, out_ref):
        for block, lines, even, odd in feature_products(core_ref[0], left_ref, head_ref, 0, held):
            out_ref[block, lines, :] = even
            out_ref[block + 1, lines, :] = odd

    return call(
        kernel, "feature_partials", pltpu.HBM((blocks, count, LANES), BF16), (width // step,),
        [
            pl.BlockSpec((count, rows), lambda i, core: (0, 0)),
            pl.BlockSpec((rows, step), lambda i, core: (0, i)),
        ],
        pl.BlockSpec((held, count, LANES), lambda i, core: (i, 0, 0)),
        [], count * rows * width, 2 * rows * width, [core], in_hbm(left), in_hbm(head_weight),
    )


def scaled_pair(device, stats, info, home, away):
    tokens = info.shape[1]
    blocks = home.shape[0]
    sections = lax.axis_size("y")
    owned = tokens // sections
    lines = tokens // LANES

    def kernel(device_ref, stats_hbm, info_ref, home_hbm, away_hbm, out_hbm, norm_ref, loss_ref,
               stats_ref, home_ref, away_ref, out_ref, stats_sem, in_sems, out_sems):
        stats_copy = pltpu.make_async_copy(stats_hbm, stats_ref, stats_sem)
        stats_copy.start()
        loads = []
        for section in range(sections):
            power = pl.ds(section * owned, owned)
            hit = pl.ds(tokens + section * owned, owned)
            loads.append([
                pltpu.make_async_copy(source.at[:, part, :], target.at[:, part, :], in_sems.at[section, place])
                for place, (source, target, part) in enumerate([
                    (home_hbm, home_ref, power), (away_hbm, away_ref, power),
                    (home_hbm, home_ref, hit), (away_hbm, away_ref, hit)])])
            for load in loads[-1]:
                load.start()

        def flat(block, first):
            return jnp.concatenate([block[first + line:first + line + 1] for line in range(lines)], axis=1)

        stats_copy.wait()
        everyone = stats_ref[...]
        peaks = jnp.max(everyone, axis=0)
        factors = jnp.exp(everyone[:, :lines] - peaks[None, :lines])
        total = jnp.sum(everyone[:, lines:2 * lines] * factors, axis=0)
        picked = flat(jnp.sum(everyone, axis=0), 2 * lines)
        norm = flat(peaks, 0) + jnp.log(flat(total, 0))
        weights = info_ref[2:3, :]
        norm_ref[...] = norm
        loss_ref[...] = (jnp.sum(weights * (norm - picked), axis=1, keepdims=True)
                         / jnp.sum(weights, axis=1, keepdims=True))
        here = device_ref[0]
        own = flat(stats_ref[here], 0)
        other = flat(stats_ref[here + 1 - 2 * (here & 1)], 0)
        scale = jnp.transpose(jnp.concatenate([
            weights * jnp.exp(own - norm),
            weights * jnp.exp(other - norm),
            weights * (jnp.exp(picked - norm) - 1.0),
            jnp.zeros((5, tokens), F32),
        ], axis=0))
        stores = []
        for section in range(sections):
            for load in loads[section]:
                load.wait()
            power = slice(section * owned, (section + 1) * owned)
            hit = slice(tokens + section * owned, tokens + (section + 1) * owned)
            one, two, three = (
                jnp.broadcast_to(scale[power, place:place + 1], (owned, LANES)) for place in range(3))
            for block in range(blocks):
                value = home_ref[block, power, :].astype(F32) * one + away_ref[block, power, :].astype(F32) * two
                hits = (home_ref[block, hit, :] + away_ref[block, hit, :]).astype(F32)
                out_ref[section * blocks + block] = (value + hits * three).astype(BF16)
            part = pl.ds(section * blocks, blocks)
            stores.append(pltpu.make_async_copy(out_ref.at[part], out_hbm.at[part], out_sems.at[section]))
            stores[-1].start()
        for store in stores:
            store.wait()

    return call(
        kernel, "scaled_pair",
        [
            pltpu.HBM((sections * blocks, owned, LANES), BF16),
            jax.ShapeDtypeStruct((1, tokens), F32),
            jax.ShapeDtypeStruct((1, 1), F32),
        ],
        (), [IN_HBM, WHOLE, IN_HBM, IN_HBM], [IN_HBM, WHOLE, WHOLE],
        [
            pltpu.VMEM(stats.shape, F32), pltpu.VMEM(home.shape, BF16), pltpu.VMEM(away.shape, BF16),
            pltpu.VMEM((sections * blocks, owned, LANES), BF16),
            pltpu.SemaphoreType.DMA, pltpu.SemaphoreType.DMA((sections, 4)), pltpu.SemaphoreType.DMA((sections,)),
        ],
        10 * tokens * blocks * LANES, 10 * tokens * blocks * LANES, [device],
        in_hbm(stats), info, in_hbm(home), in_hbm(away),
    )


def summed_parts(parts):
    count, rows, width = parts.shape
    share = count // 4

    def kernel(parts_hbm, out_ref, parts_ref, sems):
        copies = [
            pltpu.make_async_copy(parts_hbm.at[pl.ds(first, share)], parts_ref.at[pl.ds(first, share)], sems.at[place])
            for place, first in enumerate(range(0, count, share))]
        for copy in copies:
            copy.start()
        total = jnp.zeros((rows, width), F32)
        for place, copy in enumerate(copies):
            copy.wait()
            total += jnp.sum(parts_ref[place * share:(place + 1) * share].astype(F32), axis=0)
        out_ref[...] = total.astype(BF16)

    return call(
        kernel, "summed_parts", jax.ShapeDtypeStruct((rows, width), BF16), (), [IN_HBM], WHOLE,
        [pltpu.VMEM(parts.shape, BF16), pltpu.SemaphoreType.DMA((4,))],
        count * rows * width, 2 * count * rows * width, [], in_hbm(parts),
    )


def row_gradient(name, make_left, core, start, new_rows, rows, small, near, far, step=1024):
    tokens = near.shape[0]
    half = near.shape[1]
    steps = half // step

    def kernel(core_ref, start_ref, ranges_ref, *refs):
        small_refs, (near_ref, far_ref, out_ref, left_ref) = refs[:len(small)], refs[len(small):]
        index = pl.program_id(0)

        @pl.when(index == 0)
        def _():
            lane_row = lax.broadcasted_iota(I32, (8, rows), 1) + start_ref[0]
            inside = jnp.zeros((8, rows), F32)
            for place in range(new_rows.shape[0]):
                within = (lane_row >= ranges_ref[place, 0]) & (lane_row < ranges_ref[place, 1])
                inside = jnp.where(within, 1.0, inside)
            gate = jnp.transpose(inside)[:, 0:1]
            row = lax.broadcasted_iota(I32, (rows, tokens), 0) + start_ref[0]
            left_ref[...] = jnp.where(gate > 0.0, make_left(row, *small_refs), 0.0).astype(BF16)

        @pl.when(index < steps)
        def _():
            out_ref[...] = jnp.dot(left_ref[...], near_ref[...], preferred_element_type=F32).astype(BF16)

        @pl.when(index >= steps)
        def _():
            out_ref[...] = jnp.dot(left_ref[...], far_ref[...], preferred_element_type=F32).astype(BF16)

    def out_index(i, core, start, ranges):
        is_far = (i >= steps).astype(I32)
        side = core[0] + is_far - 2 * core[0] * is_far
        return (0, side * steps + i - is_far * steps)

    return call(
        kernel, name,
        jax.ShapeDtypeStruct((rows, 2 * half), BF16),
        (2 * steps,),
        [pl.BlockSpec(array.shape, lambda i, core, start, ranges: (0, 0)) for array in small] + [
            pl.BlockSpec((tokens, step), lambda i, core, start, ranges: (0, jnp.minimum(i, steps - 1))),
            pl.BlockSpec((tokens, step), lambda i, core, start, ranges: (0, jnp.maximum(i - steps, 0))),
        ],
        pl.BlockSpec((rows, step), out_index),
        [pltpu.VMEM((rows, tokens), BF16)],
        4 * rows * tokens * half, 4 * rows * half, [core, start, new_rows], *small, near, far,
    )


def slope_left(row, logits_ref, info_ref, norm_ref):
    hits = (row == info_ref[0:1, :].astype(I32)).astype(F32)
    return info_ref[2:3, :] * (jnp.exp(logits_ref[...] - norm_ref[...]) - hits)


def onehot_left(row, info_ref):
    return (row == info_ref[1:2, :].astype(I32)).astype(F32)


def local(hidden, targets, token_weight, head_weight, token_ids, embed_cotangent, new_rows):
    core = lax.axis_index("c")
    chips = lax.axis_size("y") * lax.axis_size("x") * lax.axis_size("z")
    devices = 2 * chips
    voc_rows = head_weight.shape[0]
    device = ((lax.axis_index("y") * lax.axis_size("x") + lax.axis_index("x"))
              * lax.axis_size("z") + lax.axis_index("z")) * 2 + core
    at_core = core[None].astype(I32)
    at_device = device[None].astype(I32)
    start = at_device * voc_rows

    mine, theirs = own_block(
        at_core, targets, token_weight.astype(F32), token_ids, hidden, embed_cotangent)
    blocks = chip_blocks(at_core, chips, mine, swap_cores(theirs))
    gathered = lax.all_to_all(blocks, CHIPS, 0, 0, tiled=True)
    near, near_cotangent, info = token_rows(gathered)
    far = swap_cores(near)
    partial, table = near_logits(at_core, near, head_weight)
    logits, stats, left, away = far_logits(at_core, start, devices, partial, info, far, table)

    stats = lax.all_to_all(stats, ALL, 0, 0, tiled=True)
    away = swap_cores(away)
    home = feature_partials(at_core, left, head_weight)
    far_cotangent = swap_cores(near_cotangent)

    pair, norm, loss = scaled_pair(at_device, stats, info, home, away)
    grad_hidden = summed_parts(lax.all_to_all(pair, CHIPS, 0, 0, tiled=True))

    grad_head = row_gradient(
        "grad_head", slope_left, at_core, start, new_rows, voc_rows, [logits, info, norm], near, far)
    grad_embed = row_gradient(
        "grad_embed", onehot_left, at_core, start, new_rows, voc_rows, [info], near_cotangent, far_cotangent)
    return (loss[0, 0], grad_hidden, grad_head, grad_embed)


def solution(mesh):
    grid = Mesh(mesh.devices.reshape(4, 4, 4, 2), ALL)
    rows = P(ALL)
    in_specs = (P(ALL, None), rows, rows, P(ALL, None), rows, P(ALL, None), P())
    out_specs = (P(), P("y", ("x", "z", "c")), P(ALL, None), P(ALL, None))
    return jax.shard_map(local, mesh=grid, in_specs=in_specs, out_specs=out_specs, check_vma=False)
```

time: 488 us -> 108 us (0.22)
  blocking collectives: 258 us -> 42.6 us
  waiting for transfers between devices: 174 us -> 12 us
  Pallas kernels: 0 us -> 38.7 us
  matrix products: 26.3 us -> 0 us
  between operations: 16.3 us -> 0.91 us
  starting transfers between devices: 0.34 us -> 12.2 us
  local copies, waits for them, and re-layouts: 9.41 us -> 0.09 us
    unnamed x2 -> x0, blocking collectives: 131 us -> none
    reduce_scatter x2 -> x0, waiting for transfers between devices: 106 us -> none  [the longest x1 62.4 us: local(): lax.psum_scatter(half_summed, 'group', scatter_dimension=1, tiled=True)]
    all_gather x2 -> x0, waiting for transfers between devices: 67.2 us -> none  [the longest x1 67.2 us: local(): lax.all_gather(embed_cotangent, ('section', 'group'), axis=0, tiled=True)]
    pmax x1 -> x0, blocking collectives: 64.4 us -> none  [local(): row_peak = lax.pmax(jnp.max(logits, axis=1), ('section', 'group'))]
    psum x1 -> x0, blocking collectives: 62.3 us -> none  [local(): lax.psum((jnp.sum(jnp.exp(logits - row_peak[:, None]), axis=1), picked_lo...]
    all_to_all x0 -> x1, blocking collectives: none -> 42.6 us  [local(): gathered = lax.all_to_all(blocks, CHIPS, 0, 0, tiled=True)]
    pallas_call x0 -> x10, Pallas kernels: none -> 38.7 us  [call(): pl.pallas_call(kernel, name=name, out_shape=out_shape, grid_spec=pltpu.Pr...]
    dot_general x4 -> x0, matrix products: 26.3 us -> none  [the longest x1 7.93 us: local(): jnp.dot(slopes, head_weight, preferred_element_type=jnp.float32)]
  transfers between devices with their start and end apart: 4 -> 6, of which waited for: 3 -> 3; matrix products, arithmetic and copies ran while one was open for 4% -> 0% of each run, Pallas kernels for 0% -> 28%
where the time goes in v2:
time: 108 us; the launch traced here: 107 us
  blocking collectives  42.6 us (39%)
  Pallas kernels  38.7 us (36%)
  starting transfers between devices  12.2 us (11%)
  waiting for transfers between devices  12 us (11%)
    all_to_all x1, blocking collectives, local(): gathered = lax.all_to_all(blocks, CHIPS, 0, 0, tiled=True)  42.6 us
    pallas_call x10, Pallas kernels, call(): pl.pallas_call(kernel, name=name, out_shape=out_shape, grid_spec=pltpu.Pr...  38.7 us
    all_to_all x1, waiting for transfers between devices, local(): stats = lax.all_to_all(stats, ALL, 0, 0, tiled=True)  6.27 us
    all_to_all x1, starting transfers between devices, local(): stats = lax.all_to_all(stats, ALL, 0, 0, tiled=True)  5.73 us
    all_to_all x1, starting transfers between devices, local(): grad_hidden = summed_parts(lax.all_to_all(pair, CHIPS, 0, 0, tiled=True))  5.71 us
    all_to_all x1, waiting for transfers between devices, local(): grad_hidden = summed_parts(lax.all_to_all(pair, CHIPS, 0, 0, tiled=True))  4.51 us
  transfers between devices with their start and end apart: 6, of which 3 were waited for; matrix products, arithmetic and copies ran while one was open for 0% of the time, Pallas kernels for 28%

profile of v2, /device:TPU:0, one launch (start us, length us, event | category | flops | bytes accessed | tf_op | source)
XLA Modules:
  0.0 107.1 jit_solution(3556111689701553111)
XLA Ops:
  0.6 0.7 convert_element_type.3.weights_ref
  1.3 1.4 %own_block.1 = (bf16[2,4224]{1,0:T(2,128)(2,1)S(1)}, bf16[2,4224]{1,0:T(2,128)(2,1)S(1)}) custom-call(s32[1]{0:T(128)} %bitcast.1.core_ref, s32[2]{0:T(128)} %targets_hbm.1, f32[2]{0:T(128)S(1)} %convert_element_type.3.weights_ref, s32[2]{0:T(128)} %ids_hbm.1, bf16[2,4096]{1,0:T(2,128)(2,1)} %hidden_hbm.1, bf16[2,4096]{1,0:T(2,128)(2,1)} %cotangent_hbm.1), custom_call_target="tpu_custom_call" | custom-call | bytes 65536 | tf_op jit(solution)/shard_map/own_block/pallas_call | solution.py:19
  2.7 0.1 collective-permute-start
  2.7 1.2 %collective-permute-done.theirs_ref = bf16[2,4224]{1,0:T(2,128)(2,1)S(1)} collective-permute-done((bf16[2,4224]{1,0:T(2,128)(2,1)S(1)}, bf16[2,4224]{1,0:T(2,128)(2,1)S(1)}, u32[]{:S(2)}, u32[]{:S(2)}) %collective-permute-start) | collective-permute-done | bytes 16928 | tf_op jit(solution)/shard_map/ppermute | solution.py:40
  3.9 0.2 chip_blocks.1
  4.1 42.6 %all_to_all.15.gathered_ref = bf16[64,4,4224]{2,1,0:T(4,128)(2,1)S(1)} all-to-all(bf16[64,4,4224]{2,1,0:T(4,128)(2,1)S(1)} %chip_blocks.1), channel_id=1, replica_groups=mesh['y'=4,'x'=4,'z'=4,'c'=2] {'y','x','z'}, dimensions={0} | all-to-all | bytes 4325376 | tf_op jit(solution)/shard_map/all_to_all | solution.py:420
  46.7 0.2 token_rows.1
  46.9 0.1 collective-permute-start.1
  47.0 4.5 %near_logits.1 = (f32[1024,256]{1,0:T(8,128)S(1)}, bf16[1024,4096]{1,0:T(8,128)(2,1)S(1)}) custom-call(s32[1]{0:T(128)} %bitcast.1.core_ref, bf16[256,2048]{1,0:T(8,128)(2,1)S(1)} %get-tuple-element.20.gathered_ref.refs_3_, bf16[1024,4096]{1,0:T(8,128)(2,1)} %head_ref.1), custom_call_target="tpu_custom_call" | custom-call | flops 1073741824 | bytes 8388608 | tf_op jit(solution)/shard_map/near_logits/pallas_call | solution.py:19
  51.5 4.9 %far_logits.1 = (f32[1024,256]{1,0:T(8,128)}, f32[128,8,128]{2,1,0:T(8,128)}, bf16[512,1024]{1,0:T(8,128)(2,1)}, bf16[16,512,128]{2,1,0:T(8,128)(2,1)}) custom-call(s32[1]{0:T(128)} %bitcast.1.core_ref, s32[1]{0:T(128)S(6)} %mul.15.start_ref, f32[1024,256]{1,0:T(8,128)S(1)} %get-tuple-element.21.partial_ref, ...), custom_call_target="tpu_custom_call" | custom-call | flops 3221225472 | bytes 4194304 | tf_op jit(solution)/shard_map/far_logits/pallas_call | solution.py:19
  56.5 0.6 collective-permute-start.2
  57.0 5.7 %all-to-all-start.1 = ((f32[128,8,128]{2,1,0:T(8,128)}), f32[128,8,128]{2,1,0:T(8,128)}, u32[]{:S(2)}, u32[]{:S(2)}) async-start(f32[128,8,128]{2,1,0:T(8,128)} %get-tuple-element.24), calls=%async_computation.1 | async-start | bytes 1048576 | tf_op jit(solution)/shard_map/all_to_all | solution.py:426
  62.8 0.1 collective-permute-start.3
  62.9 6.9 %feature_partials.1.home_hbm = bf16[16,512,128]{2,1,0:T(8,128)(2,1)} custom-call(s32[1]{0:T(128)} %bitcast.1.core_ref, bf16[512,1024]{1,0:T(8,128)(2,1)} %get-tuple-element.25.left_ref, bf16[1024,4096]{1,0:T(8,128)(2,1)} %head_ref.1), custom_call_target="tpu_custom_call" | custom-call | flops 2147483648 | bytes 8388608 | tf_op jit(solution)/shard_map/feature_partials/pallas_call | solution.py:19
  69.8 6.3 %all-to-all-done.1.stats_hbm = f32[128,8,128]{2,1,0:T(8,128)} async-done(((f32[128,8,128]{2,1,0:T(8,128)}), f32[128,8,128]{2,1,0:T(8,128)}, u32[]{:S(2)}, u32[]{:S(2)}) %all-to-all-start.1) | async-done | bytes 524320 | tf_op jit(solution)/shard_map/all_to_all | solution.py:426
  76.1 0.0 collective-permute-done.2.away_hbm
  76.1 5.2 %scaled_pair.1 = (bf16[64,64,128]{2,1,0:T(8,128)(2,1)}, f32[1,256]{1,0:T(1,128)S(1)}, f32[1,1]{1,0:T(1,128)}) custom-call(s32[1]{0:T(128)} %bitcast.device_ref, f32[128,8,128]{2,1,0:T(8,128)} %all-to-all-done.1.stats_hbm, f32[8,256]{1,0:T(8,128)S(1)} %get-tuple-element.22.info_ref.refs_1_.refs_0_, bf16[16,512,128]{2,1,0:T(8,128)(2,1)} %feature_partials.1.home_hbm, ...), custom_call_target="tpu_custom_call" | custom-call | flops 5242880 | bytes 5242880 | tf_op jit(solution)/shard_map/scaled_pair/pallas_call | solution.py:19
  81.3 5.7 %all-to-all-start.2 = ((bf16[64,64,128]{2,1,0:T(8,128)(2,1)}), bf16[64,64,128]{2,1,0:T(8,128)(2,1)}, u32[]{:S(2)}, u32[]{:S(2)}) async-start(bf16[64,64,128]{2,1,0:T(8,128)(2,1)} %get-tuple-element.28), calls=%async_computation.2 | async-start | bytes 2097152 | tf_op jit(solution)/shard_map/all_to_all | solution.py:432
  87.0 0.1 copy.11.ranges_ref
  87.1 0.0 collective-permute-done.3.refs_2_
  87.1 7.3 %grad_embed.1 = bf16[1024,4096]{1,0:T(8,128)(2,1)} custom-call(s32[1]{0:T(128)} %bitcast.1.core_ref, s32[1]{0:T(128)S(6)} %mul.15.start_ref, s32[8,2]{1,0:T(8,128)S(1)} %copy.11.ranges_ref, f32[8,256]{1,0:T(8,128)S(1)} %get-tuple-element.22.info_ref.refs_1_.refs_0_, bf16[256,2048]{1,0:T(8,128)(2,1)S(1)} %get-tuple-element.31.refs_1_, ...), custom_call_target="tpu_custom_call" | custom-call | flops 2147483648 | bytes 8388608 | tf_op jit(solution)/shard_map/grad_embed/pallas_call | solution.py:19
  94.4 6.2 %grad_head.1 = bf16[1024,4096]{1,0:T(8,128)(2,1)} custom-call(s32[1]{0:T(128)} %bitcast.1.core_ref, s32[1]{0:T(128)S(6)} %mul.15.start_ref, s32[8,2]{1,0:T(8,128)S(1)} %copy.11.ranges_ref, f32[1024,256]{1,0:T(8,128)S(1)} %copy-done, f32[8,256]{1,0:T(8,128)S(1)} %get-tuple-element.22.info_ref.refs_1_.refs_0_, f32[1,256]{1,0:T(1,128)S(1)} %get-tuple-element.30.refs_2_, ...), custom_call_target="tpu_custom_call" | custom-call | flops 2147483648 | bytes 8388608 | tf_op jit(solution)/shard_map/grad_head/pallas_call | solution.py:19
  100.6 4.5 %all-to-all-done.2.parts_hbm = bf16[64,64,128]{2,1,0:T(8,128)(2,1)} async-done(((bf16[64,64,128]{2,1,0:T(8,128)(2,1)}), bf16[64,64,128]{2,1,0:T(8,128)(2,1)}, u32[]{:S(2)}, u32[]{:S(2)}) %all-to-all-start.2) | async-done | bytes 1048608 | tf_op jit(solution)/shard_map/all_to_all | solution.py:432
  105.1 1.9 %summed_parts.1 = bf16[64,128]{1,0:T(8,128)(2,1)} custom-call(bf16[64,64,128]{2,1,0:T(8,128)(2,1)} %all-to-all-done.2.parts_hbm), custom_call_target="tpu_custom_call" | custom-call | flops 524288 | bytes 1048576 | tf_op jit(solution)/shard_map/summed_parts/pallas_call | solution.py:19
  (5 shorter events, 0.0 us)
Async XLA Ops:
  2.7 1.3 %collective-permute-start = (bf16[2,4224]{1,0:T(2,128)(2,1)S(1)}, bf16[2,4224]{1,0:T(2,128)(2,1)S(1)}, u32[]{:S(2)}, u32[]{:S(2)}) collective-permute-start(bf16[2,4224]{1,0:T(2,128)(2,1)S(1)} %get-tuple-element.19), channel_id=1, source_target_pairs={{0,1},{1,0},{2,3},{3,2},{4,5},{5,4},{6,7},{7,6},{8,9},{9,8},{10,11... | collective-permute-start | bytes 50696 | tf_op jit(solution)/shard_map/ppermute | solution.py:40
  46.9 4.6 %collective-permute-start.1 = (bf16[256,2048]{1,0:T(8,128)(2,1)S(1)}, bf16[256,2048]{1,0:T(8,128)(2,1)S(1)}, u32[]{:S(2)}, u32[]{:S(2)}) collective-permute-start(bf16[256,2048]{1,0:T(8,128)(2,1)S(1)} %get-tuple-element.20.gathered_ref.refs_3_), channel_id=1, source_target_pairs={{0,1},{1,0},{2,3},{3,2},{4,5},{5,4},{6,7},{7,6},{8,9},{9,8},{10,11... | collective-permute-start | bytes 3145736 | tf_op jit(solution)/shard_map/ppermute | solution.py:40
  56.5 19.6 %collective-permute-start.2 = (bf16[16,512,128]{2,1,0:T(8,128)(2,1)}, bf16[16,512,128]{2,1,0:T(8,128)(2,1)}, u32[]{:S(2)}, u32[]{:S(2)}) collective-permute-start(bf16[16,512,128]{2,1,0:T(8,128)(2,1)} %get-tuple-element.26), channel_id=1, source_target_pairs={{0,1},{1,0},{2,3},{3,2},{4,5},{5,4},{6,7},{7,6},{8,9},{9,8},{10,11... | collective-permute-start | bytes 6291464 | tf_op jit(solution)/shard_map/ppermute | solution.py:40
  57.0 19.0 %all-to-all-start.1 = ((f32[128,8,128]{2,1,0:T(8,128)}), f32[128,8,128]{2,1,0:T(8,128)}, u32[]{:S(2)}, u32[]{:S(2)}) async-start(f32[128,8,128]{2,1,0:T(8,128)} %get-tuple-element.24), calls=%async_computation.1 | async-start | bytes 1048576 | tf_op jit(solution)/shard_map/all_to_all | solution.py:426
  62.8 24.3 %collective-permute-start.3 = (bf16[256,2048]{1,0:T(8,128)(2,1)S(1)}, bf16[256,2048]{1,0:T(8,128)(2,1)}, u32[]{:S(2)}, u32[]{:S(2)}) collective-permute-start(bf16[256,2048]{1,0:T(8,128)(2,1)S(1)} %get-tuple-element.31.refs_1_), channel_id=1, source_target_pairs={{0,1},{1,0},{2,3},{3,2},{4,5},{5,4},{6,7},{7,6},{8,9},{9,8},{10,11... | collective-permute-start | bytes 3145736 | tf_op jit(solution)/shard_map/ppermute | solution.py:40
  69.8 17.2 %copy-start.1 = (s32[8,2]{0,1:T(2,128)S(1)}, s32[8,2]{0,1:T(2,128)}, u32[]{:S(2)}) copy-start(s32[8,2]{0,1:T(2,128)} %param.13) | copy-start | bytes 196
  81.3 23.8 %all-to-all-start.2 = ((bf16[64,64,128]{2,1,0:T(8,128)(2,1)}), bf16[64,64,128]{2,1,0:T(8,128)(2,1)}, u32[]{:S(2)}, u32[]{:S(2)}) async-start(bf16[64,64,128]{2,1,0:T(8,128)(2,1)} %get-tuple-element.28), calls=%async_computation.2 | async-start | bytes 2097152 | tf_op jit(solution)/shard_map/all_to_all | solution.py:432
  87.1 7.4 %copy-start = (f32[1024,256]{1,0:T(8,128)S(1)}, f32[1024,256]{1,0:T(8,128)}, u32[]{:S(2)}) copy-start(f32[1024,256]{1,0:T(8,128)} %get-tuple-element.29.refs_0_) | copy-start | bytes 3145732

commit v3 on v2

v3 whole, which is shorter than its diff:
```python
import jax
import jax.numpy as jnp
from jax import lax
from jax.experimental import pallas as pl
from jax.experimental.pallas import tpu as pltpu
from jax.sharding import Mesh, PartitionSpec as P

CHIPS = ("y", "x", "z")
ALL = ("y", "x", "z", "c")
LANES = 128
VMEM_LIMIT = 24 * 1024 * 1024
F32, BF16, I32 = jnp.float32, jnp.bfloat16, jnp.int32
NT = (((1,), (1,)), ((), ()))
WHOLE = pl.BlockSpec(memory_space=pltpu.VMEM)
IN_HBM = pl.BlockSpec(memory_space=pltpu.HBM)


def call(kernel, name, out_shape, grid, in_specs, out_specs, scratch, flops, moved, scalars, *arrays):
    return pl.pallas_call(
        kernel,
        name=name,
        out_shape=out_shape,
        grid_spec=pltpu.PrefetchScalarGridSpec(
            num_scalar_prefetch=len(scalars),
            grid=grid,
            in_specs=in_specs,
            out_specs=out_specs,
            scratch_shapes=scratch,
        ),
        compiler_params=pltpu.CompilerParams(vmem_limit_bytes=VMEM_LIMIT),
        cost_estimate=pl.CostEstimate(flops=flops, bytes_accessed=moved, transcendentals=0),
    )(*scalars, *arrays)


def in_hbm(value):
    return pltpu.with_memory_space_constraint(value, pltpu.HBM)


def swap_cores(value):
    return lax.ppermute(value, "c", [(0, 1), (1, 0)])


def quarters_around(value):
    count = lax.axis_size("x") * lax.axis_size("z")
    bits = [0, 1, lax.axis_size("z"), lax.axis_size("z") + 1]
    return [value] + [
        lax.ppermute(value, ("x", "z"), [(i, i ^ bit) for i in range(count)]) for bit in bits[1:]]


def device_blocks(targets, weights, ids, hidden, cotangent, sizes):
    held, width = hidden.shape
    half, quarter = width // 2, width // 8
    kept = half + LANES
    devices = 2 * sizes[0] * sizes[1] * sizes[2]

    def kernel(targets_hbm, weights_hbm, ids_hbm, hidden_hbm, cotangent_hbm, out_ref,
               targets_ref, weights_ref, ids_ref, hidden_ref, cotangent_ref, sems):
        pairs = [(targets_hbm, targets_ref), (ids_hbm, ids_ref), (weights_hbm, weights_ref),
                 (hidden_hbm, hidden_ref), (cotangent_hbm, cotangent_ref)]
        copies = [pltpu.make_async_copy(source, target, sems.at[place])
                  for place, (source, target) in enumerate(pairs)]
        for copy in copies:
            copy.start()
        for copy in copies:
            copy.wait()
        row = lax.broadcasted_iota(I32, (held, LANES), 0)
        lane = lax.broadcasted_iota(I32, (held, LANES), 1)
        meta = jnp.zeros((held, LANES), F32)
        for token in range(held):
            target, name = targets_ref[token], ids_ref[token]
            values = [(target >> 12) & 63, (target >> 6) & 63, target & 63,
                      (name >> 12) & 63, (name >> 6) & 63, name & 63]
            values = [value.astype(F32) for value in values]
            for place, value in enumerate(values):
                meta = jnp.where((row == token) & (lane == place), value, meta)
        weights = weights_ref[...].astype(F32).reshape(held, 1)
        meta = jnp.where(lane == 6, weights, meta).astype(BF16)
        kinds = [
            jnp.concatenate([
                hidden_ref[:, core * half:(core + 1) * half], meta,
                cotangent_ref[:, core * half + part * quarter:core * half + (part + 1) * quarter]], axis=1)
            for part in range(4) for core in range(2)]
        for device in range(devices):
            core, z, x = device % 2, device // 2 % sizes[2], device // 2 // sizes[2] % sizes[1]
            out_ref[device] = kinds[(x % 2 * 2 + z % 2) * 2 + core]

    return call(
        kernel, "device_blocks", jax.ShapeDtypeStruct((devices, held, kept + quarter), BF16), (),
        [IN_HBM] * 5, WHOLE,
        [
            pltpu.SMEM((held,), I32), pltpu.VMEM((held,), BF16), pltpu.SMEM((held,), I32),
            pltpu.VMEM((held, width), BF16), pltpu.VMEM((held, width), BF16),
            pltpu.SemaphoreType.DMA((5,)),
        ],
        0, 4 * devices * held * half, [], in_hbm(targets), in_hbm(weights), in_hbm(ids), in_hbm(hidden),
        in_hbm(cotangent),
    )


def token_rows(gathered, half):
    chips, held, _ = gathered.shape
    tokens, kept, quarter = chips * held, half + LANES, half // 4

    def kernel(gathered_ref, hidden_ref, quarter_ref, info_ref):
        hidden_ref[...] = gathered_ref[:, :, :half].reshape(tokens, half)
        quarter_ref[...] = gathered_ref[:, :, kept:].reshape(tokens, quarter)
        rows = jnp.transpose(gathered_ref[:, :, half:kept].reshape(tokens, LANES).astype(F32))
        targets = rows[0:1] * 4096.0 + rows[1:2] * 64.0 + rows[2:3]
        ids = rows[3:4] * 4096.0 + rows[4:5] * 64.0 + rows[5:6]
        info_ref[...] = jnp.concatenate([targets, ids, rows[6:7], jnp.zeros((5, tokens), F32)], axis=0)

    return call(
        kernel, "token_rows",
        [jax.ShapeDtypeStruct((tokens, half), BF16), jax.ShapeDtypeStruct((tokens, quarter), BF16),
         jax.ShapeDtypeStruct((8, tokens), F32)],
        (), [WHOLE], [WHOLE] * 3, [], 0, 4 * tokens * half, [], gathered,
    )


def joined_quarters(own, quarters, after):
    tokens, quarter = quarters[0].shape

    def kernel(own_ref, *refs):
        for place, ref in enumerate(refs[:4]):
            first = pl.multiple_of((own_ref[0] ^ place) * quarter, quarter)
            refs[-1][:, pl.ds(first, quarter)] = ref[...]

    return call(
        kernel, "joined_quarters", jax.ShapeDtypeStruct((tokens, 4 * quarter), BF16),
        (), [WHOLE] * 4 + [IN_HBM], WHOLE, [], 0, 16 * tokens * quarter, [own], *quarters, after,
    )


def feature_products(side, left_ref, head_ref, first, blocks):
    count = left_ref.shape[0]
    for block in range(first, first + blocks, 2):
        columns = jnp.concatenate([
            head_ref[:, pl.ds(pl.multiple_of((2 * place + side) * LANES, LANES), LANES)]
            for place in (block, block + 1)], axis=1)
        for line in range(0, count, count // 2):
            lines = slice(line, line + count // 2)
            total = jnp.dot(left_ref[lines, :], columns, preferred_element_type=F32).astype(BF16)
            yield block, lines, total[:, :LANES], total[:, LANES:]


def local_logits(core, start, devices, info, near, far, head_weight):
    tokens = near.shape[0]
    rows, width = head_weight.shape
    half, step = width // 2, 256
    blocks = half // LANES

    def kernel(core_ref, start_ref, info_ref, near_ref, far_ref, head_hbm,
               logits_hbm, stats_hbm, left_hbm, away_hbm, last_ref,
               logits_ref, stats_ref, left_ref, away_ref, head_ref, sems, away_sems, head_sems):
        loads = [
            pltpu.make_async_copy(
                head_hbm.at[pl.ds(place, step)], head_ref.at[pl.ds(place, step)], head_sems.at[place // step])
            for place in range(0, rows, step)]
        for load in loads:
            load.start()
        other = 1 - core_ref[0]
        near_columns = pl.ds(pl.multiple_of(core_ref[0] * half, half), half)
        far_columns = pl.ds(pl.multiple_of(other * half, half), half)
        left_ref[tokens:, :] = (
            lax.broadcasted_iota(I32, (tokens, rows), 1) + start_ref[0]
            == jnp.transpose(info_ref[...])[:, 0:1].astype(I32)).astype(F32).astype(BF16)
        for load, place in zip(loads, range(0, rows, step)):
            load.wait()
            logits_ref[place:place + step, :] = lax.dot_general(
                head_ref[place:place + step, near_columns], near_ref[...], NT, preferred_element_type=F32)
        for place in range(0, rows, step):
            logits_ref[place:place + step, :] += lax.dot_general(
                head_ref[place:place + step, far_columns], far_ref[...], NT, preferred_element_type=F32)
        copies = [pltpu.make_async_copy(logits_ref, logits_hbm, sems.at[0])]
        copies[-1].start()
        logits = logits_ref[...]
        peak = jnp.max(logits, axis=0, keepdims=True)
        powers = jnp.exp(logits - peak)
        total = jnp.sum(powers, axis=0, keepdims=True)
        row = lax.broadcasted_iota(I32, (rows, tokens), 0) + start_ref[0]
        hits = row == info_ref[0:1, :].astype(I32)
        picked = jnp.sum(jnp.where(hits, logits, 0.0), axis=0, keepdims=True)
        last_ref[...] = jnp.concatenate([peak, picked, jnp.zeros((6, tokens), F32)], axis=0)
        local_norm = peak + jnp.log(total)
        loss = jnp.sum(info_ref[2:3, :] * picked, axis=1, keepdims=True)
        block = jnp.concatenate(
            [local_norm[:, place:place + LANES] for place in range(0, tokens, LANES)]
            + [jnp.broadcast_to(loss, (4 - tokens // LANES, LANES))], axis=0)
        stats_ref[...] = jnp.broadcast_to(block[None], stats_ref.shape)
        copies.append(pltpu.make_async_copy(stats_ref, stats_hbm, sems.at[1]))
        copies[-1].start()
        left_ref[:tokens, :] = jnp.transpose(jnp.where(hits, 0.0, powers)).astype(BF16)
        copies.append(pltpu.make_async_copy(left_ref, left_hbm, sems.at[2]))
        copies[-1].start()
        for first in range(0, blocks, 4):
            for block, lines, even, odd in feature_products(other, left_ref, head_ref, first, 4):
                away_ref[block, lines, :] = even
                away_ref[block + 1, lines, :] = odd
            part = pl.ds(first, 4)
            copies.append(pltpu.make_async_copy(away_ref.at[part], away_hbm.at[part], away_sems.at[first // 4]))
            copies[-1].start()
        for copy in copies:
            copy.wait()

    shapes = [
        ((rows, tokens), F32), ((devices, 4, LANES), F32),
        ((2 * tokens, rows), BF16), ((blocks, 2 * tokens, LANES), BF16),
    ]
    return call(
        kernel, "local_logits",
        [pltpu.HBM(*shape) for shape in shapes] + [jax.ShapeDtypeStruct((8, tokens), F32)],
        (), [WHOLE] * 3 + [IN_HBM], [IN_HBM] * 4 + [WHOLE],
        [pltpu.VMEM(*shape) for shape in shapes]
        + [pltpu.VMEM((rows, width), BF16), pltpu.SemaphoreType.DMA((3,)),
           pltpu.SemaphoreType.DMA((blocks // 4,)), pltpu.SemaphoreType.DMA((rows // step,))],
        8 * tokens * rows * half, 4 * rows * half, [core, start], info, near, far, in_hbm(head_weight),
    )


def feature_partials(core, left, head_weight):
    count, rows = left.shape
    width = head_weight.shape[1]
    blocks = width // (2 * LANES)
    step = 1024
    held = step // (2 * LANES)

    def kernel(core_ref, left_ref, head_hbm, out_hbm, head_ref, out_ref, head_sems, out_sems):
        loads = [
            pltpu.make_async_copy(head_hbm.at[:, pl.ds(place * step, step)], head_ref.at[place], head_sems.at[place])
            for place in range(width // step)]
        for load in loads:
            load.start()
        stores = []
        for place, load in enumerate(loads):
            load.wait()
            for block, lines, even, odd in feature_products(core_ref[0], left_ref, head_ref.at[place], 0, held):
                out_ref[place * held + block, lines, :] = even
                out_ref[place * held + block + 1, lines, :] = odd
            part = pl.ds(place * held, held)
            stores.append(pltpu.make_async_copy(out_ref.at[part], out_hbm.at[part], out_sems.at[place]))
            stores[-1].start()
        for store in stores:
            store.wait()

    shape = ((blocks, count, LANES), BF16)
    return call(
        kernel, "feature_partials", pltpu.HBM(*shape), (), [WHOLE, IN_HBM], IN_HBM,
        [
            pltpu.VMEM((width // step, rows, step), BF16), pltpu.VMEM(*shape),
            pltpu.SemaphoreType.DMA((width // step,)), pltpu.SemaphoreType.DMA((width // step,)),
        ],
        1 << 35, 2 * rows * width, [core], left, in_hbm(head_weight),
    )


def scaled_pair(stats, info, last, other_last, home, away):
    tokens = info.shape[1]
    blocks = home.shape[0]
    sections = lax.axis_size("y")
    owned = tokens // sections
    lines = tokens // LANES

    def kernel(stats_ref, info_ref, last_ref, other_last_ref, home_hbm, away_hbm, out_hbm, norm_ref, loss_ref,
               home_ref, away_ref, out_ref, in_sems, out_sems):
        loads = []
        for section in range(sections):
            power = pl.ds(section * owned, owned)
            hit = pl.ds(tokens + section * owned, owned)
            loads.append([
                pltpu.make_async_copy(source.at[:, part, :], target.at[:, part, :], in_sems.at[section, place])
                for place, (source, target, part) in enumerate([
                    (home_hbm, home_ref, power), (away_hbm, away_ref, power),
                    (home_hbm, home_ref, hit), (away_hbm, away_ref, hit)])])
            for load in loads[-1]:
                load.start()

        def flat(block, first):
            return jnp.concatenate([block[first + line:first + line + 1] for line in range(lines)], axis=1)

        everyone = stats_ref[...]
        peaks = jnp.max(everyone, axis=0)
        totals = jnp.sum(jnp.exp(everyone - peaks[None]), axis=0)
        norm = flat(peaks, 0) + jnp.log(flat(totals, 0))
        weights = info_ref[2:3, :]
        norm_ref[...] = norm
        picked = jnp.sum(everyone, axis=0)[lines:lines + 1, 0:1]
        loss_ref[...] = ((jnp.sum(weights * norm, axis=1, keepdims=True) - picked)
                         / jnp.sum(weights, axis=1, keepdims=True))
        target = jnp.minimum(last_ref[1:2, :] + other_last_ref[1:2, :], norm)
        scale = jnp.transpose(jnp.concatenate([
            weights * jnp.exp(last_ref[0:1, :] - norm),
            weights * jnp.exp(other_last_ref[0:1, :] - norm),
            weights * (jnp.exp(target - norm) - 1.0),
            jnp.zeros((5, tokens), F32),
        ], axis=0))
        stores = []
        for section in range(sections):
            for load in loads[section]:
                load.wait()
            power = slice(section * owned, (section + 1) * owned)
            hit = slice(tokens + section * owned, tokens + (section + 1) * owned)
            one, two, three = (
                jnp.broadcast_to(scale[power, place:place + 1], (owned, LANES)) for place in range(3))
            for block in range(blocks):
                value = home_ref[block, power, :].astype(F32) * one + away_ref[block, power, :].astype(F32) * two
                hits = (home_ref[block, hit, :] + away_ref[block, hit, :]).astype(F32)
                out_ref[section * blocks + block] = (value + hits * three).astype(BF16)
            part = pl.ds(section * blocks, blocks)
            stores.append(pltpu.make_async_copy(out_ref.at[part], out_hbm.at[part], out_sems.at[section]))
            stores[-1].start()
        for store in stores:
            store.wait()

    return call(
        kernel, "scaled_pair",
        [
            pltpu.HBM((sections * blocks, owned, LANES), BF16),
            jax.ShapeDtypeStruct((1, tokens), F32),
            jax.ShapeDtypeStruct((1, 1), F32),
        ],
        (), [WHOLE] * 4 + [IN_HBM] * 2, [IN_HBM, WHOLE, WHOLE],
        [
            pltpu.VMEM(home.shape, BF16), pltpu.VMEM(away.shape, BF16),
            pltpu.VMEM((sections * blocks, owned, LANES), BF16),
            pltpu.SemaphoreType.DMA((sections, 4)), pltpu.SemaphoreType.DMA((sections,)),
        ],
        10 * tokens * blocks * LANES, 10 * tokens * blocks * LANES, [],
        stats, info, last, other_last, in_hbm(home), in_hbm(away),
    )


def summed_parts(parts):
    count, rows, width = parts.shape

    def kernel(parts_ref, out_ref):
        out_ref[...] = jnp.sum(parts_ref[...].astype(F32), axis=0).astype(BF16)

    return call(
        kernel, "summed_parts", jax.ShapeDtypeStruct((rows, width), BF16), (), [WHOLE], WHOLE,
        [], count * rows * width, 2 * count * rows * width, [], parts,
    )


def row_gradient(name, make_left, core, start, new_rows, rows, small, near, far, step=1024):
    tokens = near.shape[0]
    half = near.shape[1]
    steps = half // step

    def kernel(core_ref, start_ref, ranges_ref, *refs):
        small_refs, (near_ref, far_ref, out_ref, left_ref) = refs[:len(small)], refs[len(small):]
        index = pl.program_id(0)

        @pl.when(index == 0)
        def _():
            lane_row = lax.broadcasted_iota(I32, (8, rows), 1) + start_ref[0]
            inside = jnp.zeros((8, rows), F32)
            for place in range(new_rows.shape[0]):
                within = (lane_row >= ranges_ref[place, 0]) & (lane_row < ranges_ref[place, 1])
                inside = jnp.where(within, 1.0, inside)
            gate = jnp.transpose(inside)[:, 0:1]
            row = lax.broadcasted_iota(I32, (rows, tokens), 0) + start_ref[0]
            left_ref[...] = jnp.where(gate > 0.0, make_left(row, *small_refs), 0.0).astype(BF16)

        @pl.when(index < steps)
        def _():
            out_ref[...] = jnp.dot(left_ref[...], near_ref[...], preferred_element_type=F32).astype(BF16)

        @pl.when(index >= steps)
        def _():
            out_ref[...] = jnp.dot(left_ref[...], far_ref[...], preferred_element_type=F32).astype(BF16)

    def out_index(i, core, start, ranges):
        is_far = (i >= steps).astype(I32)
        side = core[0] + is_far - 2 * core[0] * is_far
        return (0, side * steps + i - is_far * steps)

    return call(
        kernel, name,
        jax.ShapeDtypeStruct((rows, 2 * half), BF16),
        (2 * steps,),
        [pl.BlockSpec(array.shape, lambda i, core, start, ranges: (0, 0)) for array in small] + [
            pl.BlockSpec((tokens, step), lambda i, core, start, ranges: (0, jnp.minimum(i, steps - 1))),
            pl.BlockSpec((tokens, step), lambda i, core, start, ranges: (0, jnp.maximum(i - steps, 0))),
        ],
        pl.BlockSpec((rows, step), out_index),
        [pltpu.VMEM((rows, tokens), BF16)],
        4 * rows * tokens * half, 4 * rows * half, [core, start, new_rows], *small, near, far,
    )


def slope_left(row, logits_ref, info_ref, norm_ref):
    hits = (row == info_ref[0:1, :].astype(I32)).astype(F32)
    return info_ref[2:3, :] * (jnp.exp(logits_ref[...] - norm_ref[...]) - hits)


def onehot_left(row, info_ref):
    return (row == info_ref[1:2, :].astype(I32)).astype(F32)


def local(hidden, targets, token_weight, head_weight, token_ids, embed_cotangent, new_rows):
    core = lax.axis_index("c")
    chips = lax.axis_size("y") * lax.axis_size("x") * lax.axis_size("z")
    devices = 2 * chips
    voc_rows = head_weight.shape[0]
    device = ((lax.axis_index("y") * lax.axis_size("x") + lax.axis_index("x"))
              * lax.axis_size("z") + lax.axis_index("z")) * 2 + core
    at_core = core[None].astype(I32)
    start = device[None].astype(I32) * voc_rows

    sizes = tuple(lax.axis_size(name) for name in CHIPS)
    blocks = device_blocks(targets, token_weight, token_ids, hidden, embed_cotangent, sizes)
    gathered = lax.all_to_all(blocks, ALL, 0, 0, tiled=True)
    near, quarter, info = token_rows(gathered, hidden.shape[1] // 2)
    far = swap_cores(near)
    logits, stats, left, away, last = local_logits(at_core, start, devices, info, near, far, head_weight)

    stats = lax.all_to_all(stats, ALL, 0, 0, tiled=True)
    away = swap_cores(away)
    home = feature_partials(at_core, left, head_weight)
    own_quarter = (lax.axis_index("x") % 2 * 2 + lax.axis_index("z") % 2)[None].astype(I32)
    near_cotangent = joined_quarters(own_quarter, quarters_around(quarter), last)
    far_cotangent = swap_cores(near_cotangent)

    pair, norm, loss = scaled_pair(stats, info, last, swap_cores(last), home, away)
    grad_hidden = summed_parts(lax.all_to_all(pair, CHIPS, 0, 0, tiled=True))

    grad_head = row_gradient(
        "grad_head", slope_left, at_core, start, new_rows, voc_rows, [logits, info, norm], near, far)
    grad_embed = row_gradient(
        "grad_embed", onehot_left, at_core, start, new_rows, voc_rows, [info], near_cotangent, far_cotangent)
    return (loss[0, 0], grad_hidden, grad_head, grad_embed)


def solution(mesh):
    grid = Mesh(mesh.devices.reshape(4, 4, 4, 2), ALL)
    rows = P(ALL)
    in_specs = (P(ALL, None), rows, rows, P(ALL, None), rows, P(ALL, None), P())
    out_specs = (P(), P("y", ("x", "z", "c")), P(ALL, None), P(ALL, None))
    return jax.shard_map(local, mesh=grid, in_specs=in_specs, out_specs=out_specs, check_vma=False)
```

time: 108 us -> 94.5 us (0.88)
  blocking collectives: 42.6 us -> 33.7 us
  Pallas kernels: 38.7 us -> 34.6 us
  starting transfers between devices: 12.2 us -> 15.1 us
  waiting for transfers between devices: 12 us -> 9.62 us
    all_to_all x1, blocking collectives: 42.6 us -> 33.7 us  [local(): gathered = lax.all_to_all(blocks, ALL, 0, 0, tiled=True)]
    pallas_call x10 -> x9, Pallas kernels: 38.7 us -> 34.6 us  [call(): pl.pallas_call(kernel, name=name, out_shape=out_shape, grid_spec=pltpu.Pr...]
    ppermute x0 -> x3, starting transfers between devices: none -> 3.59 us  [quarters_around(): lax.ppermute(value, ('x', 'z'), [(i, i ^ bit) for i in range(count)])]
    all_to_all x1, waiting for transfers between devices: 6.27 us -> 4.2 us  [local(): stats = lax.all_to_all(stats, ALL, 0, 0, tiled=True)]
    ppermute x4, waiting for transfers between devices: 1.18 us -> 0.01 us  [swap_cores(): return lax.ppermute(value, 'c', [(0, 1), (1, 0)])]
    all_to_all x1, starting transfers between devices: 5.73 us -> 4.61 us  [local(): stats = lax.all_to_all(stats, ALL, 0, 0, tiled=True)]
  transfers between devices with their start and end apart: 6 -> 9, of which waited for: 3 -> 2; matrix products, arithmetic and copies ran while one was open for 0% -> 0% of each run, Pallas kernels for 28% -> 35%
where the time goes in v3:
time: 94.5 us; the launch traced here: 94.1 us
  Pallas kernels  34.6 us (37%)
  blocking collectives  33.7 us (36%)
  starting transfers between devices  15.1 us (16%)
  waiting for transfers between devices  9.62 us (10%)
    pallas_call x9, Pallas kernels, call(): pl.pallas_call(kernel, name=name, out_shape=out_shape, grid_spec=pltpu.Pr...  34.6 us
    all_to_all x1, blocking collectives, local(): gathered = lax.all_to_all(blocks, ALL, 0, 0, tiled=True)  33.7 us
    all_to_all x1, starting transfers between devices, local(): grad_hidden = summed_parts(lax.all_to_all(pair, CHIPS, 0, 0, tiled=True))  5.95 us
    all_to_all x1, waiting for transfers between devices, local(): grad_hidden = summed_parts(lax.all_to_all(pair, CHIPS, 0, 0, tiled=True))  5.4 us
    all_to_all x1, starting transfers between devices, local(): stats = lax.all_to_all(stats, ALL, 0, 0, tiled=True)  4.61 us
    all_to_all x1, waiting for transfers between devices, local(): stats = lax.all_to_all(stats, ALL, 0, 0, tiled=True)  4.2 us
    ppermute x3, starting transfers between devices, quarters_around(): lax.ppermute(value, ('x', 'z'), [(i, i ^ bit) for i in range(count)])  3.59 us
  transfers between devices with their start and end apart: 9, of which 2 were waited for; matrix products, arithmetic and copies ran while one was open for 0% of the time, Pallas kernels for 35%

profile of v3, /device:TPU:0, one launch (start us, length us, event | category | flops | bytes accessed | tf_op | source)
XLA Modules:
  0.0 94.1 jit_solution(4706359972891351841)
XLA Ops:
  0.6 0.9 device_blocks.1
  1.6 33.7 %all_to_all.15.gathered_ref = bf16[128,2,2688]{2,1,0:T(2,128)(2,1)S(1)} all-to-all(bf16[128,2,2688]{2,1,0:T(2,128)(2,1)S(1)} %device_blocks.1), channel_id=1, replica_groups=mesh['y'=4,'x'=4,'z'=4,'c'=2] {'y','x','z','c'}, dimensions={0} | all-to-all | bytes 2752512 | tf_op jit(solution)/shard_map/all_to_all | solution.py:412
  35.3 0.3 token_rows.1
  35.5 0.1 collective-permute-start
  35.6 0.1 collective-permute-start.5
  35.7 1.8 %collective-permute-start.4 = (bf16[256,512]{1,0:T(8,128)(2,1)S(1)}, bf16[256,512]{1,0:T(8,128)(2,1)S(1)}, u32[]{:S(2)}, u32[]{:S(2)}) collective-permute-start(bf16[256,512]{1,0:T(8,128)(2,1)S(1)} %get-tuple-element.25.refs_0_), channel_id=1, source_target_pairs={{0,8},{2,10},{4,12},{6,14},{8,0},{10,2},{12,4},{14,6},{16,24},{18,... | collective-permute-start | bytes 786440 | tf_op jit(solution)/shard_map/ppermute | solution.py:47
  37.5 1.7 %collective-permute-start.3 = (bf16[256,512]{1,0:T(8,128)(2,1)S(1)}, bf16[256,512]{1,0:T(8,128)(2,1)S(1)}, u32[]{:S(2)}, u32[]{:S(2)}) collective-permute-start(bf16[256,512]{1,0:T(8,128)(2,1)S(1)} %get-tuple-element.25.refs_0_), channel_id=1, source_target_pairs={{0,2},{2,0},{4,6},{6,4},{8,10},{10,8},{12,14},{14,12},{16,18},{18,... | collective-permute-start | bytes 786440 | tf_op jit(solution)/shard_map/ppermute | solution.py:47
  39.2 9.5 %local_logits.1 = (f32[1024,256]{1,0:T(8,128)}, f32[128,4,128]{2,1,0:T(4,128)}, bf16[512,1024]{1,0:T(8,128)(2,1)}, bf16[16,512,128]{2,1,0:T(8,128)(2,1)}, f32[8,256]{1,0:T(8,128)S(1)}) custom-call(s32[1]{0:T(128)} %bitcast.core_ref, s32[1]{0:T(128)} %bitcast.1.start_ref, f32[8,256]{1,0:T(8,128)S(1)} %get-tuple-element.15.info_ref.refs_1_.refs_0_, ...), custom_call_target="tpu_custom_call" | custom-call | flops 4294967296 | bytes 8388608 | tf_op jit(solution)/shard_map/local_logits/pallas_call | solution.py:19
  48.8 4.6 %all-to-all-start.1 = ((f32[128,4,128]{2,1,0:T(4,128)}), f32[128,4,128]{2,1,0:T(4,128)S(1)}, u32[]{:S(2)}, u32[]{:S(2)}) async-start(f32[128,4,128]{2,1,0:T(4,128)} %get-tuple-element.17), calls=%async_computation.1 | async-start | bytes 524288 | tf_op jit(solution)/shard_map/all_to_all | solution.py:417
  53.4 0.0 copy-start.3
  53.4 0.1 collective-permute-start.1
  53.5 0.1 joined_quarters.1.refs_1_
  53.6 0.6 collective-permute-start.6
  54.2 0.3 collective-permute-start.2
  54.5 0.2 copy-done.3
  54.6 5.5 %feature_partials.1.home_hbm = bf16[16,512,128]{2,1,0:T(8,128)(2,1)} custom-call(s32[1]{0:T(128)} %bitcast.core_ref, bf16[512,1024]{1,0:T(8,128)(2,1)S(1)} %copy-done.3, bf16[1024,4096]{1,0:T(8,128)(2,1)} %head_hbm.3), custom_call_target="tpu_custom_call" | custom-call | flops 34359738368 | bytes 8388608 | tf_op jit(solution)/shard_map/feature_partials/pallas_call | solution.py:19
  60.1 4.2 %all-to-all-done.1.stats_ref = f32[128,4,128]{2,1,0:T(4,128)S(1)} async-done(((f32[128,4,128]{2,1,0:T(4,128)}), f32[128,4,128]{2,1,0:T(4,128)S(1)}, u32[]{:S(2)}, u32[]{:S(2)}) %all-to-all-start.1) | async-done | bytes 262176 | tf_op jit(solution)/shard_map/all_to_all | solution.py:417
  64.3 4.0 %scaled_pair.1 = (bf16[64,64,128]{2,1,0:T(8,128)(2,1)}, f32[1,256]{1,0:T(1,128)S(1)}, f32[1,1]{1,0:T(1,128)}) custom-call(f32[128,4,128]{2,1,0:T(4,128)S(1)} %all-to-all-done.1.stats_ref, f32[8,256]{1,0:T(8,128)S(1)} %get-tuple-element.15.info_ref.refs_1_.refs_0_, f32[8,256]{1,0:T(8,128)S(1)} %get-tuple-element.18.last_ref.refs_4_, ...), custom_call_target="tpu_custom_call" | custom-call | flops 5242880 | bytes 5242880 | tf_op jit(solution)/shard_map/scaled_pair/pallas_call | solution.py:19
  68.4 5.9 %all-to-all-start.2 = ((bf16[64,64,128]{2,1,0:T(8,128)(2,1)}), bf16[64,64,128]{2,1,0:T(8,128)(2,1)S(1)}, u32[]{:S(2)}, u32[]{:S(2)}) async-start(bf16[64,64,128]{2,1,0:T(8,128)(2,1)} %get-tuple-element.22), calls=%async_computation.2 | async-start | bytes 2097152 | tf_op jit(solution)/shard_map/all_to_all | solution.py:425
  74.3 0.1 copy.11.ranges_ref
  74.4 7.3 %grad_embed.1 = bf16[1024,4096]{1,0:T(8,128)(2,1)} custom-call(s32[1]{0:T(128)} %bitcast.core_ref, s32[1]{0:T(128)} %bitcast.1.start_ref, s32[8,2]{1,0:T(8,128)S(1)} %copy.11.ranges_ref, f32[8,256]{1,0:T(8,128)S(1)} %get-tuple-element.15.info_ref.refs_1_.refs_0_, bf16[256,2048]{1,0:T(8,128)(2,1)S(1)} %joined_quarters.1.refs_1_, ...), custom_call_target="tpu_custom_call" | custom-call | flops 2147483648 | bytes 8388608 | tf_op jit(solution)/shard_map/grad_embed/pallas_call | solution.py:19
  81.8 6.2 %grad_head.1 = bf16[1024,4096]{1,0:T(8,128)(2,1)} custom-call(s32[1]{0:T(128)} %bitcast.core_ref, s32[1]{0:T(128)} %bitcast.1.start_ref, s32[8,2]{1,0:T(8,128)S(1)} %copy.11.ranges_ref, f32[1024,256]{1,0:T(8,128)S(1)} %copy-done.2, f32[8,256]{1,0:T(8,128)S(1)} %get-tuple-element.15.info_ref.refs_1_.refs_0_, f32[1,256]{1,0:T(1,128)S(1)} %get-tuple-element.24.refs_2_, ...), custom_call_target="tpu_custom_call" | custom-call | flops 2147483648 | bytes 8388608 | tf_op jit(solution)/shard_map/grad_head/pallas_call | solution.py:19
  87.9 5.4 %all-to-all-done.2.parts_ref = bf16[64,64,128]{2,1,0:T(8,128)(2,1)S(1)} async-done(((bf16[64,64,128]{2,1,0:T(8,128)(2,1)}), bf16[64,64,128]{2,1,0:T(8,128)(2,1)S(1)}, u32[]{:S(2)}, u32[]{:S(2)}) %all-to-all-start.2) | async-done | bytes 1048608 | tf_op jit(solution)/shard_map/all_to_all | solution.py:425
  93.3 0.8 summed_parts.1
  (15 shorter events, 0.0 us)
Async XLA Ops:
  35.5 3.7 %collective-permute-start = (bf16[256,2048]{1,0:T(8,128)(2,1)S(1)}, bf16[256,2048]{1,0:T(8,128)(2,1)S(1)}, u32[]{:S(2)}, u32[]{:S(2)}) collective-permute-start(bf16[256,2048]{1,0:T(8,128)(2,1)S(1)} %get-tuple-element.16.near_ref.refs_3_), channel_id=1, source_target_pairs={{0,1},{1,0},{2,3},{3,2},{4,5},{5,4},{6,7},{7,6},{8,9},{9,8},{10,11... | collective-permute-start | bytes 3145736 | tf_op jit(solution)/shard_map/ppermute | solution.py:40
  35.6 17.9 %collective-permute-start.5 = (bf16[256,512]{1,0:T(8,128)(2,1)S(1)}, bf16[256,512]{1,0:T(8,128)(2,1)S(1)}, u32[]{:S(2)}, u32[]{:S(2)}) collective-permute-start(bf16[256,512]{1,0:T(8,128)(2,1)S(1)} %get-tuple-element.25.refs_0_), channel_id=1, source_target_pairs={{0,10},{2,8},{4,14},{6,12},{8,2},{10,0},{12,6},{14,4},{16,26},{18,... | collective-permute-start | bytes 786440 | tf_op jit(solution)/shard_map/ppermute | solution.py:47
  35.7 17.8 %collective-permute-start.4 = (bf16[256,512]{1,0:T(8,128)(2,1)S(1)}, bf16[256,512]{1,0:T(8,128)(2,1)S(1)}, u32[]{:S(2)}, u32[]{:S(2)}) collective-permute-start(bf16[256,512]{1,0:T(8,128)(2,1)S(1)} %get-tuple-element.25.refs_0_), channel_id=1, source_target_pairs={{0,8},{2,10},{4,12},{6,14},{8,0},{10,2},{12,4},{14,6},{16,24},{18,... | collective-permute-start | bytes 786440 | tf_op jit(solution)/shard_map/ppermute | solution.py:47
  37.5 16.0 %collective-permute-start.3 = (bf16[256,512]{1,0:T(8,128)(2,1)S(1)}, bf16[256,512]{1,0:T(8,128)(2,1)S(1)}, u32[]{:S(2)}, u32[]{:S(2)}) collective-permute-start(bf16[256,512]{1,0:T(8,128)(2,1)S(1)} %get-tuple-element.25.refs_0_), channel_id=1, source_target_pairs={{0,2},{2,0},{4,6},{6,4},{8,10},{10,8},{12,14},{14,12},{16,18},{18,... | collective-permute-start | bytes 786440 | tf_op jit(solution)/shard_map/ppermute | solution.py:47
  39.2 9.6 %copy-start = (bf16[256,2048]{1,0:T(8,128)(2,1)}, bf16[256,2048]{1,0:T(8,128)(2,1)S(1)}, u32[]{:S(2)}) copy-start(bf16[256,2048]{1,0:T(8,128)(2,1)S(1)} %collective-permute-done.far_ref.refs_4_) | copy-start | bytes 3145732
  48.8 15.5 %all-to-all-start.1 = ((f32[128,4,128]{2,1,0:T(4,128)}), f32[128,4,128]{2,1,0:T(4,128)S(1)}, u32[]{:S(2)}, u32[]{:S(2)}) async-start(f32[128,4,128]{2,1,0:T(4,128)} %get-tuple-element.17), calls=%async_computation.1 | async-start | bytes 524288 | tf_op jit(solution)/shard_map/all_to_all | solution.py:417
  53.4 1.2 %copy-start.3 = (bf16[512,1024]{1,0:T(8,128)(2,1)S(1)}, bf16[512,1024]{1,0:T(8,128)(2,1)}, u32[]{:S(2)}) copy-start(bf16[512,1024]{1,0:T(8,128)(2,1)} %get-tuple-element.19.left_ref) | copy-start | bytes 3145732
  53.4 6.7 %collective-permute-start.1 = (f32[8,256]{1,0:T(8,128)S(1)}, f32[8,256]{1,0:T(8,128)S(1)}, u32[]{:S(2)}, u32[]{:S(2)}) collective-permute-start(f32[8,256]{1,0:T(8,128)S(1)} %get-tuple-element.18.last_ref.refs_4_), channel_id=1, source_target_pairs={{0,1},{1,0},{2,3},{3,2},{4,5},{5,4},{6,7},{7,6},{8,9},{9,8},{10,11... | collective-permute-start | bytes 24584 | tf_op jit(solution)/shard_map/ppermute | solution.py:40
  53.6 20.8 %collective-permute-start.6 = (bf16[256,2048]{1,0:T(8,128)(2,1)S(1)}, bf16[256,2048]{1,0:T(8,128)(2,1)}, u32[]{:S(2)}, u32[]{:S(2)}) collective-permute-start(bf16[256,2048]{1,0:T(8,128)(2,1)S(1)} %joined_quarters.1.refs_1_), channel_id=1, source_target_pairs={{0,1},{1,0},{2,3},{3,2},{4,5},{5,4},{6,7},{7,6},{8,9},{9,8},{10,11... | collective-permute-start | bytes 3145736 | tf_op jit(solution)/shard_map/ppermute | solution.py:40
  54.2 10.2 %collective-permute-start.2 = (bf16[16,512,128]{2,1,0:T(8,128)(2,1)}, bf16[16,512,128]{2,1,0:T(8,128)(2,1)}, u32[]{:S(2)}, u32[]{:S(2)}) collective-permute-start(bf16[16,512,128]{2,1,0:T(8,128)(2,1)} %get-tuple-element.20), channel_id=1, source_target_pairs={{0,1},{1,0},{2,3},{3,2},{4,5},{5,4},{6,7},{7,6},{8,9},{9,8},{10,11... | collective-permute-start | bytes 6291464 | tf_op jit(solution)/shard_map/ppermute | solution.py:40
  68.3 6.0 %copy-start.4 = (s32[8,2]{0,1:T(2,128)S(1)}, s32[8,2]{0,1:T(2,128)}, u32[]{:S(2)}) copy-start(s32[8,2]{0,1:T(2,128)} %param.13) | copy-start | bytes 196
  68.4 25.0 %all-to-all-start.2 = ((bf16[64,64,128]{2,1,0:T(8,128)(2,1)}), bf16[64,64,128]{2,1,0:T(8,128)(2,1)S(1)}, u32[]{:S(2)}, u32[]{:S(2)}) async-start(bf16[64,64,128]{2,1,0:T(8,128)(2,1)} %get-tuple-element.22), calls=%async_computation.2 | async-start | bytes 2097152 | tf_op jit(solution)/shard_map/all_to_all | solution.py:425
  74.4 7.4 %copy-start.1 = (bf16[256,2048]{1,0:T(8,128)(2,1)S(1)}, bf16[256,2048]{1,0:T(8,128)(2,1)}, u32[]{:S(2)}) copy-start(bf16[256,2048]{1,0:T(8,128)(2,1)} %copy-done) | copy-start | bytes 3145732
  74.4 7.4 %copy-start.2 = (f32[1024,256]{1,0:T(8,128)S(1)}, f32[1024,256]{1,0:T(8,128)}, u32[]{:S(2)}) copy-start(f32[1024,256]{1,0:T(8,128)} %get-tuple-element.23.refs_0_) | copy-start | bytes 3145732

commit v4 on v3

--- a/solution.py
+++ b/solution.py
@@ -47,13 +47,13 @@
         lax.ppermute(value, ("x", "z"), [(i, i ^ bit) for i in range(count)]) for bit in bits[1:]]
 
 
-def device_blocks(targets, weights, ids, hidden, cotangent, sizes):
+def device_blocks(places, targets, weights, ids, hidden, cotangent, sizes):
     held, width = hidden.shape
     half, quarter = width // 2, width // 8
     kept = half + LANES
     devices = 2 * sizes[0] * sizes[1] * sizes[2]
 
-    def kernel(targets_hbm, weights_hbm, ids_hbm, hidden_hbm, cotangent_hbm, out_ref,
+    def kernel(core_ref, start_ref, quarter_ref, targets_hbm, weights_hbm, ids_hbm, hidden_hbm, cotangent_hbm, out_ref,
                targets_ref, weights_ref, ids_ref, hidden_ref, cotangent_ref, sems):
         pairs = [(targets_hbm, targets_ref), (ids_hbm, ids_ref), (weights_hbm, weights_ref),
                  (hidden_hbm, hidden_ref), (cotangent_hbm, cotangent_ref)]
@@ -92,7 +92,7 @@
             pltpu.VMEM((held, width), BF16), pltpu.VMEM((held, width), BF16),
             pltpu.SemaphoreType.DMA((5,)),
         ],
-        0, 4 * devices * held * half, [], in_hbm(targets), in_hbm(weights), in_hbm(ids), in_hbm(hidden),
+        0, 4 * devices * held * half, places, in_hbm(targets), in_hbm(weights), in_hbm(ids), in_hbm(hidden),
         in_hbm(cotangent),
     )
 
@@ -113,7 +113,7 @@
         kernel, "token_rows",
         [jax.ShapeDtypeStruct((tokens, half), BF16), jax.ShapeDtypeStruct((tokens, quarter), BF16),
          jax.ShapeDtypeStruct((8, tokens), F32)],
-        (), [WHOLE], [WHOLE] * 3, [], 0, 4 * tokens * half, [], gathered,
+        (), [WHOLE], [WHOLE] * 3, [], 1 << 33, 4 * tokens * half, [], gathered,
     )
 
 
@@ -149,23 +149,16 @@
     half, step = width // 2, 256
     blocks = half // LANES
 
-    def kernel(core_ref, start_ref, info_ref, near_ref, far_ref, head_hbm,
+    def kernel(core_ref, start_ref, info_ref, near_ref, far_ref, head_ref,
                logits_hbm, stats_hbm, left_hbm, away_hbm, last_ref,
-               logits_ref, stats_ref, left_ref, away_ref, head_ref, sems, away_sems, head_sems):
-        loads = [
-            pltpu.make_async_copy(
-                head_hbm.at[pl.ds(place, step)], head_ref.at[pl.ds(place, step)], head_sems.at[place // step])
-            for place in range(0, rows, step)]
-        for load in loads:
-            load.start()
+               logits_ref, stats_ref, left_ref, away_ref, sems, away_sems):
         other = 1 - core_ref[0]
         near_columns = pl.ds(pl.multiple_of(core_ref[0] * half, half), half)
         far_columns = pl.ds(pl.multiple_of(other * half, half), half)
         left_ref[tokens:, :] = (
             lax.broadcasted_iota(I32, (tokens, rows), 1) + start_ref[0]
             == jnp.transpose(info_ref[...])[:, 0:1].astype(I32)).astype(F32).astype(BF16)
-        for load, place in zip(loads, range(0, rows, step)):
-            load.wait()
+        for place in range(0, rows, step):
             logits_ref[place:place + step, :] = lax.dot_general(
                 head_ref[place:place + step, near_columns], near_ref[...], NT, preferred_element_type=F32)
         for place in range(0, rows, step):
@@ -209,11 +202,10 @@
     return call(
         kernel, "local_logits",
         [pltpu.HBM(*shape) for shape in shapes] + [jax.ShapeDtypeStruct((8, tokens), F32)],
-        (), [WHOLE] * 3 + [IN_HBM], [IN_HBM] * 4 + [WHOLE],
+        (), [WHOLE] * 4, [IN_HBM] * 4 + [WHOLE],
         [pltpu.VMEM(*shape) for shape in shapes]
-        + [pltpu.VMEM((rows, width), BF16), pltpu.SemaphoreType.DMA((3,)),
-           pltpu.SemaphoreType.DMA((blocks // 4,)), pltpu.SemaphoreType.DMA((rows // step,))],
-        8 * tokens * rows * half, 4 * rows * half, [core, start], info, near, far, in_hbm(head_weight),
+        + [pltpu.SemaphoreType.DMA((3,)), pltpu.SemaphoreType.DMA((blocks // 4,))],
+        8 * tokens * rows * half, 4 * rows * half, [core, start], info, near, far, head_weight,
     )
 
 
@@ -406,9 +398,10 @@
               * lax.axis_size("z") + lax.axis_index("z")) * 2 + core
     at_core = core[None].astype(I32)
     start = device[None].astype(I32) * voc_rows
+    own_quarter = (lax.axis_index("x") % 2 * 2 + lax.axis_index("z") % 2)[None].astype(I32)
 
     sizes = tuple(lax.axis_size(name) for name in CHIPS)
-    blocks = device_blocks(targets, token_weight, token_ids, hidden, embed_cotangent, sizes)
+    blocks = device_blocks([at_core, start, own_quarter], targets, token_weight, token_ids, hidden, embed_cotangent, sizes)
     gathered = lax.all_to_all(blocks, ALL, 0, 0, tiled=True)
     near, quarter, info = token_rows(gathered, hidden.shape[1] // 2)
     far = swap_cores(near)
@@ -417,7 +410,6 @@
     stats = lax.all_to_all(stats, ALL, 0, 0, tiled=True)
     away = swap_cores(away)
     home = feature_partials(at_core, left, head_weight)
-    own_quarter = (lax.axis_index("x") % 2 * 2 + lax.axis_index("z") % 2)[None].astype(I32)
     near_cotangent = joined_quarters(own_quarter, quarters_around(quarter), last)
     far_cotangent = swap_cores(near_cotangent)
 

time: 94.5 us -> 91 us (0.963)
  Pallas kernels: 34.6 us -> 31.1 us
    pallas_call x9, Pallas kernels: 34.6 us -> 31.1 us  [call(): pl.pallas_call(kernel, name=name, out_shape=out_shape, grid_spec=pltpu.Pr...]
  transfers between devices with their start and end apart: 9 -> 9, of which waited for: 2 -> 3; matrix products, arithmetic and copies ran while one was open for 0% -> 0% of each run, Pallas kernels for 35% -> 32%
where the time goes in v4:
time: 91 us; the launch traced here: 90.7 us
  blocking collectives  33.7 us (37%)
  Pallas kernels  31.1 us (34%)
  starting transfers between devices  14.9 us (16%)
  waiting for transfers between devices  10 us (11%)
    all_to_all x1, blocking collectives, local(): gathered = lax.all_to_all(blocks, ALL, 0, 0, tiled=True)  33.7 us
    pallas_call x9, Pallas kernels, call(): pl.pallas_call(kernel, name=name, out_shape=out_shape, grid_spec=pltpu.Pr...  31.1 us
    all_to_all x1, starting transfers between devices, local(): grad_hidden = summed_parts(lax.all_to_all(pair, CHIPS, 0, 0, tiled=True))  5.95 us
    all_to_all x1, waiting for transfers between devices, local(): grad_hidden = summed_parts(lax.all_to_all(pair, CHIPS, 0, 0, tiled=True))  5.4 us
    all_to_all x1, starting transfers between devices, local(): stats = lax.all_to_all(stats, ALL, 0, 0, tiled=True)  4.63 us
    all_to_all x1, waiting for transfers between devices, local(): stats = lax.all_to_all(stats, ALL, 0, 0, tiled=True)  3.81 us
    ppermute x3, starting transfers between devices, quarters_around(): lax.ppermute(value, ('x', 'z'), [(i, i ^ bit) for i in range(count)])  3.56 us
  transfers between devices with their start and end apart: 9, of which 3 were waited for; matrix products, arithmetic and copies ran while one was open for 0% of the time, Pallas kernels for 32%

profile of v4, /device:TPU:0, one launch (start us, length us, event | category | flops | bytes accessed | tf_op | source)
XLA Modules:
  0.0 90.7 jit_solution(12468383622935576591)
XLA Ops:
  0.7 0.9 %device_blocks.1 = bf16[128,2,2688]{2,1,0:T(2,128)(2,1)S(1)} custom-call(s32[1]{0:T(128)} %bitcast.core_ref, s32[1]{0:T(128)} %bitcast.1.start_ref, s32[1]{0:T(128)} %bitcast.2.quarter_ref.own_ref, s32[2]{0:T(128)} %targets_hbm.1, bf16[2]{0:T(256)(128)(2,1)} %weights_hbm.1, s32[2]{0:T(128)} %ids_hbm.1, bf16[2,4096]{1,0:T(2,128)(2,1)} %hidden_hbm.1, ...), custom_call_target="tpu_custom_call" | custom-call | bytes 2097152 | tf_op jit(solution)/shard_map/device_blocks/pallas_call | solution.py:19
  1.6 0.0 slice-start
  1.6 33.7 %all_to_all.15.gathered_ref = bf16[128,2,2688]{2,1,0:T(2,128)(2,1)S(1)} all-to-all(bf16[128,2,2688]{2,1,0:T(2,128)(2,1)S(1)} %device_blocks.1), channel_id=1, replica_groups=mesh['y'=4,'x'=4,'z'=4,'c'=2] {'y','x','z','c'}, dimensions={0} | all-to-all | bytes 2752512 | tf_op jit(solution)/shard_map/all_to_all | solution.py:405
  35.3 0.3 token_rows.1
  35.6 0.1 collective-permute-start
  35.6 0.1 collective-permute-start.5
  35.7 1.7 %collective-permute-start.4 = (bf16[256,512]{1,0:T(8,128)(2,1)S(1)}, bf16[256,512]{1,0:T(8,128)(2,1)S(1)}, u32[]{:S(2)}, u32[]{:S(2)}) collective-permute-start(bf16[256,512]{1,0:T(8,128)(2,1)S(1)} %get-tuple-element.25.refs_0_), channel_id=1, source_target_pairs={{0,8},{2,10},{4,12},{6,14},{8,0},{10,2},{12,4},{14,6},{16,24},{18,... | collective-permute-start | bytes 786440 | tf_op jit(solution)/shard_map/ppermute | solution.py:47
  37.5 1.7 %collective-permute-start.3 = (bf16[256,512]{1,0:T(8,128)(2,1)S(1)}, bf16[256,512]{1,0:T(8,128)(2,1)S(1)}, u32[]{:S(2)}, u32[]{:S(2)}) collective-permute-start(bf16[256,512]{1,0:T(8,128)(2,1)S(1)} %get-tuple-element.25.refs_0_), channel_id=1, source_target_pairs={{0,2},{2,0},{4,6},{6,4},{8,10},{10,8},{12,14},{14,12},{16,18},{18,... | collective-permute-start | bytes 786440 | tf_op jit(solution)/shard_map/ppermute | solution.py:47
  39.2 6.0 %local_logits.1 = (f32[1024,256]{1,0:T(8,128)}, f32[128,4,128]{2,1,0:T(4,128)}, bf16[512,1024]{1,0:T(8,128)(2,1)}, bf16[16,512,128]{2,1,0:T(8,128)(2,1)}, f32[8,256]{1,0:T(8,128)S(1)}) custom-call(s32[1]{0:T(128)} %bitcast.core_ref, s32[1]{0:T(128)} %bitcast.1.start_ref, f32[8,256]{1,0:T(8,128)S(1)} %get-tuple-element.15.info_ref.refs_1_.refs_0_, ...), custom_call_target="tpu_custom_call" | custom-call | flops 4294967296 | bytes 8388608 | tf_op jit(solution)/shard_map/local_logits/pallas_call | solution.py:19
  45.3 4.6 %all-to-all-start.1 = ((f32[128,4,128]{2,1,0:T(4,128)}), f32[128,4,128]{2,1,0:T(4,128)S(1)}, u32[]{:S(2)}, u32[]{:S(2)}) async-start(f32[128,4,128]{2,1,0:T(4,128)} %get-tuple-element.17), calls=%async_computation.1 | async-start | bytes 524288 | tf_op jit(solution)/shard_map/all_to_all | solution.py:410
  49.9 0.1 collective-permute-start.1
  50.1 0.8 collective-permute-done.3.refs_1_
  50.9 0.1 joined_quarters.1.refs_1_
  50.9 0.1 collective-permute-start.6
  51.0 0.5 collective-permute-start.2
  51.5 5.5 %feature_partials.1.home_hbm = bf16[16,512,128]{2,1,0:T(8,128)(2,1)} custom-call(s32[1]{0:T(128)} %bitcast.core_ref, bf16[512,1024]{1,0:T(8,128)(2,1)S(1)} %copy-done.3, bf16[1024,4096]{1,0:T(8,128)(2,1)} %head_hbm.1), custom_call_target="tpu_custom_call" | custom-call | flops 34359738368 | bytes 8388608 | tf_op jit(solution)/shard_map/feature_partials/pallas_call | solution.py:19
  57.0 3.8 %all-to-all-done.1.stats_ref = f32[128,4,128]{2,1,0:T(4,128)S(1)} async-done(((f32[128,4,128]{2,1,0:T(4,128)}), f32[128,4,128]{2,1,0:T(4,128)S(1)}, u32[]{:S(2)}, u32[]{:S(2)}) %all-to-all-start.1) | async-done | bytes 262176 | tf_op jit(solution)/shard_map/all_to_all | solution.py:410
  60.9 4.0 %scaled_pair.1 = (bf16[64,64,128]{2,1,0:T(8,128)(2,1)}, f32[1,256]{1,0:T(1,128)S(1)}, f32[1,1]{1,0:T(1,128)}) custom-call(f32[128,4,128]{2,1,0:T(4,128)S(1)} %all-to-all-done.1.stats_ref, f32[8,256]{1,0:T(8,128)S(1)} %get-tuple-element.15.info_ref.refs_1_.refs_0_, f32[8,256]{1,0:T(8,128)S(1)} %get-tuple-element.18.last_ref.refs_4_, ...), custom_call_target="tpu_custom_call" | custom-call | flops 5242880 | bytes 5242880 | tf_op jit(solution)/shard_map/scaled_pair/pallas_call | solution.py:19
  64.9 6.0 %all-to-all-start.2 = ((bf16[64,64,128]{2,1,0:T(8,128)(2,1)}), bf16[64,64,128]{2,1,0:T(8,128)(2,1)S(1)}, u32[]{:S(2)}, u32[]{:S(2)}) async-start(bf16[64,64,128]{2,1,0:T(8,128)(2,1)} %get-tuple-element.22), calls=%async_computation.2 | async-start | bytes 2097152 | tf_op jit(solution)/shard_map/all_to_all | solution.py:417
  70.9 0.1 copy.11.ranges_ref
  71.0 7.3 %grad_embed.1 = bf16[1024,4096]{1,0:T(8,128)(2,1)} custom-call(s32[1]{0:T(128)} %bitcast.core_ref, s32[1]{0:T(128)} %bitcast.1.start_ref, s32[8,2]{1,0:T(8,128)S(1)} %copy.11.ranges_ref, f32[8,256]{1,0:T(8,128)S(1)} %get-tuple-element.15.info_ref.refs_1_.refs_0_, bf16[256,2048]{1,0:T(8,128)(2,1)S(1)} %joined_quarters.1.refs_1_, ...), custom_call_target="tpu_custom_call" | custom-call | flops 2147483648 | bytes 8388608 | tf_op jit(solution)/shard_map/grad_embed/pallas_call | solution.py:19
  78.3 6.2 %grad_head.1 = bf16[1024,4096]{1,0:T(8,128)(2,1)} custom-call(s32[1]{0:T(128)} %bitcast.core_ref, s32[1]{0:T(128)} %bitcast.1.start_ref, s32[8,2]{1,0:T(8,128)S(1)} %copy.11.ranges_ref, f32[1024,256]{1,0:T(8,128)S(1)} %copy-done.2, f32[8,256]{1,0:T(8,128)S(1)} %get-tuple-element.15.info_ref.refs_1_.refs_0_, f32[1,256]{1,0:T(1,128)S(1)} %get-tuple-element.24.refs_2_, ...), custom_call_target="tpu_custom_call" | custom-call | flops 2147483648 | bytes 8388608 | tf_op jit(solution)/shard_map/grad_head/pallas_call | solution.py:19
  84.5 5.4 %all-to-all-done.2.parts_ref = bf16[64,64,128]{2,1,0:T(8,128)(2,1)S(1)} async-done(((bf16[64,64,128]{2,1,0:T(8,128)(2,1)}), bf16[64,64,128]{2,1,0:T(8,128)(2,1)S(1)}, u32[]{:S(2)}, u32[]{:S(2)}) %all-to-all-start.2) | async-done | bytes 1048608 | tf_op jit(solution)/shard_map/all_to_all | solution.py:417
  89.9 0.8 summed_parts.1
  (20 shorter events, 0.0 us)
Async XLA Ops:
  1.6 37.6 %slice-start = ((s8[8388608]{0:T(1024)(128)(4,1)}), s8[4194304]{0:T(1024)(128)(4,1)S(1)}, s32[]{:S(2)}) async-start(s8[8388608]{0:T(1024)(128)(4,1)} %bitcast.4), calls=%async_computation.3 | async-start | bytes 8388608
  35.3 3.9 %slice-start.1 = ((s8[8388608]{0:T(1024)(128)(4,1)}), s8[4194304]{0:T(1024)(128)(4,1)S(1)}, s32[]{:S(2)}) async-start(s8[8388608]{0:T(1024)(128)(4,1)} %bitcast.4), calls=%async_computation.4 | async-start | bytes 8388608
  35.6 3.6 %collective-permute-start = (bf16[256,2048]{1,0:T(8,128)(2,1)S(1)}, bf16[256,2048]{1,0:T(8,128)(2,1)S(1)}, u32[]{:S(2)}, u32[]{:S(2)}) collective-permute-start(bf16[256,2048]{1,0:T(8,128)(2,1)S(1)} %get-tuple-element.16.near_ref.refs_3_), channel_id=1, source_target_pairs={{0,1},{1,0},{2,3},{3,2},{4,5},{5,4},{6,7},{7,6},{8,9},{9,8},{10,11... | collective-permute-start | bytes 3145736 | tf_op jit(solution)/shard_map/ppermute | solution.py:40
  35.6 14.4 %collective-permute-start.5 = (bf16[256,512]{1,0:T(8,128)(2,1)S(1)}, bf16[256,512]{1,0:T(8,128)(2,1)S(1)}, u32[]{:S(2)}, u32[]{:S(2)}) collective-permute-start(bf16[256,512]{1,0:T(8,128)(2,1)S(1)} %get-tuple-element.25.refs_0_), channel_id=1, source_target_pairs={{0,10},{2,8},{4,14},{6,12},{8,2},{10,0},{12,6},{14,4},{16,26},{18,... | collective-permute-start | bytes 786440 | tf_op jit(solution)/shard_map/ppermute | solution.py:47
  35.7 14.3 %collective-permute-start.4 = (bf16[256,512]{1,0:T(8,128)(2,1)S(1)}, bf16[256,512]{1,0:T(8,128)(2,1)S(1)}, u32[]{:S(2)}, u32[]{:S(2)}) collective-permute-start(bf16[256,512]{1,0:T(8,128)(2,1)S(1)} %get-tuple-element.25.refs_0_), channel_id=1, source_target_pairs={{0,8},{2,10},{4,12},{6,14},{8,0},{10,2},{12,4},{14,6},{16,24},{18,... | collective-permute-start | bytes 786440 | tf_op jit(solution)/shard_map/ppermute | solution.py:47
  37.5 13.4 %collective-permute-start.3 = (bf16[256,512]{1,0:T(8,128)(2,1)S(1)}, bf16[256,512]{1,0:T(8,128)(2,1)S(1)}, u32[]{:S(2)}, u32[]{:S(2)}) collective-permute-start(bf16[256,512]{1,0:T(8,128)(2,1)S(1)} %get-tuple-element.25.refs_0_), channel_id=1, source_target_pairs={{0,2},{2,0},{4,6},{6,4},{8,10},{10,8},{12,14},{14,12},{16,18},{18,... | collective-permute-start | bytes 786440 | tf_op jit(solution)/shard_map/ppermute | solution.py:47
  39.2 6.1 %copy-start = (bf16[256,2048]{1,0:T(8,128)(2,1)}, bf16[256,2048]{1,0:T(8,128)(2,1)S(1)}, u32[]{:S(2)}) copy-start(bf16[256,2048]{1,0:T(8,128)(2,1)S(1)} %collective-permute-done.far_ref.refs_4_) | copy-start | bytes 3145732
  45.3 15.6 %all-to-all-start.1 = ((f32[128,4,128]{2,1,0:T(4,128)}), f32[128,4,128]{2,1,0:T(4,128)S(1)}, u32[]{:S(2)}, u32[]{:S(2)}) async-start(f32[128,4,128]{2,1,0:T(4,128)} %get-tuple-element.17), calls=%async_computation.1 | async-start | bytes 524288 | tf_op jit(solution)/shard_map/all_to_all | solution.py:410
  49.9 1.6 %copy-start.3 = (bf16[512,1024]{1,0:T(8,128)(2,1)S(1)}, bf16[512,1024]{1,0:T(8,128)(2,1)}, u32[]{:S(2)}) copy-start(bf16[512,1024]{1,0:T(8,128)(2,1)} %get-tuple-element.19.left_ref) | copy-start | bytes 3145732
  49.9 7.1 %collective-permute-start.1 = (f32[8,256]{1,0:T(8,128)S(1)}, f32[8,256]{1,0:T(8,128)S(1)}, u32[]{:S(2)}, u32[]{:S(2)}) collective-permute-start(f32[8,256]{1,0:T(8,128)S(1)} %get-tuple-element.18.last_ref.refs_4_), channel_id=1, source_target_pairs={{0,1},{1,0},{2,3},{3,2},{4,5},{5,4},{6,7},{7,6},{8,9},{9,8},{10,11... | collective-permute-start | bytes 24584 | tf_op jit(solution)/shard_map/ppermute | solution.py:40
  50.9 20.0 %collective-permute-start.6 = (bf16[256,2048]{1,0:T(8,128)(2,1)S(1)}, bf16[256,2048]{1,0:T(8,128)(2,1)}, u32[]{:S(2)}, u32[]{:S(2)}) collective-permute-start(bf16[256,2048]{1,0:T(8,128)(2,1)S(1)} %joined_quarters.1.refs_1_), channel_id=1, source_target_pairs={{0,1},{1,0},{2,3},{3,2},{4,5},{5,4},{6,7},{7,6},{8,9},{9,8},{10,11... | collective-permute-start | bytes 3145736 | tf_op jit(solution)/shard_map/ppermute | solution.py:40
  51.0 9.8 %collective-permute-start.2 = (bf16[16,512,128]{2,1,0:T(8,128)(2,1)}, bf16[16,512,128]{2,1,0:T(8,128)(2,1)}, u32[]{:S(2)}, u32[]{:S(2)}) collective-permute-start(bf16[16,512,128]{2,1,0:T(8,128)(2,1)} %get-tuple-element.20), channel_id=1, source_target_pairs={{0,1},{1,0},{2,3},{3,2},{4,5},{5,4},{6,7},{7,6},{8,9},{9,8},{10,11... | collective-permute-start | bytes 6291464 | tf_op jit(solution)/shard_map/ppermute | solution.py:40
  64.9 6.0 %copy-start.4 = (s32[8,2]{0,1:T(2,128)S(1)}, s32[8,2]{0,1:T(2,128)}, u32[]{:S(2)}) copy-start(s32[8,2]{0,1:T(2,128)} %param.13) | copy-start | bytes 196
  64.9 25.0 %all-to-all-start.2 = ((bf16[64,64,128]{2,1,0:T(8,128)(2,1)}), bf16[64,64,128]{2,1,0:T(8,128)(2,1)S(1)}, u32[]{:S(2)}, u32[]{:S(2)}) async-start(bf16[64,64,128]{2,1,0:T(8,128)(2,1)} %get-tuple-element.22), calls=%async_computation.2 | async-start | bytes 2097152 | tf_op jit(solution)/shard_map/all_to_all | solution.py:417
  70.9 7.4 %copy-start.1 = (bf16[256,2048]{1,0:T(8,128)(2,1)S(1)}, bf16[256,2048]{1,0:T(8,128)(2,1)}, u32[]{:S(2)}) copy-start(bf16[256,2048]{1,0:T(8,128)(2,1)} %copy-done) | copy-start | bytes 3145732
  70.9 7.4 %copy-start.2 = (f32[1024,256]{1,0:T(8,128)S(1)}, f32[1024,256]{1,0:T(8,128)}, u32[]{:S(2)}) copy-start(f32[1024,256]{1,0:T(8,128)} %get-tuple-element.23.refs_0_) | copy-start | bytes 3145732

commit v5 on v4

--- a/solution.py
+++ b/solution.py
@@ -176,9 +176,7 @@
         last_ref[...] = jnp.concatenate([peak, picked, jnp.zeros((6, tokens), F32)], axis=0)
         local_norm = peak + jnp.log(total)
         loss = jnp.sum(info_ref[2:3, :] * picked, axis=1, keepdims=True)
-        block = jnp.concatenate(
-            [local_norm[:, place:place + LANES] for place in range(0, tokens, LANES)]
-            + [jnp.broadcast_to(loss, (4 - tokens // LANES, LANES))], axis=0)
+        block = jnp.concatenate([local_norm, jnp.broadcast_to(loss, (1, LANES))], axis=1)
         stats_ref[...] = jnp.broadcast_to(block[None], stats_ref.shape)
         copies.append(pltpu.make_async_copy(stats_ref, stats_hbm, sems.at[1]))
         copies[-1].start()
@@ -196,7 +194,7 @@
             copy.wait()
 
     shapes = [
-        ((rows, tokens), F32), ((devices, 4, LANES), F32),
+        ((rows, tokens), F32), ((devices, 1, tokens + LANES), F32),
         ((2 * tokens, rows), BF16), ((blocks, 2 * tokens, LANES), BF16),
     ]
     return call(
@@ -250,7 +248,6 @@
     blocks = home.shape[0]
     sections = lax.axis_size("y")
     owned = tokens // sections
-    lines = tokens // LANES
 
     def kernel(stats_ref, info_ref, last_ref, other_last_ref, home_hbm, away_hbm, out_hbm, norm_ref, loss_ref,
                home_ref, away_ref, out_ref, in_sems, out_sems):
@@ -266,16 +263,13 @@
             for load in loads[-1]:
                 load.start()
 
-        def flat(block, first):
-            return jnp.concatenate([block[first + line:first + line + 1] for line in range(lines)], axis=1)
-
-        everyone = stats_ref[...]
-        peaks = jnp.max(everyone, axis=0)
-        totals = jnp.sum(jnp.exp(everyone - peaks[None]), axis=0)
-        norm = flat(peaks, 0) + jnp.log(flat(totals, 0))
+        everyone = stats_ref[:, 0, :]
+        norms = everyone[:, :tokens]
+        peak = jnp.max(norms, axis=0, keepdims=True)
+        norm = peak + jnp.log(jnp.sum(jnp.exp(norms - peak), axis=0, keepdims=True))
         weights = info_ref[2:3, :]
         norm_ref[...] = norm
-        picked = jnp.sum(everyone, axis=0)[lines:lines + 1, 0:1]
+        picked = jnp.sum(everyone[:, tokens:tokens + 1], axis=0, keepdims=True)
         loss_ref[...] = ((jnp.sum(weights * norm, axis=1, keepdims=True) - picked)
                          / jnp.sum(weights, axis=1, keepdims=True))
         target = jnp.minimum(last_ref[1:2, :] + other_last_ref[1:2, :], norm)
@@ -398,7 +392,7 @@
               * lax.axis_size("z") + lax.axis_index("z")) * 2 + core
     at_core = core[None].astype(I32)
     start = device[None].astype(I32) * voc_rows
-    own_quarter = (lax.axis_index("x") % 2 * 2 + lax.axis_index("z") % 2)[None].astype(I32)
+    own_quarter = ((lax.axis_index("x") & 1) * 2 + (lax.axis_index("z") & 1))[None].astype(I32)
 
     sizes = tuple(lax.axis_size(name) for name in CHIPS)
     blocks = device_blocks([at_core, start, own_quarter], targets, token_weight, token_ids, hidden, embed_cotangent, sizes)

time: 91 us -> 90.9 us (level)
  no operation moved by 1% of the time
where the time goes in v5:
time: 90.9 us; the launch traced here: 90.5 us
  blocking collectives  33.7 us (37%)
  Pallas kernels  31 us (34%)
  starting transfers between devices  15.6 us (17%)
  waiting for transfers between devices  9.35 us (10%)
    all_to_all x1, blocking collectives, local(): gathered = lax.all_to_all(blocks, ALL, 0, 0, tiled=True)  33.7 us
    pallas_call x9, Pallas kernels, call(): pl.pallas_call(kernel, name=name, out_shape=out_shape, grid_spec=pltpu.Pr...  31 us
    all_to_all x1, starting transfers between devices, local(): grad_hidden = summed_parts(lax.all_to_all(pair, CHIPS, 0, 0, tiled=True))  6.65 us
    all_to_all x1, waiting for transfers between devices, local(): grad_hidden = summed_parts(lax.all_to_all(pair, CHIPS, 0, 0, tiled=True))  5.41 us
    all_to_all x1, starting transfers between devices, local(): stats = lax.all_to_all(stats, ALL, 0, 0, tiled=True)  4.63 us
    ppermute x3, starting transfers between devices, quarters_around(): lax.ppermute(value, ('x', 'z'), [(i, i ^ bit) for i in range(count)])  3.56 us
    all_to_all x1, waiting for transfers between devices, local(): stats = lax.all_to_all(stats, ALL, 0, 0, tiled=True)  3.09 us
  transfers between devices with their start and end apart: 9, of which 3 were waited for; matrix products, arithmetic and copies ran while one was open for 0% of the time, Pallas kernels for 32%

profile of v5, /device:TPU:0, one launch (start us, length us, event | category | flops | bytes accessed | tf_op | source)
XLA Modules:
  0.0 90.5 jit_solution(4296690143889378441)
XLA Ops:
  0.6 0.9 %device_blocks.1 = bf16[128,2,2688]{2,1,0:T(2,128)(2,1)S(1)} custom-call(s32[1]{0:T(128)} %bitcast.core_ref, s32[1]{0:T(128)} %bitcast.1.start_ref, s32[1]{0:T(128)} %bitcast.2.quarter_ref.own_ref, s32[2]{0:T(128)} %targets_hbm.1, bf16[2]{0:T(256)(128)(2,1)} %weights_hbm.1, s32[2]{0:T(128)} %ids_hbm.1, bf16[2,4096]{1,0:T(2,128)(2,1)} %hidden_hbm.1, ...), custom_call_target="tpu_custom_call" | custom-call | bytes 2097152 | tf_op jit(solution)/shard_map/device_blocks/pallas_call | solution.py:19
  1.6 0.0 slice-start
  1.6 33.7 %all_to_all.15.gathered_ref = bf16[128,2,2688]{2,1,0:T(2,128)(2,1)S(1)} all-to-all(bf16[128,2,2688]{2,1,0:T(2,128)(2,1)S(1)} %device_blocks.1), channel_id=1, replica_groups=mesh['y'=4,'x'=4,'z'=4,'c'=2] {'y','x','z','c'}, dimensions={0} | all-to-all | bytes 2752512 | tf_op jit(solution)/shard_map/all_to_all | solution.py:399
  35.3 0.3 token_rows.1
  35.6 0.1 collective-permute-start
  35.6 0.1 collective-permute-start.5
  35.7 1.7 %collective-permute-start.4 = (bf16[256,512]{1,0:T(8,128)(2,1)S(1)}, bf16[256,512]{1,0:T(8,128)(2,1)S(1)}, u32[]{:S(2)}, u32[]{:S(2)}) collective-permute-start(bf16[256,512]{1,0:T(8,128)(2,1)S(1)} %get-tuple-element.25.refs_0_), channel_id=1, source_target_pairs={{0,8},{2,10},{4,12},{6,14},{8,0},{10,2},{12,4},{14,6},{16,24},{18,... | collective-permute-start | bytes 786440 | tf_op jit(solution)/shard_map/ppermute | solution.py:47
  37.5 1.7 %collective-permute-start.3 = (bf16[256,512]{1,0:T(8,128)(2,1)S(1)}, bf16[256,512]{1,0:T(8,128)(2,1)S(1)}, u32[]{:S(2)}, u32[]{:S(2)}) collective-permute-start(bf16[256,512]{1,0:T(8,128)(2,1)S(1)} %get-tuple-element.25.refs_0_), channel_id=1, source_target_pairs={{0,2},{2,0},{4,6},{6,4},{8,10},{10,8},{12,14},{14,12},{16,18},{18,... | collective-permute-start | bytes 786440 | tf_op jit(solution)/shard_map/ppermute | solution.py:47
  39.2 6.0 %local_logits.1 = (f32[1024,256]{1,0:T(8,128)}, f32[128,1,384]{2,1,0:T(1,128)}, bf16[512,1024]{1,0:T(8,128)(2,1)}, bf16[16,512,128]{2,1,0:T(8,128)(2,1)}, f32[8,256]{1,0:T(8,128)S(1)}) custom-call(s32[1]{0:T(128)} %bitcast.core_ref, s32[1]{0:T(128)} %bitcast.1.start_ref, f32[8,256]{1,0:T(8,128)S(1)} %get-tuple-element.15.info_ref.refs_1_.refs_0_, ...), custom_call_target="tpu_custom_call" | custom-call | flops 4294967296 | bytes 8388608 | tf_op jit(solution)/shard_map/local_logits/pallas_call | solution.py:19
  45.3 4.6 %all-to-all-start.1 = ((f32[128,1,384]{2,1,0:T(1,128)}), f32[128,1,384]{2,1,0:T(1,128)S(1)}, u32[]{:S(2)}, u32[]{:S(2)}) async-start(f32[128,1,384]{2,1,0:T(1,128)} %get-tuple-element.17), calls=%async_computation.1 | async-start | bytes 393216 | tf_op jit(solution)/shard_map/all_to_all | solution.py:404
  49.9 0.1 collective-permute-start.1
  50.0 0.8 collective-permute-done.3.refs_1_
  50.9 0.1 joined_quarters.1.refs_1_
  50.9 0.1 collective-permute-start.6
  51.0 0.5 collective-permute-start.2
  51.5 5.5 %feature_partials.1.home_hbm = bf16[16,512,128]{2,1,0:T(8,128)(2,1)} custom-call(s32[1]{0:T(128)} %bitcast.core_ref, bf16[512,1024]{1,0:T(8,128)(2,1)S(1)} %copy-done.3, bf16[1024,4096]{1,0:T(8,128)(2,1)} %head_hbm.1), custom_call_target="tpu_custom_call" | custom-call | flops 34359738368 | bytes 8388608 | tf_op jit(solution)/shard_map/feature_partials/pallas_call | solution.py:19
  57.0 3.1 %all-to-all-done.1.stats_ref = f32[128,1,384]{2,1,0:T(1,128)S(1)} async-done(((f32[128,1,384]{2,1,0:T(1,128)}), f32[128,1,384]{2,1,0:T(1,128)S(1)}, u32[]{:S(2)}, u32[]{:S(2)}) %all-to-all-start.1) | async-done | bytes 196640 | tf_op jit(solution)/shard_map/all_to_all | solution.py:404
  60.1 3.9 %scaled_pair.1 = (bf16[64,64,128]{2,1,0:T(8,128)(2,1)}, f32[1,256]{1,0:T(1,128)S(1)}, f32[1,1]{1,0:T(1,128)}) custom-call(f32[128,1,384]{2,1,0:T(1,128)S(1)} %all-to-all-done.1.stats_ref, f32[8,256]{1,0:T(8,128)S(1)} %get-tuple-element.15.info_ref.refs_1_.refs_0_, f32[8,256]{1,0:T(8,128)S(1)} %get-tuple-element.18.last_ref.refs_4_, ...), custom_call_target="tpu_custom_call" | custom-call | flops 5242880 | bytes 5242880 | tf_op jit(solution)/shard_map/scaled_pair/pallas_call | solution.py:19
  64.1 6.6 %all-to-all-start.2 = ((bf16[64,64,128]{2,1,0:T(8,128)(2,1)}), bf16[64,64,128]{2,1,0:T(8,128)(2,1)S(1)}, u32[]{:S(2)}, u32[]{:S(2)}) async-start(bf16[64,64,128]{2,1,0:T(8,128)(2,1)} %get-tuple-element.22), calls=%async_computation.2 | async-start | bytes 2097152 | tf_op jit(solution)/shard_map/all_to_all | solution.py:411
  70.7 0.1 copy.11.ranges_ref
  70.8 7.3 %grad_embed.1 = bf16[1024,4096]{1,0:T(8,128)(2,1)} custom-call(s32[1]{0:T(128)} %bitcast.core_ref, s32[1]{0:T(128)} %bitcast.1.start_ref, s32[8,2]{1,0:T(8,128)S(1)} %copy.11.ranges_ref, f32[8,256]{1,0:T(8,128)S(1)} %get-tuple-element.15.info_ref.refs_1_.refs_0_, bf16[256,2048]{1,0:T(8,128)(2,1)S(1)} %joined_quarters.1.refs_1_, ...), custom_call_target="tpu_custom_call" | custom-call | flops 2147483648 | bytes 8388608 | tf_op jit(solution)/shard_map/grad_embed/pallas_call | solution.py:19
  78.2 6.2 %grad_head.1 = bf16[1024,4096]{1,0:T(8,128)(2,1)} custom-call(s32[1]{0:T(128)} %bitcast.core_ref, s32[1]{0:T(128)} %bitcast.1.start_ref, s32[8,2]{1,0:T(8,128)S(1)} %copy.11.ranges_ref, f32[1024,256]{1,0:T(8,128)S(1)} %copy-done.2, f32[8,256]{1,0:T(8,128)S(1)} %get-tuple-element.15.info_ref.refs_1_.refs_0_, f32[1,256]{1,0:T(1,128)S(1)} %get-tuple-element.24.refs_2_, ...), custom_call_target="tpu_custom_call" | custom-call | flops 2147483648 | bytes 8388608 | tf_op jit(solution)/shard_map/grad_head/pallas_call | solution.py:19
  84.4 5.4 %all-to-all-done.2.parts_ref = bf16[64,64,128]{2,1,0:T(8,128)(2,1)S(1)} async-done(((bf16[64,64,128]{2,1,0:T(8,128)(2,1)}), bf16[64,64,128]{2,1,0:T(8,128)(2,1)S(1)}, u32[]{:S(2)}, u32[]{:S(2)}) %all-to-all-start.2) | async-done | bytes 1048608 | tf_op jit(solution)/shard_map/all_to_all | solution.py:411
  89.8 0.8 summed_parts.1
  (20 shorter events, 0.0 us)
Async XLA Ops:
  1.6 37.6 %slice-start = ((s8[8388608]{0:T(1024)(128)(4,1)}), s8[4194304]{0:T(1024)(128)(4,1)S(1)}, s32[]{:S(2)}) async-start(s8[8388608]{0:T(1024)(128)(4,1)} %bitcast.4), calls=%async_computation.3 | async-start | bytes 8388608
  35.3 3.9 %slice-start.1 = ((s8[8388608]{0:T(1024)(128)(4,1)}), s8[4194304]{0:T(1024)(128)(4,1)S(1)}, s32[]{:S(2)}) async-start(s8[8388608]{0:T(1024)(128)(4,1)} %bitcast.4), calls=%async_computation.4 | async-start | bytes 8388608
  35.6 3.6 %collective-permute-start = (bf16[256,2048]{1,0:T(8,128)(2,1)S(1)}, bf16[256,2048]{1,0:T(8,128)(2,1)S(1)}, u32[]{:S(2)}, u32[]{:S(2)}) collective-permute-start(bf16[256,2048]{1,0:T(8,128)(2,1)S(1)} %get-tuple-element.16.near_ref.refs_3_), channel_id=1, source_target_pairs={{0,1},{1,0},{2,3},{3,2},{4,5},{5,4},{6,7},{7,6},{8,9},{9,8},{10,11... | collective-permute-start | bytes 3145736 | tf_op jit(solution)/shard_map/ppermute | solution.py:40
  35.6 14.4 %collective-permute-start.5 = (bf16[256,512]{1,0:T(8,128)(2,1)S(1)}, bf16[256,512]{1,0:T(8,128)(2,1)S(1)}, u32[]{:S(2)}, u32[]{:S(2)}) collective-permute-start(bf16[256,512]{1,0:T(8,128)(2,1)S(1)} %get-tuple-element.25.refs_0_), channel_id=1, source_target_pairs={{0,10},{2,8},{4,14},{6,12},{8,2},{10,0},{12,6},{14,4},{16,26},{18,... | collective-permute-start | bytes 786440 | tf_op jit(solution)/shard_map/ppermute | solution.py:47
  35.7 14.3 %collective-permute-start.4 = (bf16[256,512]{1,0:T(8,128)(2,1)S(1)}, bf16[256,512]{1,0:T(8,128)(2,1)S(1)}, u32[]{:S(2)}, u32[]{:S(2)}) collective-permute-start(bf16[256,512]{1,0:T(8,128)(2,1)S(1)} %get-tuple-element.25.refs_0_), channel_id=1, source_target_pairs={{0,8},{2,10},{4,12},{6,14},{8,0},{10,2},{12,4},{14,6},{16,24},{18,... | collective-permute-start | bytes 786440 | tf_op jit(solution)/shard_map/ppermute | solution.py:47
  37.5 13.4 %collective-permute-start.3 = (bf16[256,512]{1,0:T(8,128)(2,1)S(1)}, bf16[256,512]{1,0:T(8,128)(2,1)S(1)}, u32[]{:S(2)}, u32[]{:S(2)}) collective-permute-start(bf16[256,512]{1,0:T(8,128)(2,1)S(1)} %get-tuple-element.25.refs_0_), channel_id=1, source_target_pairs={{0,2},{2,0},{4,6},{6,4},{8,10},{10,8},{12,14},{14,12},{16,18},{18,... | collective-permute-start | bytes 786440 | tf_op jit(solution)/shard_map/ppermute | solution.py:47
  39.2 6.1 %copy-start = (bf16[256,2048]{1,0:T(8,128)(2,1)}, bf16[256,2048]{1,0:T(8,128)(2,1)S(1)}, u32[]{:S(2)}) copy-start(bf16[256,2048]{1,0:T(8,128)(2,1)S(1)} %collective-permute-done.far_ref.refs_4_) | copy-start | bytes 3145732
  45.3 14.9 %all-to-all-start.1 = ((f32[128,1,384]{2,1,0:T(1,128)}), f32[128,1,384]{2,1,0:T(1,128)S(1)}, u32[]{:S(2)}, u32[]{:S(2)}) async-start(f32[128,1,384]{2,1,0:T(1,128)} %get-tuple-element.17), calls=%async_computation.1 | async-start | bytes 393216 | tf_op jit(solution)/shard_map/all_to_all | solution.py:404
  49.9 1.6 %copy-start.3 = (bf16[512,1024]{1,0:T(8,128)(2,1)S(1)}, bf16[512,1024]{1,0:T(8,128)(2,1)}, u32[]{:S(2)}) copy-start(bf16[512,1024]{1,0:T(8,128)(2,1)} %get-tuple-element.19.left_ref) | copy-start | bytes 3145732
  49.9 7.1 %collective-permute-start.1 = (f32[8,256]{1,0:T(8,128)S(1)}, f32[8,256]{1,0:T(8,128)S(1)}, u32[]{:S(2)}, u32[]{:S(2)}) collective-permute-start(f32[8,256]{1,0:T(8,128)S(1)} %get-tuple-element.18.last_ref.refs_4_), channel_id=1, source_target_pairs={{0,1},{1,0},{2,3},{3,2},{4,5},{5,4},{6,7},{7,6},{8,9},{9,8},{10,11... | collective-permute-start | bytes 24584 | tf_op jit(solution)/shard_map/ppermute | solution.py:40
  50.9 19.9 %collective-permute-start.6 = (bf16[256,2048]{1,0:T(8,128)(2,1)S(1)}, bf16[256,2048]{1,0:T(8,128)(2,1)}, u32[]{:S(2)}, u32[]{:S(2)}) collective-permute-start(bf16[256,2048]{1,0:T(8,128)(2,1)S(1)} %joined_quarters.1.refs_1_), channel_id=1, source_target_pairs={{0,1},{1,0},{2,3},{3,2},{4,5},{5,4},{6,7},{7,6},{8,9},{9,8},{10,11... | collective-permute-start | bytes 3145736 | tf_op jit(solution)/shard_map/ppermute | solution.py:40
  51.0 9.1 %collective-permute-start.2 = (bf16[16,512,128]{2,1,0:T(8,128)(2,1)}, bf16[16,512,128]{2,1,0:T(8,128)(2,1)}, u32[]{:S(2)}, u32[]{:S(2)}) collective-permute-start(bf16[16,512,128]{2,1,0:T(8,128)(2,1)} %get-tuple-element.20), channel_id=1, source_target_pairs={{0,1},{1,0},{2,3},{3,2},{4,5},{5,4},{6,7},{7,6},{8,9},{9,8},{10,11... | collective-permute-start | bytes 6291464 | tf_op jit(solution)/shard_map/ppermute | solution.py:40
  64.1 6.7 %copy-start.4 = (s32[8,2]{0,1:T(2,128)S(1)}, s32[8,2]{0,1:T(2,128)}, u32[]{:S(2)}) copy-start(s32[8,2]{0,1:T(2,128)} %param.13) | copy-start | bytes 196
  64.1 25.7 %all-to-all-start.2 = ((bf16[64,64,128]{2,1,0:T(8,128)(2,1)}), bf16[64,64,128]{2,1,0:T(8,128)(2,1)S(1)}, u32[]{:S(2)}, u32[]{:S(2)}) async-start(bf16[64,64,128]{2,1,0:T(8,128)(2,1)} %get-tuple-element.22), calls=%async_computation.2 | async-start | bytes 2097152 | tf_op jit(solution)/shard_map/all_to_all | solution.py:411
  70.8 7.4 %copy-start.1 = (bf16[256,2048]{1,0:T(8,128)(2,1)S(1)}, bf16[256,2048]{1,0:T(8,128)(2,1)}, u32[]{:S(2)}) copy-start(bf16[256,2048]{1,0:T(8,128)(2,1)} %copy-done) | copy-start | bytes 3145732
  70.8 7.4 %copy-start.2 = (f32[1024,256]{1,0:T(8,128)S(1)}, f32[1024,256]{1,0:T(8,128)}, u32[]{:S(2)}) copy-start(f32[1024,256]{1,0:T(8,128)} %get-tuple-element.23.refs_0_) | copy-start | bytes 3145732

commit v6 on v5

--- a/solution.py
+++ b/solution.py
@@ -211,23 +211,25 @@
     count, rows = left.shape
     width = head_weight.shape[1]
     blocks = width // (2 * LANES)
-    step = 1024
-    held = step // (2 * LANES)
 
     def kernel(core_ref, left_ref, head_hbm, out_hbm, head_ref, out_ref, head_sems, out_sems):
-        loads = [
-            pltpu.make_async_copy(head_hbm.at[:, pl.ds(place * step, step)], head_ref.at[place], head_sems.at[place])
-            for place in range(width // step)]
-        for load in loads:
-            load.start()
+        loads = []
+        for block in range(blocks):
+            columns = pl.ds(pl.multiple_of((2 * block + core_ref[0]) * LANES, LANES), LANES)
+            loads.append(pltpu.make_async_copy(head_hbm.at[:, columns], head_ref.at[block], head_sems.at[block]))
+            loads[-1].start()
         stores = []
-        for place, load in enumerate(loads):
-            load.wait()
-            for block, lines, even, odd in feature_products(core_ref[0], left_ref, head_ref.at[place], 0, held):
-                out_ref[place * held + block, lines, :] = even
-                out_ref[place * held + block + 1, lines, :] = odd
-            part = pl.ds(place * held, held)
-            stores.append(pltpu.make_async_copy(out_ref.at[part], out_hbm.at[part], out_sems.at[place]))
+        for block in range(0, blocks, 2):
+            loads[block].wait()
+            loads[block + 1].wait()
+            columns = jnp.concatenate([head_ref[block], head_ref[block + 1]], axis=1)
+            for line in range(0, count, count // 2):
+                lines = slice(line, line + count // 2)
+                total = jnp.dot(left_ref[lines, :], columns, preferred_element_type=F32).astype(BF16)
+                out_ref[block, lines, :] = total[:, :LANES]
+                out_ref[block + 1, lines, :] = total[:, LANES:]
+            done = pl.ds(block, 2)
+            stores.append(pltpu.make_async_copy(out_ref.at[done], out_hbm.at[done], out_sems.at[block // 2]))
             stores[-1].start()
         for store in stores:
             store.wait()
@@ -236,8 +238,8 @@
     return call(
         kernel, "feature_partials", pltpu.HBM(*shape), (), [WHOLE, IN_HBM], IN_HBM,
         [
-            pltpu.VMEM((width // step, rows, step), BF16), pltpu.VMEM(*shape),
-            pltpu.SemaphoreType.DMA((width // step,)), pltpu.SemaphoreType.DMA((width // step,)),
+            pltpu.VMEM((blocks, rows, LANES), BF16), pltpu.VMEM(*shape),
+            pltpu.SemaphoreType.DMA((blocks,)), pltpu.SemaphoreType.DMA((blocks // 2,)),
         ],
         1 << 35, 2 * rows * width, [core], left, in_hbm(head_weight),
     )

time: 90.9 us -> 90.9 us (level)
  no operation moved by 1% of the time
where the time goes in v6:
time: 90.9 us; the launch traced here: 90.5 us
  blocking collectives  33.7 us (37%)
  Pallas kernels  31 us (34%)
  starting transfers between devices  15.6 us (17%)
  waiting for transfers between devices  9.35 us (10%)
    all_to_all x1, blocking collectives, local(): gathered = lax.all_to_all(blocks, ALL, 0, 0, tiled=True)  33.7 us
    pallas_call x9, Pallas kernels, call(): pl.pallas_call(kernel, name=name, out_shape=out_shape, grid_spec=pltpu.Pr...  31 us
    all_to_all x1, starting transfers between devices, local(): grad_hidden = summed_parts(lax.all_to_all(pair, CHIPS, 0, 0, tiled=True))  6.64 us
    all_to_all x1, waiting for transfers between devices, local(): grad_hidden = summed_parts(lax.all_to_all(pair, CHIPS, 0, 0, tiled=True))  5.4 us
    all_to_all x1, starting transfers between devices, local(): stats = lax.all_to_all(stats, ALL, 0, 0, tiled=True)  4.63 us
    ppermute x3, starting transfers between devices, quarters_around(): lax.ppermute(value, ('x', 'z'), [(i, i ^ bit) for i in range(count)])  3.56 us
    all_to_all x1, waiting for transfers between devices, local(): stats = lax.all_to_all(stats, ALL, 0, 0, tiled=True)  3.1 us
  transfers between devices with their start and end apart: 9, of which 3 were waited for; matrix products, arithmetic and copies ran while one was open for 0% of the time, Pallas kernels for 32%

profile of v6, /device:TPU:0, one launch (start us, length us, event | category | flops | bytes accessed | tf_op | source)
XLA Modules:
  0.0 90.5 jit_solution(12541182640907800851)
XLA Ops:
  0.6 0.9 %device_blocks.1 = bf16[128,2,2688]{2,1,0:T(2,128)(2,1)S(1)} custom-call(s32[1]{0:T(128)} %bitcast.core_ref, s32[1]{0:T(128)} %bitcast.1.start_ref, s32[1]{0:T(128)} %bitcast.2.quarter_ref.own_ref, s32[2]{0:T(128)} %targets_hbm.1, bf16[2]{0:T(256)(128)(2,1)} %weights_hbm.1, s32[2]{0:T(128)} %ids_hbm.1, bf16[2,4096]{1,0:T(2,128)(2,1)} %hidden_hbm.1, ...), custom_call_target="tpu_custom_call" | custom-call | bytes 2097152 | tf_op jit(solution)/shard_map/device_blocks/pallas_call | solution.py:19
  1.6 0.0 slice-start
  1.6 33.7 %all_to_all.15.gathered_ref = bf16[128,2,2688]{2,1,0:T(2,128)(2,1)S(1)} all-to-all(bf16[128,2,2688]{2,1,0:T(2,128)(2,1)S(1)} %device_blocks.1), channel_id=1, replica_groups=mesh['y'=4,'x'=4,'z'=4,'c'=2] {'y','x','z','c'}, dimensions={0} | all-to-all | bytes 2752512 | tf_op jit(solution)/shard_map/all_to_all | solution.py:401
  35.3 0.3 token_rows.1
  35.6 0.1 collective-permute-start
  35.6 0.1 collective-permute-start.5
  35.7 1.7 %collective-permute-start.4 = (bf16[256,512]{1,0:T(8,128)(2,1)S(1)}, bf16[256,512]{1,0:T(8,128)(2,1)S(1)}, u32[]{:S(2)}, u32[]{:S(2)}) collective-permute-start(bf16[256,512]{1,0:T(8,128)(2,1)S(1)} %get-tuple-element.25.refs_0_), channel_id=1, source_target_pairs={{0,8},{2,10},{4,12},{6,14},{8,0},{10,2},{12,4},{14,6},{16,24},{18,... | collective-permute-start | bytes 786440 | tf_op jit(solution)/shard_map/ppermute | solution.py:47
  37.5 1.7 %collective-permute-start.3 = (bf16[256,512]{1,0:T(8,128)(2,1)S(1)}, bf16[256,512]{1,0:T(8,128)(2,1)S(1)}, u32[]{:S(2)}, u32[]{:S(2)}) collective-permute-start(bf16[256,512]{1,0:T(8,128)(2,1)S(1)} %get-tuple-element.25.refs_0_), channel_id=1, source_target_pairs={{0,2},{2,0},{4,6},{6,4},{8,10},{10,8},{12,14},{14,12},{16,18},{18,... | collective-permute-start | bytes 786440 | tf_op jit(solution)/shard_map/ppermute | solution.py:47
  39.2 6.0 %local_logits.1 = (f32[1024,256]{1,0:T(8,128)}, f32[128,1,384]{2,1,0:T(1,128)}, bf16[512,1024]{1,0:T(8,128)(2,1)}, bf16[16,512,128]{2,1,0:T(8,128)(2,1)}, f32[8,256]{1,0:T(8,128)S(1)}) custom-call(s32[1]{0:T(128)} %bitcast.core_ref, s32[1]{0:T(128)} %bitcast.1.start_ref, f32[8,256]{1,0:T(8,128)S(1)} %get-tuple-element.15.info_ref.refs_1_.refs_0_, ...), custom_call_target="tpu_custom_call" | custom-call | flops 4294967296 | bytes 8388608 | tf_op jit(solution)/shard_map/local_logits/pallas_call | solution.py:19
  45.3 4.6 %all-to-all-start.1 = ((f32[128,1,384]{2,1,0:T(1,128)}), f32[128,1,384]{2,1,0:T(1,128)S(1)}, u32[]{:S(2)}, u32[]{:S(2)}) async-start(f32[128,1,384]{2,1,0:T(1,128)} %get-tuple-element.17), calls=%async_computation.1 | async-start | bytes 393216 | tf_op jit(solution)/shard_map/all_to_all | solution.py:406
  49.9 0.1 collective-permute-start.1
  50.0 0.8 collective-permute-done.3.refs_1_
  50.9 0.1 joined_quarters.1.refs_1_
  50.9 0.1 collective-permute-start.6
  51.0 0.5 collective-permute-start.2
  51.5 5.5 %feature_partials.1.home_hbm = bf16[16,512,128]{2,1,0:T(8,128)(2,1)} custom-call(s32[1]{0:T(128)} %bitcast.core_ref, bf16[512,1024]{1,0:T(8,128)(2,1)S(1)} %copy-done.3, bf16[1024,4096]{1,0:T(8,128)(2,1)} %head_hbm.1), custom_call_target="tpu_custom_call" | custom-call | flops 34359738368 | bytes 8388608 | tf_op jit(solution)/shard_map/feature_partials/pallas_call | solution.py:19
  57.0 3.1 %all-to-all-done.1.stats_ref = f32[128,1,384]{2,1,0:T(1,128)S(1)} async-done(((f32[128,1,384]{2,1,0:T(1,128)}), f32[128,1,384]{2,1,0:T(1,128)S(1)}, u32[]{:S(2)}, u32[]{:S(2)}) %all-to-all-start.1) | async-done | bytes 196640 | tf_op jit(solution)/shard_map/all_to_all | solution.py:406
  60.1 3.9 %scaled_pair.1 = (bf16[64,64,128]{2,1,0:T(8,128)(2,1)}, f32[1,256]{1,0:T(1,128)S(1)}, f32[1,1]{1,0:T(1,128)}) custom-call(f32[128,1,384]{2,1,0:T(1,128)S(1)} %all-to-all-done.1.stats_ref, f32[8,256]{1,0:T(8,128)S(1)} %get-tuple-element.15.info_ref.refs_1_.refs_0_, f32[8,256]{1,0:T(8,128)S(1)} %get-tuple-element.18.last_ref.refs_4_, ...), custom_call_target="tpu_custom_call" | custom-call | flops 5242880 | bytes 5242880 | tf_op jit(solution)/shard_map/scaled_pair/pallas_call | solution.py:19
  64.1 6.6 %all-to-all-start.2 = ((bf16[64,64,128]{2,1,0:T(8,128)(2,1)}), bf16[64,64,128]{2,1,0:T(8,128)(2,1)S(1)}, u32[]{:S(2)}, u32[]{:S(2)}) async-start(bf16[64,64,128]{2,1,0:T(8,128)(2,1)} %get-tuple-element.22), calls=%async_computation.2 | async-start | bytes 2097152 | tf_op jit(solution)/shard_map/all_to_all | solution.py:413
  70.7 0.1 copy.11.ranges_ref
  70.8 7.3 %grad_embed.1 = bf16[1024,4096]{1,0:T(8,128)(2,1)} custom-call(s32[1]{0:T(128)} %bitcast.core_ref, s32[1]{0:T(128)} %bitcast.1.start_ref, s32[8,2]{1,0:T(8,128)S(1)} %copy.11.ranges_ref, f32[8,256]{1,0:T(8,128)S(1)} %get-tuple-element.15.info_ref.refs_1_.refs_0_, bf16[256,2048]{1,0:T(8,128)(2,1)S(1)} %joined_quarters.1.refs_1_, ...), custom_call_target="tpu_custom_call" | custom-call | flops 2147483648 | bytes 8388608 | tf_op jit(solution)/shard_map/grad_embed/pallas_call | solution.py:19
  78.2 6.2 %grad_head.1 = bf16[1024,4096]{1,0:T(8,128)(2,1)} custom-call(s32[1]{0:T(128)} %bitcast.core_ref, s32[1]{0:T(128)} %bitcast.1.start_ref, s32[8,2]{1,0:T(8,128)S(1)} %copy.11.ranges_ref, f32[1024,256]{1,0:T(8,128)S(1)} %copy-done.2, f32[8,256]{1,0:T(8,128)S(1)} %get-tuple-element.15.info_ref.refs_1_.refs_0_, f32[1,256]{1,0:T(1,128)S(1)} %get-tuple-element.24.refs_2_, ...), custom_call_target="tpu_custom_call" | custom-call | flops 2147483648 | bytes 8388608 | tf_op jit(solution)/shard_map/grad_head/pallas_call | solution.py:19
  84.4 5.4 %all-to-all-done.2.parts_ref = bf16[64,64,128]{2,1,0:T(8,128)(2,1)S(1)} async-done(((bf16[64,64,128]{2,1,0:T(8,128)(2,1)}), bf16[64,64,128]{2,1,0:T(8,128)(2,1)S(1)}, u32[]{:S(2)}, u32[]{:S(2)}) %all-to-all-start.2) | async-done | bytes 1048608 | tf_op jit(solution)/shard_map/all_to_all | solution.py:413
  89.8 0.8 summed_parts.1
  (20 shorter events, 0.0 us)
Async XLA Ops:
  1.6 37.6 %slice-start = ((s8[8388608]{0:T(1024)(128)(4,1)}), s8[4194304]{0:T(1024)(128)(4,1)S(1)}, s32[]{:S(2)}) async-start(s8[8388608]{0:T(1024)(128)(4,1)} %bitcast.4), calls=%async_computation.3 | async-start | bytes 8388608
  35.3 3.9 %slice-start.1 = ((s8[8388608]{0:T(1024)(128)(4,1)}), s8[4194304]{0:T(1024)(128)(4,1)S(1)}, s32[]{:S(2)}) async-start(s8[8388608]{0:T(1024)(128)(4,1)} %bitcast.4), calls=%async_computation.4 | async-start | bytes 8388608
  35.6 3.6 %collective-permute-start = (bf16[256,2048]{1,0:T(8,128)(2,1)S(1)}, bf16[256,2048]{1,0:T(8,128)(2,1)S(1)}, u32[]{:S(2)}, u32[]{:S(2)}) collective-permute-start(bf16[256,2048]{1,0:T(8,128)(2,1)S(1)} %get-tuple-element.16.near_ref.refs_3_), channel_id=1, source_target_pairs={{0,1},{1,0},{2,3},{3,2},{4,5},{5,4},{6,7},{7,6},{8,9},{9,8},{10,11... | collective-permute-start | bytes 3145736 | tf_op jit(solution)/shard_map/ppermute | solution.py:40
  35.6 14.4 %collective-permute-start.5 = (bf16[256,512]{1,0:T(8,128)(2,1)S(1)}, bf16[256,512]{1,0:T(8,128)(2,1)S(1)}, u32[]{:S(2)}, u32[]{:S(2)}) collective-permute-start(bf16[256,512]{1,0:T(8,128)(2,1)S(1)} %get-tuple-element.25.refs_0_), channel_id=1, source_target_pairs={{0,10},{2,8},{4,14},{6,12},{8,2},{10,0},{12,6},{14,4},{16,26},{18,... | collective-permute-start | bytes 786440 | tf_op jit(solution)/shard_map/ppermute | solution.py:47
  35.7 14.3 %collective-permute-start.4 = (bf16[256,512]{1,0:T(8,128)(2,1)S(1)}, bf16[256,512]{1,0:T(8,128)(2,1)S(1)}, u32[]{:S(2)}, u32[]{:S(2)}) collective-permute-start(bf16[256,512]{1,0:T(8,128)(2,1)S(1)} %get-tuple-element.25.refs_0_), channel_id=1, source_target_pairs={{0,8},{2,10},{4,12},{6,14},{8,0},{10,2},{12,4},{14,6},{16,24},{18,... | collective-permute-start | bytes 786440 | tf_op jit(solution)/shard_map/ppermute | solution.py:47
  37.5 13.4 %collective-permute-start.3 = (bf16[256,512]{1,0:T(8,128)(2,1)S(1)}, bf16[256,512]{1,0:T(8,128)(2,1)S(1)}, u32[]{:S(2)}, u32[]{:S(2)}) collective-permute-start(bf16[256,512]{1,0:T(8,128)(2,1)S(1)} %get-tuple-element.25.refs_0_), channel_id=1, source_target_pairs={{0,2},{2,0},{4,6},{6,4},{8,10},{10,8},{12,14},{14,12},{16,18},{18,... | collective-permute-start | bytes 786440 | tf_op jit(solution)/shard_map/ppermute | solution.py:47
  39.2 6.1 %copy-start = (bf16[256,2048]{1,0:T(8,128)(2,1)}, bf16[256,2048]{1,0:T(8,128)(2,1)S(1)}, u32[]{:S(2)}) copy-start(bf16[256,2048]{1,0:T(8,128)(2,1)S(1)} %collective-permute-done.far_ref.refs_4_) | copy-start | bytes 3145732
  45.3 14.9 %all-to-all-start.1 = ((f32[128,1,384]{2,1,0:T(1,128)}), f32[128,1,384]{2,1,0:T(1,128)S(1)}, u32[]{:S(2)}, u32[]{:S(2)}) async-start(f32[128,1,384]{2,1,0:T(1,128)} %get-tuple-element.17), calls=%async_computation.1 | async-start | bytes 393216 | tf_op jit(solution)/shard_map/all_to_all | solution.py:406
  49.9 1.6 %copy-start.3 = (bf16[512,1024]{1,0:T(8,128)(2,1)S(1)}, bf16[512,1024]{1,0:T(8,128)(2,1)}, u32[]{:S(2)}) copy-start(bf16[512,1024]{1,0:T(8,128)(2,1)} %get-tuple-element.19.left_ref) | copy-start | bytes 3145732
  49.9 7.1 %collective-permute-start.1 = (f32[8,256]{1,0:T(8,128)S(1)}, f32[8,256]{1,0:T(8,128)S(1)}, u32[]{:S(2)}, u32[]{:S(2)}) collective-permute-start(f32[8,256]{1,0:T(8,128)S(1)} %get-tuple-element.18.last_ref.refs_4_), channel_id=1, source_target_pairs={{0,1},{1,0},{2,3},{3,2},{4,5},{5,4},{6,7},{7,6},{8,9},{9,8},{10,11... | collective-permute-start | bytes 24584 | tf_op jit(solution)/shard_map/ppermute | solution.py:40
  50.9 19.9 %collective-permute-start.6 = (bf16[256,2048]{1,0:T(8,128)(2,1)S(1)}, bf16[256,2048]{1,0:T(8,128)(2,1)}, u32[]{:S(2)}, u32[]{:S(2)}) collective-permute-start(bf16[256,2048]{1,0:T(8,128)(2,1)S(1)} %joined_quarters.1.refs_1_), channel_id=1, source_target_pairs={{0,1},{1,0},{2,3},{3,2},{4,5},{5,4},{6,7},{7,6},{8,9},{9,8},{10,11... | collective-permute-start | bytes 3145736 | tf_op jit(solution)/shard_map/ppermute | solution.py:40
  51.0 9.1 %collective-permute-start.2 = (bf16[16,512,128]{2,1,0:T(8,128)(2,1)}, bf16[16,512,128]{2,1,0:T(8,128)(2,1)}, u32[]{:S(2)}, u32[]{:S(2)}) collective-permute-start(bf16[16,512,128]{2,1,0:T(8,128)(2,1)} %get-tuple-element.20), channel_id=1, source_target_pairs={{0,1},{1,0},{2,3},{3,2},{4,5},{5,4},{6,7},{7,6},{8,9},{9,8},{10,11... | collective-permute-start | bytes 6291464 | tf_op jit(solution)/shard_map/ppermute | solution.py:40
  64.1 6.7 %copy-start.4 = (s32[8,2]{0,1:T(2,128)S(1)}, s32[8,2]{0,1:T(2,128)}, u32[]{:S(2)}) copy-start(s32[8,2]{0,1:T(2,128)} %param.13) | copy-start | bytes 196
  64.1 25.7 %all-to-all-start.2 = ((bf16[64,64,128]{2,1,0:T(8,128)(2,1)}), bf16[64,64,128]{2,1,0:T(8,128)(2,1)S(1)}, u32[]{:S(2)}, u32[]{:S(2)}) async-start(bf16[64,64,128]{2,1,0:T(8,128)(2,1)} %get-tuple-element.22), calls=%async_computation.2 | async-start | bytes 2097152 | tf_op jit(solution)/shard_map/all_to_all | solution.py:413
  70.8 7.4 %copy-start.1 = (bf16[256,2048]{1,0:T(8,128)(2,1)S(1)}, bf16[256,2048]{1,0:T(8,128)(2,1)}, u32[]{:S(2)}) copy-start(bf16[256,2048]{1,0:T(8,128)(2,1)} %copy-done) | copy-start | bytes 3145732
  70.8 7.4 %copy-start.2 = (f32[1024,256]{1,0:T(8,128)S(1)}, f32[1024,256]{1,0:T(8,128)}, u32[]{:S(2)}) copy-start(f32[1024,256]{1,0:T(8,128)} %get-tuple-element.23.refs_0_) | copy-start | bytes 3145732

commit v7 on v5

--- a/solution.py
+++ b/solution.py
@@ -146,7 +146,7 @@
 def local_logits(core, start, devices, info, near, far, head_weight):
     tokens = near.shape[0]
     rows, width = head_weight.shape
-    half, step = width // 2, 256
+    half, step = width // 2, 512
     blocks = half // LANES
 
     def kernel(core_ref, start_ref, info_ref, near_ref, far_ref, head_ref,

time: 90.9 us -> 91.1 us (level)
  no operation moved by 1% of the time
where the time goes in v7:
time: 91.1 us; the launch traced here: 90.7 us
  blocking collectives  33.7 us (37%)
  Pallas kernels  30.9 us (34%)
  starting transfers between devices  15.8 us (17%)
  waiting for transfers between devices  9.34 us (10%)
    all_to_all x1, blocking collectives, local(): gathered = lax.all_to_all(blocks, ALL, 0, 0, tiled=True)  33.7 us
    pallas_call x9, Pallas kernels, call(): pl.pallas_call(kernel, name=name, out_shape=out_shape, grid_spec=pltpu.Pr...  30.9 us
    all_to_all x1, starting transfers between devices, local(): grad_hidden = summed_parts(lax.all_to_all(pair, CHIPS, 0, 0, tiled=True))  6.83 us
    all_to_all x1, waiting for transfers between devices, local(): grad_hidden = summed_parts(lax.all_to_all(pair, CHIPS, 0, 0, tiled=True))  5.4 us
    all_to_all x1, starting transfers between devices, local(): stats = lax.all_to_all(stats, ALL, 0, 0, tiled=True)  4.63 us
    ppermute x3, starting transfers between devices, quarters_around(): lax.ppermute(value, ('x', 'z'), [(i, i ^ bit) for i in range(count)])  3.56 us
    all_to_all x1, waiting for transfers between devices, local(): stats = lax.all_to_all(stats, ALL, 0, 0, tiled=True)  3.07 us
  transfers between devices with their start and end apart: 9, of which 3 were waited for; matrix products, arithmetic and copies ran while one was open for 0% of the time, Pallas kernels for 32%

profile of v7, /device:TPU:0, one launch (start us, length us, event | category | flops | bytes accessed | tf_op | source)
XLA Modules:
  0.0 90.7 jit_solution(7499594887223011801)
XLA Ops:
  0.6 0.9 %device_blocks.1 = bf16[128,2,2688]{2,1,0:T(2,128)(2,1)S(1)} custom-call(s32[1]{0:T(128)} %bitcast.core_ref, s32[1]{0:T(128)} %bitcast.1.start_ref, s32[1]{0:T(128)} %bitcast.2.quarter_ref.own_ref, s32[2]{0:T(128)} %targets_hbm.1, bf16[2]{0:T(256)(128)(2,1)} %weights_hbm.1, s32[2]{0:T(128)} %ids_hbm.1, bf16[2,4096]{1,0:T(2,128)(2,1)} %hidden_hbm.1, ...), custom_call_target="tpu_custom_call" | custom-call | bytes 2097152 | tf_op jit(solution)/shard_map/device_blocks/pallas_call | solution.py:19
  1.6 0.0 slice-start
  1.6 33.7 %all_to_all.15.gathered_ref = bf16[128,2,2688]{2,1,0:T(2,128)(2,1)S(1)} all-to-all(bf16[128,2,2688]{2,1,0:T(2,128)(2,1)S(1)} %device_blocks.1), channel_id=1, replica_groups=mesh['y'=4,'x'=4,'z'=4,'c'=2] {'y','x','z','c'}, dimensions={0} | all-to-all | bytes 2752512 | tf_op jit(solution)/shard_map/all_to_all | solution.py:399
  35.3 0.3 token_rows.1
  35.6 0.1 collective-permute-start
  35.6 0.1 collective-permute-start.5
  35.7 1.7 %collective-permute-start.4 = (bf16[256,512]{1,0:T(8,128)(2,1)S(1)}, bf16[256,512]{1,0:T(8,128)(2,1)S(1)}, u32[]{:S(2)}, u32[]{:S(2)}) collective-permute-start(bf16[256,512]{1,0:T(8,128)(2,1)S(1)} %get-tuple-element.25.refs_0_), channel_id=1, source_target_pairs={{0,8},{2,10},{4,12},{6,14},{8,0},{10,2},{12,4},{14,6},{16,24},{18,... | collective-permute-start | bytes 786440 | tf_op jit(solution)/shard_map/ppermute | solution.py:47
  37.5 1.7 %collective-permute-start.3 = (bf16[256,512]{1,0:T(8,128)(2,1)S(1)}, bf16[256,512]{1,0:T(8,128)(2,1)S(1)}, u32[]{:S(2)}, u32[]{:S(2)}) collective-permute-start(bf16[256,512]{1,0:T(8,128)(2,1)S(1)} %get-tuple-element.25.refs_0_), channel_id=1, source_target_pairs={{0,2},{2,0},{4,6},{6,4},{8,10},{10,8},{12,14},{14,12},{16,18},{18,... | collective-permute-start | bytes 786440 | tf_op jit(solution)/shard_map/ppermute | solution.py:47
  39.2 6.0 %local_logits.1 = (f32[1024,256]{1,0:T(8,128)}, f32[128,1,384]{2,1,0:T(1,128)}, bf16[512,1024]{1,0:T(8,128)(2,1)}, bf16[16,512,128]{2,1,0:T(8,128)(2,1)}, f32[8,256]{1,0:T(8,128)S(1)}) custom-call(s32[1]{0:T(128)} %bitcast.core_ref, s32[1]{0:T(128)} %bitcast.1.start_ref, f32[8,256]{1,0:T(8,128)S(1)} %get-tuple-element.15.info_ref.refs_1_.refs_0_, ...), custom_call_target="tpu_custom_call" | custom-call | flops 4294967296 | bytes 8388608 | tf_op jit(solution)/shard_map/local_logits/pallas_call | solution.py:19
  45.2 4.6 %all-to-all-start.1 = ((f32[128,1,384]{2,1,0:T(1,128)}), f32[128,1,384]{2,1,0:T(1,128)S(1)}, u32[]{:S(2)}, u32[]{:S(2)}) async-start(f32[128,1,384]{2,1,0:T(1,128)} %get-tuple-element.17), calls=%async_computation.1 | async-start | bytes 393216 | tf_op jit(solution)/shard_map/all_to_all | solution.py:404
  49.9 0.1 collective-permute-start.1
  50.0 0.9 collective-permute-done.3.refs_1_
  50.9 0.1 joined_quarters.1.refs_1_
  50.9 0.1 collective-permute-start.6
  51.0 0.5 collective-permute-start.2
  51.5 5.5 %feature_partials.1.home_hbm = bf16[16,512,128]{2,1,0:T(8,128)(2,1)} custom-call(s32[1]{0:T(128)} %bitcast.core_ref, bf16[512,1024]{1,0:T(8,128)(2,1)S(1)} %copy-done.3, bf16[1024,4096]{1,0:T(8,128)(2,1)} %head_hbm.1), custom_call_target="tpu_custom_call" | custom-call | flops 34359738368 | bytes 8388608 | tf_op jit(solution)/shard_map/feature_partials/pallas_call | solution.py:19
  57.0 3.1 %all-to-all-done.1.stats_ref = f32[128,1,384]{2,1,0:T(1,128)S(1)} async-done(((f32[128,1,384]{2,1,0:T(1,128)}), f32[128,1,384]{2,1,0:T(1,128)S(1)}, u32[]{:S(2)}, u32[]{:S(2)}) %all-to-all-start.1) | async-done | bytes 196640 | tf_op jit(solution)/shard_map/all_to_all | solution.py:404
  60.1 3.9 %scaled_pair.1 = (bf16[64,64,128]{2,1,0:T(8,128)(2,1)}, f32[1,256]{1,0:T(1,128)S(1)}, f32[1,1]{1,0:T(1,128)}) custom-call(f32[128,1,384]{2,1,0:T(1,128)S(1)} %all-to-all-done.1.stats_ref, f32[8,256]{1,0:T(8,128)S(1)} %get-tuple-element.15.info_ref.refs_1_.refs_0_, f32[8,256]{1,0:T(8,128)S(1)} %get-tuple-element.18.last_ref.refs_4_, ...), custom_call_target="tpu_custom_call" | custom-call | flops 5242880 | bytes 5242880 | tf_op jit(solution)/shard_map/scaled_pair/pallas_call | solution.py:19
  64.1 6.8 %all-to-all-start.2 = ((bf16[64,64,128]{2,1,0:T(8,128)(2,1)}), bf16[64,64,128]{2,1,0:T(8,128)(2,1)S(1)}, u32[]{:S(2)}, u32[]{:S(2)}) async-start(bf16[64,64,128]{2,1,0:T(8,128)(2,1)} %get-tuple-element.22), calls=%async_computation.2 | async-start | bytes 2097152 | tf_op jit(solution)/shard_map/all_to_all | solution.py:411
  70.9 0.1 copy.11.ranges_ref
  71.0 7.3 %grad_embed.1 = bf16[1024,4096]{1,0:T(8,128)(2,1)} custom-call(s32[1]{0:T(128)} %bitcast.core_ref, s32[1]{0:T(128)} %bitcast.1.start_ref, s32[8,2]{1,0:T(8,128)S(1)} %copy.11.ranges_ref, f32[8,256]{1,0:T(8,128)S(1)} %get-tuple-element.15.info_ref.refs_1_.refs_0_, bf16[256,2048]{1,0:T(8,128)(2,1)S(1)} %joined_quarters.1.refs_1_, ...), custom_call_target="tpu_custom_call" | custom-call | flops 2147483648 | bytes 8388608 | tf_op jit(solution)/shard_map/grad_embed/pallas_call | solution.py:19
  78.3 6.2 %grad_head.1 = bf16[1024,4096]{1,0:T(8,128)(2,1)} custom-call(s32[1]{0:T(128)} %bitcast.core_ref, s32[1]{0:T(128)} %bitcast.1.start_ref, s32[8,2]{1,0:T(8,128)S(1)} %copy.11.ranges_ref, f32[1024,256]{1,0:T(8,128)S(1)} %copy-done.2, f32[8,256]{1,0:T(8,128)S(1)} %get-tuple-element.15.info_ref.refs_1_.refs_0_, f32[1,256]{1,0:T(1,128)S(1)} %get-tuple-element.24.refs_2_, ...), custom_call_target="tpu_custom_call" | custom-call | flops 2147483648 | bytes 8388608 | tf_op jit(solution)/shard_map/grad_head/pallas_call | solution.py:19
  84.5 5.4 %all-to-all-done.2.parts_ref = bf16[64,64,128]{2,1,0:T(8,128)(2,1)S(1)} async-done(((bf16[64,64,128]{2,1,0:T(8,128)(2,1)}), bf16[64,64,128]{2,1,0:T(8,128)(2,1)S(1)}, u32[]{:S(2)}, u32[]{:S(2)}) %all-to-all-start.2) | async-done | bytes 1048608 | tf_op jit(solution)/shard_map/all_to_all | solution.py:411
  89.9 0.8 summed_parts.1
  (20 shorter events, 0.0 us)
Async XLA Ops:
  1.6 37.6 %slice-start = ((s8[8388608]{0:T(1024)(128)(4,1)}), s8[4194304]{0:T(1024)(128)(4,1)S(1)}, s32[]{:S(2)}) async-start(s8[8388608]{0:T(1024)(128)(4,1)} %bitcast.4), calls=%async_computation.3 | async-start | bytes 8388608
  35.3 3.9 %slice-start.1 = ((s8[8388608]{0:T(1024)(128)(4,1)}), s8[4194304]{0:T(1024)(128)(4,1)S(1)}, s32[]{:S(2)}) async-start(s8[8388608]{0:T(1024)(128)(4,1)} %bitcast.4), calls=%async_computation.4 | async-start | bytes 8388608
  35.6 3.6 %collective-permute-start = (bf16[256,2048]{1,0:T(8,128)(2,1)S(1)}, bf16[256,2048]{1,0:T(8,128)(2,1)S(1)}, u32[]{:S(2)}, u32[]{:S(2)}) collective-permute-start(bf16[256,2048]{1,0:T(8,128)(2,1)S(1)} %get-tuple-element.16.near_ref.refs_3_), channel_id=1, source_target_pairs={{0,1},{1,0},{2,3},{3,2},{4,5},{5,4},{6,7},{7,6},{8,9},{9,8},{10,11... | collective-permute-start | bytes 3145736 | tf_op jit(solution)/shard_map/ppermute | solution.py:40
  35.6 14.4 %collective-permute-start.5 = (bf16[256,512]{1,0:T(8,128)(2,1)S(1)}, bf16[256,512]{1,0:T(8,128)(2,1)S(1)}, u32[]{:S(2)}, u32[]{:S(2)}) collective-permute-start(bf16[256,512]{1,0:T(8,128)(2,1)S(1)} %get-tuple-element.25.refs_0_), channel_id=1, source_target_pairs={{0,10},{2,8},{4,14},{6,12},{8,2},{10,0},{12,6},{14,4},{16,26},{18,... | collective-permute-start | bytes 786440 | tf_op jit(solution)/shard_map/ppermute | solution.py:47
  35.7 14.3 %collective-permute-start.4 = (bf16[256,512]{1,0:T(8,128)(2,1)S(1)}, bf16[256,512]{1,0:T(8,128)(2,1)S(1)}, u32[]{:S(2)}, u32[]{:S(2)}) collective-permute-start(bf16[256,512]{1,0:T(8,128)(2,1)S(1)} %get-tuple-element.25.refs_0_), channel_id=1, source_target_pairs={{0,8},{2,10},{4,12},{6,14},{8,0},{10,2},{12,4},{14,6},{16,24},{18,... | collective-permute-start | bytes 786440 | tf_op jit(solution)/shard_map/ppermute | solution.py:47
  37.5 13.4 %collective-permute-start.3 = (bf16[256,512]{1,0:T(8,128)(2,1)S(1)}, bf16[256,512]{1,0:T(8,128)(2,1)S(1)}, u32[]{:S(2)}, u32[]{:S(2)}) collective-permute-start(bf16[256,512]{1,0:T(8,128)(2,1)S(1)} %get-tuple-element.25.refs_0_), channel_id=1, source_target_pairs={{0,2},{2,0},{4,6},{6,4},{8,10},{10,8},{12,14},{14,12},{16,18},{18,... | collective-permute-start | bytes 786440 | tf_op jit(solution)/shard_map/ppermute | solution.py:47
  39.2 6.0 %copy-start = (bf16[256,2048]{1,0:T(8,128)(2,1)}, bf16[256,2048]{1,0:T(8,128)(2,1)S(1)}, u32[]{:S(2)}) copy-start(bf16[256,2048]{1,0:T(8,128)(2,1)S(1)} %collective-permute-done.far_ref.refs_4_) | copy-start | bytes 3145732
  45.2 14.9 %all-to-all-start.1 = ((f32[128,1,384]{2,1,0:T(1,128)}), f32[128,1,384]{2,1,0:T(1,128)S(1)}, u32[]{:S(2)}, u32[]{:S(2)}) async-start(f32[128,1,384]{2,1,0:T(1,128)} %get-tuple-element.17), calls=%async_computation.1 | async-start | bytes 393216 | tf_op jit(solution)/shard_map/all_to_all | solution.py:404
  49.9 1.7 %copy-start.3 = (bf16[512,1024]{1,0:T(8,128)(2,1)S(1)}, bf16[512,1024]{1,0:T(8,128)(2,1)}, u32[]{:S(2)}) copy-start(bf16[512,1024]{1,0:T(8,128)(2,1)} %get-tuple-element.19.left_ref) | copy-start | bytes 3145732
  49.9 7.1 %collective-permute-start.1 = (f32[8,256]{1,0:T(8,128)S(1)}, f32[8,256]{1,0:T(8,128)S(1)}, u32[]{:S(2)}, u32[]{:S(2)}) collective-permute-start(f32[8,256]{1,0:T(8,128)S(1)} %get-tuple-element.18.last_ref.refs_4_), channel_id=1, source_target_pairs={{0,1},{1,0},{2,3},{3,2},{4,5},{5,4},{6,7},{7,6},{8,9},{9,8},{10,11... | collective-permute-start | bytes 24584 | tf_op jit(solution)/shard_map/ppermute | solution.py:40
  50.9 20.0 %collective-permute-start.6 = (bf16[256,2048]{1,0:T(8,128)(2,1)S(1)}, bf16[256,2048]{1,0:T(8,128)(2,1)}, u32[]{:S(2)}, u32[]{:S(2)}) collective-permute-start(bf16[256,2048]{1,0:T(8,128)(2,1)S(1)} %joined_quarters.1.refs_1_), channel_id=1, source_target_pairs={{0,1},{1,0},{2,3},{3,2},{4,5},{5,4},{6,7},{7,6},{8,9},{9,8},{10,11... | collective-permute-start | bytes 3145736 | tf_op jit(solution)/shard_map/ppermute | solution.py:40
  51.0 9.1 %collective-permute-start.2 = (bf16[16,512,128]{2,1,0:T(8,128)(2,1)}, bf16[16,512,128]{2,1,0:T(8,128)(2,1)}, u32[]{:S(2)}, u32[]{:S(2)}) collective-permute-start(bf16[16,512,128]{2,1,0:T(8,128)(2,1)} %get-tuple-element.20), channel_id=1, source_target_pairs={{0,1},{1,0},{2,3},{3,2},{4,5},{5,4},{6,7},{7,6},{8,9},{9,8},{10,11... | collective-permute-start | bytes 6291464 | tf_op jit(solution)/shard_map/ppermute | solution.py:40
  64.0 6.9 %copy-start.4 = (s32[8,2]{0,1:T(2,128)S(1)}, s32[8,2]{0,1:T(2,128)}, u32[]{:S(2)}) copy-start(s32[8,2]{0,1:T(2,128)} %param.13) | copy-start | bytes 196
  64.1 25.9 %all-to-all-start.2 = ((bf16[64,64,128]{2,1,0:T(8,128)(2,1)}), bf16[64,64,128]{2,1,0:T(8,128)(2,1)S(1)}, u32[]{:S(2)}, u32[]{:S(2)}) async-start(bf16[64,64,128]{2,1,0:T(8,128)(2,1)} %get-tuple-element.22), calls=%async_computation.2 | async-start | bytes 2097152 | tf_op jit(solution)/shard_map/all_to_all | solution.py:411
  71.0 7.4 %copy-start.1 = (bf16[256,2048]{1,0:T(8,128)(2,1)S(1)}, bf16[256,2048]{1,0:T(8,128)(2,1)}, u32[]{:S(2)}) copy-start(bf16[256,2048]{1,0:T(8,128)(2,1)} %copy-done) | copy-start | bytes 3145732
  71.0 7.4 %copy-start.2 = (f32[1024,256]{1,0:T(8,128)S(1)}, f32[1024,256]{1,0:T(8,128)}, u32[]{:S(2)}) copy-start(f32[1024,256]{1,0:T(8,128)} %get-tuple-element.23.refs_0_) | copy-start | bytes 3145732
